TPU v7x, 1024 devices: a whole 4x8x16 slice. The times are simulated.
1024 devices in a mesh: path: 64 (over z_lo, y, core), fsdp: 16 (over z_hi, x).
Axes of the slice: x: 4, y: 8, z: 16 (z_hi: 4, z_lo: 4; z = z_hi * 4 + z_lo), core: 2. Of those that a mesh axis runs over, the one named last changes fastest.
Arguments:
- cotangent: bfloat16 [64, 2048, 1024], P('path', 'fsdp'), may hold values from -6 to 6
- hidden: bfloat16 [64, 2048, 4096], P('path', 'fsdp'), may hold values from -6 to 6
- drift: bfloat16 [2, 64, 1024, 4096], P(None, 'path', None, 'fsdp'), may hold values from -6 to 6
- counts: int32 [64], replicated, may hold values from 512 to 2048, as said below
- assignment: int32 [2, 64], replicated, may hold values from 0 to 7, as said below
- outer_params: float32 [2, 8, 1024, 4096], P(None, None, 'path', 'fsdp'), may hold values from -6 to 6
- outer_moment: float32 [2, 8, 1024, 4096], P(None, None, 'path', 'fsdp'), may hold values from -3 to 3
Outputs:
- new_params: float32 [2, 8, 1024, 4096], P(None, None, 'path', 'fsdp')
- new_moment: float32 [2, 8, 1024, 4096], P(None, None, 'path', 'fsdp')
Inputs may be any that keep to these rules, and one draw needn't show every extreme that they name: `counts`: some path has exactly 2048 live tokens and some exactly 512. `assignment`: at each level every module has exactly 8 paths.
All inputs are finite; a program needn't handle non-finite values.
Results may differ from a plain program's by a relative error of at most 0.0016.
Values may be sent and summed in bfloat16 or wider, within the bound.
No kernel may reach another device: no remote copies, remote signals or barrier semaphores. Data moves between devices by JAX's collectives and lax.ppermute only.
A program may use at most 32 MiB of HBM per device.

v0:
```python
import jax
import jax.numpy as jnp
from jax import lax
from jax.sharding import PartitionSpec as P

inner_step = 0.02
momentum_rate = 0.9
outer_rate = 0.7


def combine(received, shares):
    return jnp.einsum(
        "lmp,lprc->lmrc", shares, received.astype(jnp.float32), precision=lax.Precision.HIGHEST
    )


def body(cotangent, hidden, drift, counts, assignment, outer_params, outer_moment):
    path_index = lax.axis_index("path")
    shard_index = lax.axis_index("fsdp")
    paths = counts.shape[0]
    modules = outer_params.shape[1]
    owner_rows = outer_params.shape[2]
    columns_dev = outer_params.shape[3]
    rows = cotangent.shape[1]
    member = (assignment[:, None, :] == jnp.arange(modules, dtype=jnp.int32)[None, :, None]).astype(
        jnp.float32
    )
    weighted = member * counts[None, None, :].astype(jnp.float32)
    shares = weighted / jnp.sum(weighted, axis=-1, keepdims=True)
    my_count = jnp.sum(jnp.where(jnp.arange(paths, dtype=jnp.int32) == path_index, counts, 0))
    positions = shard_index * rows + jnp.arange(rows, dtype=jnp.int32)
    masked = jnp.where(
        (positions < my_count)[:, None], cotangent[0], jnp.zeros((), cotangent.dtype)
    )
    columns = lax.all_to_all(hidden[0], "fsdp", split_axis=1, concat_axis=0, tiled=True)
    grad = lax.dot_general(
        lax.all_gather(masked, "fsdp", axis=0, tiled=True),
        columns,
        (((0,), (0,)), ((), ())),
        preferred_element_type=jnp.float32,
    )
    upper = (drift[1, 0].astype(jnp.float32) + inner_step * grad).astype(jnp.bfloat16)
    both_send = jnp.stack([drift[0, 0], upper]).reshape(2, paths, owner_rows, columns_dev)
    both_got = lax.all_to_all(both_send, "path", split_axis=1, concat_axis=1, tiled=True)
    average = combine(both_got, shares)
    new_moment = momentum_rate * outer_moment + average
    new_params = outer_params - outer_rate * (average + momentum_rate * new_moment)
    return (new_params, new_moment)


def solution(mesh):
    placed = (
        P("path", "fsdp", None),
        P("path", "fsdp", None),
        P(None, "path", None, "fsdp"),
        P(),
        P(),
        P(None, None, "path", "fsdp"),
        P(None, None, "path", "fsdp"),
    )
    return jax.shard_map(
        body,
        mesh=mesh,
        in_specs=placed,
        out_specs=(P(None, None, "path", "fsdp"), P(None, None, "path", "fsdp")),
        check_vma=False,
    )
```

profile of v0, /device:TPU:1, one launch (start us, length us, event | category | flops | bytes accessed | tf_op | source)
XLA Modules:
  0.0 252.6 jit_solution(9560640208668575613)
XLA Ops:
  7.2 0.0 copy-start
  7.2 0.0 all-gather.2.cloned.1.call-start
  7.2 1.4 fusion.13
  8.6 0.7 add_compare_fusion
  9.3 1.7 bitcast_select_fusion
  11.0 0.0 all-gather.2.cloned.1.call-update
  11.0 2.3 copy.28
  13.3 21.8 %all-to-all-start = ((bf16[128,16,256]{0,2,1:T(8,128)(2,1)}), bf16[128,16,256]{0,2,1:T(8,128)(2,1)S(1)}, u32[]{:S(2)}, u32[]{:S(2)}) async-start(bf16[128,16,256]{0,2,1:T(8,128)(2,1)} %bitcast.5), calls=%async_computation | async-start | bytes 2097152 | tf_op jit(solution)/shard_map/all_to_all | solution.py:35
  35.2 36.2 %all-to-all-done = bf16[128,16,256]{0,2,1:T(8,128)(2,1)S(1)} async-done(((bf16[128,16,256]{0,2,1:T(8,128)(2,1)}), bf16[128,16,256]{0,2,1:T(8,128)(2,1)S(1)}, u32[]{:S(2)}, u32[]{:S(2)}) %all-to-all-start) | async-done | bytes 1048608 | tf_op jit(solution)/shard_map/all_to_all | solution.py:35
  71.3 0.5 copy.29
  71.8 126.2 %all-gather.2.cloned.1.call-done = bf16[2048,1024]{1,0:T(8,128)(2,1)} async-done(((bf16[128,1024]{1,0:T(8,128)(2,1)}), bf16[2048,1024]{1,0:T(8,128)(2,1)}) %all-gather.2.cloned.1.call-update) | async-done | bytes 4194320 | tf_op jit(solution)/shard_map/all_gather | solution.py:37
  198.1 0.0 copy-done
  198.1 0.0 slice-start
  198.1 3.5 %fusion.1 = bf16[1024,256]{1,0:T(8,128)(2,1)S(1)} fusion(bf16[2048,1024]{1,0:T(8,128)(2,1)} %all-gather.2.cloned.1.call-done, bf16[2048,256]{1,0:T(8,128)(2,1)S(1)} %bitcast.21, bf16[2,1,1024,256]{3,2,1,0:T(8,128)(2,1)S(1)} %copy-done), kind=kOutput, calls=%fused_computation.2 | convolution fusion | flops 1074790400 | bytes 6291456 | tf_op jit(solution)/shard_map/dot_general | solution.py:36
  201.6 0.0 copy-start.3
  201.7 0.0 copy-start.1
  201.7 0.0 copy-start.2
  201.7 0.0 slice-done
  201.7 0.1 pad_maximum_fusion
  201.8 1.1 copy.30
  202.9 11.4 %all-to-all-start.1 = ((bf16[2,64,16,256]{3,2,0,1:T(8,128)(2,1)}), bf16[2,64,16,256]{3,2,0,1:T(8,128)(2,1)S(1)}, u32[]{:S(2)}, u32[]{:S(2)}) async-start(bf16[2,64,16,256]{3,2,0,1:T(8,128)(2,1)} %copy.30), calls=%async_computation.1 | async-start | bytes 2097152 | tf_op jit(solution)/shard_map/all_to_all | solution.py:44
  214.4 0.0 copy-done.3
  214.4 0.1 select_reduce_fusion
  214.5 28.5 %all-to-all-done.1 = bf16[2,64,16,256]{3,2,0,1:T(8,128)(2,1)S(1)} async-done(((bf16[2,64,16,256]{3,2,0,1:T(8,128)(2,1)}), bf16[2,64,16,256]{3,2,0,1:T(8,128)(2,1)S(1)}, u32[]{:S(2)}, u32[]{:S(2)}) %all-to-all-start.1) | async-done | bytes 1048608 | tf_op jit(solution)/shard_map/all_to_all | solution.py:44
  243.0 0.0 copy-done.1
  243.0 0.0 copy-done.2
  243.0 1.1 fusion.4
  244.1 0.8 copy.34
  244.9 0.8 copy.35
Async XLA Ops:
  7.2 190.9 %copy-start = (bf16[2,1,1024,256]{3,2,1,0:T(8,128)(2,1)S(1)}, bf16[2,1,1024,256]{3,2,1,0:T(8,128)(2,1)}, u32[]{:S(2)}) copy-start(bf16[2,1,1024,256]{3,2,1,0:T(8,128)(2,1)} %param.9) | copy-start | bytes 3145732
  7.2 190.9 %all-gather.2.cloned.1.call-start = ((), (), s32[]{:S(2)}) async-start(), calls=%async_computation.2 | async-start | bytes 4456448 | tf_op jit(solution)/shard_map/all_gather | solution.py:37
  13.3 58.0 %all-to-all-start = ((bf16[128,16,256]{0,2,1:T(8,128)(2,1)}), bf16[128,16,256]{0,2,1:T(8,128)(2,1)S(1)}, u32[]{:S(2)}, u32[]{:S(2)}) async-start(bf16[128,16,256]{0,2,1:T(8,128)(2,1)} %bitcast.5), calls=%async_computation | async-start | bytes 2097152 | tf_op jit(solution)/shard_map/all_to_all | solution.py:35
  198.1 3.6 %slice-start = ((bf16[2,1,1024,256]{3,2,1,0:T(8,128)(2,1)}), bf16[1,1,1024,256]{3,2,1,0:T(8,128)(2,1)S(1)}, s32[]{:S(2)}) async-start(bf16[2,1,1024,256]{3,2,1,0:T(8,128)(2,1)} %param.9), calls=%async_computation.3 | async-start | bytes 1048576 | tf_op jit(solution)/shard_map/slice | solution.py:43
  201.6 12.7 %copy-start.3 = (s32[2,64]{1,0:T(2,128)S(1)}, s32[2,64]{1,0:T(2,128)}, u32[]{:S(2)}) copy-start(s32[2,64]{1,0:T(2,128)} %param.11) | copy-start | bytes 1540
  201.7 41.3 %copy-start.1 = (f32[2,8,16,256]{3,2,1,0:T(8,128)S(1)}, f32[2,8,16,256]{3,2,1,0:T(8,128)}, u32[]{:S(2)}) copy-start(f32[2,8,16,256]{3,2,1,0:T(8,128)} %param.13) | copy-start | bytes 786436
  201.7 41.3 %copy-start.2 = (f32[2,8,16,256]{3,2,1,0:T(8,128)S(1)}, f32[2,8,16,256]{3,2,1,0:T(8,128)}, u32[]{:S(2)}) copy-start(f32[2,8,16,256]{3,2,1,0:T(8,128)} %param.12) | copy-start | bytes 786436
  202.9 40.1 %all-to-all-start.1 = ((bf16[2,64,16,256]{3,2,0,1:T(8,128)(2,1)}), bf16[2,64,16,256]{3,2,0,1:T(8,128)(2,1)S(1)}, u32[]{:S(2)}, u32[]{:S(2)}) async-start(bf16[2,64,16,256]{3,2,0,1:T(8,128)(2,1)} %copy.30), calls=%async_computation.1 | async-start | bytes 2097152 | tf_op jit(solution)/shard_map/all_to_all | solution.py:44
Sparse Core Ops, SparseCore 0:
  12.8 185.2 all-gather.1
where the time goes:
time: 253 us
  waiting for transfers between devices  191 us (75%)
  starting transfers between devices  33.3 us (13%)
  between operations  14.1 us (6%)
  local copies, waits for them, and re-layouts  5.5 us (2%)
  matrix products  4.69 us (2%)
  other arithmetic  3.97 us (2%)
    all_gather x1, waiting for transfers between devices, body(): lax.all_gather(masked, 'fsdp', axis=0, tiled=True)  126 us
    all_to_all x1, waiting for transfers between devices, body(): lax.all_to_all(hidden[0], 'fsdp', split_axis=1, concat_axis=0, tiled=True)  36.2 us
    all_to_all x1, waiting for transfers between devices, body(): lax.all_to_all(both_send, 'path', split_axis=1, concat_axis=1, tiled=True)  28.5 us
    all_to_all x1, starting transfers between devices, body(): lax.all_to_all(hidden[0], 'fsdp', split_axis=1, concat_axis=0, tiled=True)  21.8 us
    all_to_all x1, starting transfers between devices, body(): lax.all_to_all(both_send, 'path', split_axis=1, concat_axis=1, tiled=True)  11.4 us
  transfers between devices with their start and end apart: 3, of which 3 were waited for; matrix products, arithmetic and copies ran while one was open for 1% of the time, Pallas kernels for 0%

commit v1 on v0

v1 whole, which is shorter than its diff:
```python
import jax
import jax.numpy as jnp
from jax import lax
from jax.sharding import Mesh, PartitionSpec as P

inner_step = 0.02
momentum_rate = 0.9
outer_rate = 0.7

PATH = ("zl", "y", "core")
FSDP = ("zh", "x")
NX = 4
NZ = 4


def shift(axis, size, by):
    return [(i, (i + by) % size) for i in range(size)]


def combine(received, shares):
    return jnp.einsum(
        "mp,prc->mrc", shares, received.astype(jnp.float32), precision=lax.Precision.HIGHEST
    )


def body(cotangent, hidden, drift, counts, assignment, outer_params, outer_moment):
    path_index = lax.axis_index(PATH)
    zh = lax.axis_index("zh")
    x = lax.axis_index("x")
    paths = counts.shape[0]
    modules = outer_params.shape[1]
    owner_rows = outer_params.shape[2]
    cols = outer_params.shape[3]
    rows = cotangent.shape[1]
    width = cotangent.shape[2]
    member = (assignment[:, None, :] == jnp.arange(modules, dtype=jnp.int32)[None, :, None]).astype(
        jnp.float32
    )
    weighted = member * counts[None, None, :].astype(jnp.float32)
    shares = weighted / jnp.sum(weighted, axis=-1, keepdims=True)
    my_count = jnp.sum(jnp.where(jnp.arange(paths, dtype=jnp.int32) == path_index, counts, 0))

    got0 = lax.all_to_all(
        drift[0, 0].reshape(paths, owner_rows, cols), PATH, split_axis=0, concat_axis=0, tiled=True
    )

    positions = (zh * NX + x) * rows + jnp.arange(rows, dtype=jnp.int32)
    masked = jnp.where(
        (positions < my_count)[:, None], cotangent[0], jnp.zeros((), cotangent.dtype)
    )
    by_x = hidden[0].reshape(rows, NZ, NX, cols)

    def piece(to):
        return lax.dynamic_index_in_dim(by_x, to, 2, keepdims=False).reshape(rows, NZ * cols)

    pieces = [jnp.concatenate([masked, piece(x)], axis=1)]
    for by in (1, 2, 3):
        packed = jnp.concatenate([masked, piece((x + by) % NX)], axis=1)
        pieces.append(lax.ppermute(packed, "x", shift("x", NX, by)))
    tokens = jnp.concatenate(pieces, axis=0)
    grad = lax.dot_general(
        tokens[:, :width],
        tokens[:, width:],
        (((0,), (0,)), ((), ())),
        preferred_element_type=jnp.float32,
    )
    own = (jnp.arange(NZ) == zh)[None, :, None]
    upper = inner_step * grad.reshape(width, NZ, cols) + jnp.where(
        own, drift[1, 0].astype(jnp.float32)[:, None, :], 0.0
    )
    upper = upper.astype(jnp.bfloat16).reshape(paths, owner_rows, NZ * cols)
    got1 = lax.all_to_all(upper, PATH, split_axis=0, concat_axis=0, tiled=True)
    part1 = combine(got1, shares[1]).reshape(modules, owner_rows, NZ, cols)
    average0 = combine(got0, shares[0])
    average1 = lax.dynamic_index_in_dim(part1, zh, 2, keepdims=False)
    for by in (1, 2, 3):
        block = lax.dynamic_index_in_dim(part1, (zh + by) % NZ, 2, keepdims=False)
        average1 = average1 + lax.ppermute(
            block.astype(jnp.bfloat16), "zh", shift("zh", NZ, by)
        ).astype(jnp.float32)
    average = jnp.stack([average0, average1])
    new_moment = momentum_rate * outer_moment + average
    new_params = outer_params - outer_rate * (average + momentum_rate * new_moment)
    return (new_params, new_moment)


def solution(mesh):
    fine = Mesh(mesh.devices.reshape(4, 8, 2, 4, 4), ("zl", "y", "core", "zh", "x"))
    placed = (
        P(PATH, FSDP, None),
        P(PATH, FSDP, None),
        P(None, PATH, None, FSDP),
        P(),
        P(),
        P(None, None, PATH, FSDP),
        P(None, None, PATH, FSDP),
    )
    return jax.shard_map(
        body,
        mesh=fine,
        in_specs=placed,
        out_specs=(P(None, None, PATH, FSDP), P(None, None, PATH, FSDP)),
        check_vma=False,
    )
```

time: 253 us -> 162 us (0.64)
  the two profiles are of different devices: /device:TPU:1 before, /device:TPU:2 now
where the time goes in v1:
time: 162 us
  blocking collectives  63.8 us (39%)
  starting transfers between devices  59.4 us (37%)
  local copies, waits for them, and re-layouts  17.3 us (11%)
  waiting for transfers between devices  9.2 us (6%)
  other arithmetic  7.31 us (5%)
  matrix products  3.49 us (2%)
    all_to_all x1, blocking collectives, body(): got1 = lax.all_to_all(upper, PATH, split_axis=0, concat_axis=0, tiled=True)  63.8 us
    ppermute x3, starting transfers between devices, body(): lax.ppermute(block.astype(jnp.bfloat16), 'zh', shift('zh', NZ, by))  26.8 us
    ppermute x3, starting transfers between devices, body(): pieces.append(lax.ppermute(packed, 'x', shift('x', NX, by)))  21 us
    all_to_all x1, starting transfers between devices, body(): lax.all_to_all(drift[0, 0].reshape(paths, owner_rows, cols), PATH, split_...  11.7 us
    broadcast_in_dim x4, local copies, waits for them, and re-layouts, body(): jnp.where(own, drift[1, 0].astype(jnp.float32)[:, None, :], 0.0)  8.56 us
    ppermute x3, waiting for transfers between devices, body(): lax.ppermute(block.astype(jnp.bfloat16), 'zh', shift('zh', NZ, by))  7.77 us
    unnamed x12, local copies, waits for them, and re-layouts  5.29 us
    dot_general x1, local copies, waits for them, and re-layouts, combine(): jnp.einsum('mp,prc->mrc', shares, received.astype(jnp.float32), precision...  3.33 us
  transfers between devices with their start and end apart: 7, of which 3 were waited for; matrix products, arithmetic and copies ran while one was open for 9% of the time, Pallas kernels for 0%

profile of v1, /device:TPU:2, one launch (start us, length us, event | category | flops | bytes accessed | tf_op | source)
XLA Modules:
  0.0 161.5 jit_solution(10408155927557743231)
XLA Ops:
  0.7 1.2 copy.40
  1.9 1.6 %copy.41 = bf16[1,128,4096]{1,2,0:T(8,128)(2,1)S(1)} copy(bf16[1,128,4096]{2,1,0:T(8,128)(2,1)} %param.8) | data formatting | bytes 2097152 | tf_op args[1]
  3.5 1.4 fusion.14
  4.9 0.7 add_compare_fusion
  5.6 0.1 constant_dynamic-slice_fusion.3
  5.7 0.1 pad_maximum_fusion.3
  5.8 3.4 %collective-permute-start = (bf16[128,2048]{0,1:T(8,128)(2,1)S(1)}, bf16[128,2048]{0,1:T(8,128)(2,1)}, u32[]{:S(2)}, u32[]{:S(2)}) collective-permute-start(bf16[128,2048]{0,1:T(8,128)(2,1)S(1)} %get-tuple-element.21), channel_id=1, source_target_pairs={{0,1},{1,2},{2,3},{3,0},{4,5},{5,6},{6,7},{7,4},{8,9},{9,10},{10,1... | collective-permute-start | bytes 1572872 | tf_op jit(solution)/shard_map/ppermute | solution.py:59
  9.2 15.7 %collective-permute-start.1 = (bf16[128,2048]{0,1:T(8,128)(2,1)S(1)}, bf16[128,2048]{0,1:T(8,128)(2,1)}, u32[]{:S(2)}, u32[]{:S(2)}) collective-permute-start(bf16[128,2048]{0,1:T(8,128)(2,1)S(1)} %get-tuple-element.22), channel_id=1, source_target_pairs={{0,2},{1,3},{2,0},{3,1},{4,6},{5,7},{6,4},{7,5},{8,10},{9,11},{10,... | collective-permute-start | bytes 1572872 | tf_op jit(solution)/shard_map/ppermute | solution.py:59
  24.9 1.9 %collective-permute-start.2 = (bf16[128,2048]{0,1:T(8,128)(2,1)S(1)}, bf16[128,2048]{0,1:T(8,128)(2,1)}, u32[]{:S(2)}, u32[]{:S(2)}) collective-permute-start(bf16[128,2048]{0,1:T(8,128)(2,1)S(1)} %get-tuple-element.23), channel_id=1, source_target_pairs={{0,3},{1,0},{2,1},{3,2},{4,7},{5,4},{6,5},{7,6},{8,11},{9,8},{10,9... | collective-permute-start | bytes 1572872 | tf_op jit(solution)/shard_map/ppermute | solution.py:59
  26.9 0.9 fusion.13
  27.9 2.7 %broadcast_in_dim.55 = f32[1024,4,256]{2,1,0:T(4,128)} broadcast(f32[1024,256]{1,0:T(8,128)S(1)} %get-tuple-element.11), dimensions={0,2} | broadcast | bytes 5242880 | tf_op jit(solution)/shard_map/jit(_where)/broadcast_in_dim | solution.py:68
  30.5 5.8 %broadcast_in_dim.56 = f32[64,16,1024]{2,1,0:T(8,128)} reshape(f32[1024,4,256]{2,1,0:T(4,128)} %broadcast_in_dim.55) | data formatting | bytes 8388608 | tf_op jit(solution)/shard_map/jit(_where)/broadcast_in_dim | solution.py:68
  36.3 1.4 collective-permute-done.2
  37.8 1.6 pad_maximum_fusion
  39.4 1.3 convolution_multiply_fusion
  40.7 0.9 copy-done
  41.5 1.1 add_convert_fusion
  42.7 63.8 %all_to_all.10 = bf16[64,16,1024]{2,1,0:T(8,128)(2,1)} all-to-all(bf16[64,16,1024]{2,1,0:T(8,128)(2,1)S(1)} %add_convert_fusion), channel_id=1, replica_groups=mesh['zl'=4,'y'=8,'core'=2,'zh'=4,'x'=4] {'zl','y','core'}, dimensions={0} | all-to-all | bytes 4194304 | tf_op jit(solution)/shard_map/all_to_all | solution.py:72
  106.5 11.7 %all-to-all-start = ((bf16[64,16,256]{2,1,0:T(8,128)(2,1)}), bf16[64,16,256]{2,1,0:T(8,128)(2,1)S(1)}, u32[]{:S(2)}, u32[]{:S(2)}) async-start(bf16[64,16,256]{2,1,0:T(8,128)(2,1)} %bitcast.2), calls=%async_computation | async-start | bytes 1048576 | tf_op jit(solution)/shard_map/all_to_all | solution.py:43
  118.3 0.1 select_reduce_fusion
  118.4 0.1 select_divide_fusion
  118.4 3.3 %reshape.59 = bf16[16,4,256,64]{2,1,0,3:T(4,128)(2,1)S(1)} reshape(bf16[16,1024,64]{1,0,2:T(8,128)(2,1)} %bitcast.56) | data formatting | bytes 4194304 | tf_op jit(solution)/shard_map/mp,prc->mrc/dot_general | solution.py:21
  121.8 1.8 %fusion = f32[8,16,4,256]{3,0,2,1:T(8,128)S(1)} fusion(bf16[16,4,256,64]{2,1,0,3:T(4,128)(2,1)S(1)} %reshape.59, f32[2,8,64]{2,1,0:T(8,128)S(1)} %select_divide_fusion), kind=kOutput, calls=%fused_computation.3 | convolution fusion | flops 100663296 | bytes 2625536 | tf_op jit(solution)/shard_map/mp,prc->mrc/dot_general | solution.py:21
  123.6 10.9 %collective-permute-start.3 = (bf16[8,16,256]{2,0,1:T(8,128)(2,1)S(1)}, bf16[8,16,256]{2,0,1:T(8,128)(2,1)S(1)}, u32[]{:S(2)}, u32[]{:S(2)}) collective-permute-start(bf16[8,16,256]{2,0,1:T(8,128)(2,1)S(1)} %get-tuple-element.18), channel_id=1, source_target_pairs={{0,4},{4,8},{8,12},{12,0},{1,5},{5,9},{9,13},{13,1},{2,6},{6,10},{... | collective-permute-start | bytes 196616 | tf_op jit(solution)/shard_map/ppermute | solution.py:78
  134.5 11.9 %collective-permute-start.4 = (bf16[8,16,256]{2,0,1:T(8,128)(2,1)S(1)}, bf16[8,16,256]{2,0,1:T(8,128)(2,1)S(1)}, u32[]{:S(2)}, u32[]{:S(2)}) collective-permute-start(bf16[8,16,256]{2,0,1:T(8,128)(2,1)S(1)} %get-tuple-element.19), channel_id=1, source_target_pairs={{0,8},{4,12},{8,0},{12,4},{1,9},{5,13},{9,1},{13,5},{2,10},{6,14},... | collective-permute-start | bytes 196616 | tf_op jit(solution)/shard_map/ppermute | solution.py:78
  146.4 4.0 %collective-permute-start.5 = (bf16[8,16,256]{2,0,1:T(8,128)(2,1)S(1)}, bf16[8,16,256]{2,0,1:T(8,128)(2,1)S(1)}, u32[]{:S(2)}, u32[]{:S(2)}) collective-permute-start(bf16[8,16,256]{2,0,1:T(8,128)(2,1)S(1)} %get-tuple-element.20), channel_id=1, source_target_pairs={{0,12},{4,0},{8,4},{12,8},{1,13},{5,1},{9,5},{13,9},{2,14},{6,2},{... | collective-permute-start | bytes 196616 | tf_op jit(solution)/shard_map/ppermute | solution.py:78
  150.4 0.4 convolution_bitcast_fusion
  150.9 4.8 %collective-permute-done.4 = bf16[8,16,256]{2,0,1:T(8,128)(2,1)S(1)} collective-permute-done((bf16[8,16,256]{2,0,1:T(8,128)(2,1)S(1)}, bf16[8,16,256]{2,0,1:T(8,128)(2,1)S(1)}, u32[]{:S(2)}, u32[]{:S(2)}) %collective-permute-start.4) | collective-permute-done | bytes 65568 | tf_op jit(solution)/shard_map/ppermute | solution.py:78
  155.7 3.0 %collective-permute-done.5 = bf16[8,16,256]{2,0,1:T(8,128)(2,1)S(1)} collective-permute-done((bf16[8,16,256]{2,0,1:T(8,128)(2,1)S(1)}, bf16[8,16,256]{2,0,1:T(8,128)(2,1)S(1)}, u32[]{:S(2)}, u32[]{:S(2)}) %collective-permute-start.5) | collective-permute-done | bytes 65568 | tf_op jit(solution)/shard_map/ppermute | solution.py:78
  158.7 1.3 fusion.5
  160.0 0.8 copy.50
  160.8 0.8 copy.49
  (17 shorter events, 0.2 us)
Async XLA Ops:
  0.6 26.3 %copy-start.1 = (bf16[2,1,1024,256]{3,2,1,0:T(8,128)(2,1)S(1)}, bf16[2,1,1024,256]{3,2,1,0:T(8,128)(2,1)}, u32[]{:S(2)}) copy-start(bf16[2,1,1024,256]{3,2,1,0:T(8,128)(2,1)} %param.9) | copy-start | bytes 3145732
  5.8 30.5 %collective-permute-start = (bf16[128,2048]{0,1:T(8,128)(2,1)S(1)}, bf16[128,2048]{0,1:T(8,128)(2,1)}, u32[]{:S(2)}, u32[]{:S(2)}) collective-permute-start(bf16[128,2048]{0,1:T(8,128)(2,1)S(1)} %get-tuple-element.21), channel_id=1, source_target_pairs={{0,1},{1,2},{2,3},{3,0},{4,5},{5,6},{6,7},{7,4},{8,9},{9,10},{10,1... | collective-permute-start | bytes 1572872 | tf_op jit(solution)/shard_map/ppermute | solution.py:59
  9.2 27.1 %collective-permute-start.1 = (bf16[128,2048]{0,1:T(8,128)(2,1)S(1)}, bf16[128,2048]{0,1:T(8,128)(2,1)}, u32[]{:S(2)}, u32[]{:S(2)}) collective-permute-start(bf16[128,2048]{0,1:T(8,128)(2,1)S(1)} %get-tuple-element.22), channel_id=1, source_target_pairs={{0,2},{1,3},{2,0},{3,1},{4,6},{5,7},{6,4},{7,5},{8,10},{9,11},{10,... | collective-permute-start | bytes 1572872 | tf_op jit(solution)/shard_map/ppermute | solution.py:59
  24.9 12.9 %collective-permute-start.2 = (bf16[128,2048]{0,1:T(8,128)(2,1)S(1)}, bf16[128,2048]{0,1:T(8,128)(2,1)}, u32[]{:S(2)}, u32[]{:S(2)}) collective-permute-start(bf16[128,2048]{0,1:T(8,128)(2,1)S(1)} %get-tuple-element.23), channel_id=1, source_target_pairs={{0,3},{1,0},{2,1},{3,2},{4,7},{5,4},{6,5},{7,6},{8,11},{9,8},{10,9... | collective-permute-start | bytes 1572872 | tf_op jit(solution)/shard_map/ppermute | solution.py:59
  39.4 2.2 %copy-start = (f32[64,16,1024]{2,1,0:T(8,128)S(1)}, f32[64,16,1024]{2,1,0:T(8,128)}, u32[]{:S(2)}) copy-start(f32[64,16,1024]{2,1,0:T(8,128)} %broadcast_in_dim.56) | copy-start | bytes 12582916
  42.7 75.6 %copy-start.3 = (s32[2,64]{1,0:T(2,128)S(1)}, s32[2,64]{1,0:T(2,128)}, u32[]{:S(2)}) copy-start(s32[2,64]{1,0:T(2,128)} %param.11) | copy-start | bytes 1540
  106.5 43.9 %all-to-all-start = ((bf16[64,16,256]{2,1,0:T(8,128)(2,1)}), bf16[64,16,256]{2,1,0:T(8,128)(2,1)S(1)}, u32[]{:S(2)}, u32[]{:S(2)}) async-start(bf16[64,16,256]{2,1,0:T(8,128)(2,1)} %bitcast.2), calls=%async_computation | async-start | bytes 1048576 | tf_op jit(solution)/shard_map/all_to_all | solution.py:43
  118.2 40.4 %copy-start.2 = (f32[2,8,16,256]{3,2,1,0:T(8,128)S(1)}, f32[2,8,16,256]{3,2,1,0:T(8,128)}, u32[]{:S(2)}) copy-start(f32[2,8,16,256]{3,2,1,0:T(8,128)} %param.13) | copy-start | bytes 786436
  123.6 27.2 %collective-permute-start.3 = (bf16[8,16,256]{2,0,1:T(8,128)(2,1)S(1)}, bf16[8,16,256]{2,0,1:T(8,128)(2,1)S(1)}, u32[]{:S(2)}, u32[]{:S(2)}) collective-permute-start(bf16[8,16,256]{2,0,1:T(8,128)(2,1)S(1)} %get-tuple-element.18), channel_id=1, source_target_pairs={{0,4},{4,8},{8,12},{12,0},{1,5},{5,9},{9,13},{13,1},{2,6},{6,10},{... | collective-permute-start | bytes 196616 | tf_op jit(solution)/shard_map/ppermute | solution.py:78
  134.5 21.1 %collective-permute-start.4 = (bf16[8,16,256]{2,0,1:T(8,128)(2,1)S(1)}, bf16[8,16,256]{2,0,1:T(8,128)(2,1)S(1)}, u32[]{:S(2)}, u32[]{:S(2)}) collective-permute-start(bf16[8,16,256]{2,0,1:T(8,128)(2,1)S(1)} %get-tuple-element.19), channel_id=1, source_target_pairs={{0,8},{4,12},{8,0},{12,4},{1,9},{5,13},{9,1},{13,5},{2,10},{6,14},... | collective-permute-start | bytes 196616 | tf_op jit(solution)/shard_map/ppermute | solution.py:78
  146.4 12.2 %collective-permute-start.5 = (bf16[8,16,256]{2,0,1:T(8,128)(2,1)S(1)}, bf16[8,16,256]{2,0,1:T(8,128)(2,1)S(1)}, u32[]{:S(2)}, u32[]{:S(2)}) collective-permute-start(bf16[8,16,256]{2,0,1:T(8,128)(2,1)S(1)} %get-tuple-element.20), channel_id=1, source_target_pairs={{0,12},{4,0},{8,4},{12,8},{1,13},{5,1},{9,5},{13,9},{2,14},{6,2},{... | collective-permute-start | bytes 196616 | tf_op jit(solution)/shard_map/ppermute | solution.py:78

commit v2 on v1

v2 whole, which is shorter than its diff:
```python
import functools

import jax
import jax.numpy as jnp
from jax import lax
from jax.experimental import pallas as pl
from jax.experimental.pallas import tpu as pltpu
from jax.sharding import Mesh, PartitionSpec as P

inner_step = 0.02
momentum_rate = 0.9
outer_rate = 0.7

PATH = ("zl", "y", "core")
FSDP = ("zh", "x")
NX = 4
NZ = 4
LIMIT = 24 * 2**20
SMEM = pl.BlockSpec(memory_space=pltpu.SMEM)
VMEM = pl.BlockSpec(memory_space=pltpu.VMEM)


def shift(axis, size, by):
    return [(i, (i + by) % size) for i in range(size)]


def params():
    return pltpu.CompilerParams(vmem_limit_bytes=LIMIT)


def pack_kernel(where, cot, hid, *outs):
    width = cot.shape[2]
    cols = hid.shape[2] // (NX * NZ)
    for k, out in enumerate(outs):
        to = (where[1] + k) % NX
        out[:, :width] = cot[0]
        for j in range(NZ):
            z = (where[0] + j) % NZ
            start = pl.multiple_of((z * NX + to) * cols, cols)
            out[:, width + j * cols : width + (j + 1) * cols] = hid[0, :, pl.ds(start, cols)]


def masked_product(where, pieces, at, block, first, last):
    rows = pieces[0].shape[0]
    left = []
    for k, piece in enumerate(pieces):
        source = (where[1] - k + NX) % NX
        token = (where[0] * NX + source) * rows + lax.broadcasted_iota(jnp.int32, (rows, block), 0)
        value = piece[:, pl.ds(at, block)].astype(jnp.float32)
        left.append(jnp.where(token < where[2], value, 0.0).astype(jnp.bfloat16))
    return inner_step * lax.dot_general(
        jnp.concatenate(left, axis=0),
        jnp.concatenate([piece[:, first:last] for piece in pieces], axis=0),
        (((0,), (0,)), ((), ())),
        preferred_element_type=jnp.float32,
    )


def grad_kernel(where, *refs):
    *pieces, drift, out = refs
    block, cols = drift.shape[2:]
    at = pl.multiple_of(pl.program_id(0) * block, block)
    first = pieces[0].shape[1] - NZ * cols
    part = masked_product(where, pieces, at, block, first, first + NZ * cols)
    out[:, :cols] = (part[:, :cols] + drift[1, 0].astype(jnp.float32)).astype(out.dtype)
    out[:, cols : NZ * cols] = part[:, cols:].astype(out.dtype)
    out[:, NZ * cols :] = drift[0, 0]


def add_paths(weights, modules, level, got, at, total):
    wide = total.shape[2]

    def add(p, carry):
        m = modules[level, p]
        total[m] = total[m] + weights[level, p] * got[p, :, at : at + wide].astype(jnp.float32)
        return carry

    lax.fori_loop(0, got.shape[0], add, 0, unroll=4)


def level1_kernel(where, weights, modules, got, own, out, total):
    cols = out.shape[3]
    total[...] = jnp.zeros_like(total)
    add_paths(weights, modules, 1, got, 0, total)
    own[...] = total[:, :, :cols]
    out[where[0]] = jnp.zeros(out.shape[1:], out.dtype)
    for k in range(1, NZ):
        out[(where[0] + k) % NZ] = total[:, :, k * cols : (k + 1) * cols].astype(out.dtype)


def level0_kernel(weights, modules, got, out):
    out[...] = jnp.zeros_like(out)
    add_paths(weights, modules, 0, got, got.shape[2] - out.shape[2], out)


def update_kernel(average0, own, parts, outer_params, outer_moment, new_params, new_moment):
    for level in range(2):
        if level == 0:
            average = average0[...]
        else:
            average = functools.reduce(lambda a, b: a + b, [parts[k].astype(jnp.float32) for k in range(NZ)])
            average = average + own[...]
        moment = momentum_rate * outer_moment[level] + average
        new_moment[level] = moment
        new_params[level] = outer_params[level] - outer_rate * (average + momentum_rate * moment)


def body(cotangent, hidden, drift, counts, assignment, outer_params, outer_moment):
    path_index = lax.axis_index(PATH)
    zh = lax.axis_index("zh")
    x = lax.axis_index("x")
    paths = counts.shape[0]
    modules = outer_params.shape[1]
    owner_rows = outer_params.shape[2]
    cols = outer_params.shape[3]
    rows = cotangent.shape[1]
    width = cotangent.shape[2]
    packed_shape = (rows, width + NZ * cols)
    bf16, f32 = jnp.bfloat16, jnp.float32

    place = jnp.stack([zh, x]).astype(jnp.int32)
    packed = pl.pallas_call(
        pack_kernel,
        out_shape=[jax.ShapeDtypeStruct(packed_shape, bf16)] * NX,
        in_specs=[SMEM, VMEM, VMEM],
        out_specs=[VMEM] * NX,
        compiler_params=params(),
    )(place, cotangent, hidden)
    pieces = [packed[0]] + [lax.ppermute(packed[k], "x", shift("x", NX, k)) for k in range(1, NX)]

    member = (assignment[:, None, :] == jnp.arange(modules, dtype=jnp.int32)[None, :, None]).astype(f32)
    weighted = member * counts[None, None, :].astype(f32)
    shares = weighted / jnp.sum(weighted, axis=-1, keepdims=True)
    weights = jnp.sum(shares, axis=1)
    my_count = jnp.sum(jnp.where(jnp.arange(paths, dtype=jnp.int32) == path_index, counts, 0))
    where = jnp.stack([zh, x, my_count]).astype(jnp.int32)

    block = 256
    whole = pl.BlockSpec(packed_shape, lambda r: (0, 0))
    wide = (NZ + 1) * cols
    send = pl.pallas_call(
        grad_kernel,
        out_shape=jax.ShapeDtypeStruct((width, wide), bf16),
        grid=(width // block,),
        in_specs=[SMEM]
        + [whole] * NX
        + [pl.BlockSpec((2, 1, block, cols), lambda r: (0, 0, r, 0))],
        out_specs=pl.BlockSpec((block, wide), lambda r: (r, 0)),
        compiler_params=params(),
    )(where, *pieces, drift)
    got = lax.all_to_all(
        send.reshape(paths, owner_rows, wide), PATH, split_axis=0, concat_axis=0, tiled=True
    )
    own, sums = pl.pallas_call(
        level1_kernel,
        out_shape=[
            jax.ShapeDtypeStruct((modules, owner_rows, cols), f32),
            jax.ShapeDtypeStruct((NZ, modules, owner_rows, cols), bf16),
        ],
        in_specs=[SMEM, SMEM, SMEM, VMEM],
        out_specs=[VMEM, VMEM],
        scratch_shapes=[pltpu.VMEM((modules, owner_rows, NZ * cols), f32)],
        compiler_params=params(),
    )(place, weights, assignment, got)
    parts = lax.all_to_all(sums, "zh", split_axis=0, concat_axis=0, tiled=True)
    average0 = pl.pallas_call(
        level0_kernel,
        out_shape=jax.ShapeDtypeStruct((modules, owner_rows, cols), f32),
        in_specs=[SMEM, SMEM, VMEM],
        out_specs=VMEM,
        compiler_params=params(),
    )(weights, assignment, got)
    return pl.pallas_call(
        update_kernel,
        out_shape=[jax.ShapeDtypeStruct(outer_params.shape, f32)] * 2,
        in_specs=[VMEM] * 5,
        out_specs=[VMEM] * 2,
        compiler_params=params(),
    )(average0, own, parts, outer_params, outer_moment)


def solution(mesh):
    fine = Mesh(mesh.devices.reshape(4, 8, 2, 4, 4), ("zl", "y", "core", "zh", "x"))
    placed = (
        P(PATH, FSDP, None),
        P(PATH, FSDP, None),
        P(None, PATH, None, FSDP),
        P(),
        P(),
        P(None, None, PATH, FSDP),
        P(None, None, PATH, FSDP),
    )
    return jax.shard_map(
        lambda *a: tuple(body(*a)),
        mesh=fine,
        in_specs=placed,
        out_specs=(P(None, None, PATH, FSDP), P(None, None, PATH, FSDP)),
        check_vma=False,
    )
```

time: 162 us -> 163 us (level)
  the two profiles are of different devices: /device:TPU:2 before, /device:TPU:146 now
where the time goes in v2:
time: 163 us
  waiting for transfers between devices  106 us (65%)
  starting transfers between devices  38.6 us (24%)
  Pallas kernels  8.08 us (5%)
  local copies, waits for them, and re-layouts  6.49 us (4%)
  other arithmetic  2.26 us (1%)
    all_to_all x1, waiting for transfers between devices, body(): lax.all_to_all(send.reshape(paths, owner_rows, wide), PATH, split_axis=0,...  67.5 us
    all_to_all x1, waiting for transfers between devices, body(): parts = lax.all_to_all(sums, 'zh', split_axis=0, concat_axis=0, tiled=True)  20 us
    ppermute x3, waiting for transfers between devices, body(): lax.ppermute(packed[k], 'x', shift('x', NX, k))  19 us
    all_to_all x1, starting transfers between devices, body(): parts = lax.all_to_all(sums, 'zh', split_axis=0, concat_axis=0, tiled=True)  16.3 us
    all_to_all x1, starting transfers between devices, body(): lax.all_to_all(send.reshape(paths, owner_rows, wide), PATH, split_axis=0,...  11.9 us
    ppermute x3, starting transfers between devices, body(): lax.ppermute(packed[k], 'x', shift('x', NX, k))  10.5 us
    unnamed x18, local copies, waits for them, and re-layouts  6.49 us
  transfers between devices with their start and end apart: 5, of which 5 were waited for; matrix products, arithmetic and copies ran while one was open for 1% of the time, Pallas kernels for 1%

profile of v2, /device:TPU:146, one launch (start us, length us, event | category | flops | bytes accessed | tf_op | source)
XLA Modules:
  0.0 162.7 jit_solution(10738858357402246992)
XLA Ops:
  0.6 0.1 pad_add_fusion.1.where
  0.7 0.0 copy-start.1
  0.7 1.2 copy-done.1
  1.9 0.0 copy-start.3
  1.9 0.9 copy-done.3
  2.9 1.7 %shard_map.86 = (bf16[128,2048]{1,0:T(8,128)(2,1)S(1)}, bf16[128,2048]{1,0:T(8,128)(2,1)}, bf16[128,2048]{1,0:T(8,128)(2,1)}, bf16[128,2048]{1,0:T(8,128)(2,1)S(1)}) custom-call(s32[2]{0:T(128)S(1)} %pad_add_fusion.1.where, bf16[1,128,1024]{2,1,0:T(8,128)(2,1)S(1)} %copy-done.3, bf16[1,128,4096]{2,1,0:T(8,128)(2,1)S(1)} %copy-done.1), custom_call_target="tpu_custom_call" | custom-call | tf_op jit(solution)/shard_map/pallas_call | solution.py:122
  4.6 3.4 %collective-permute-start = (bf16[128,2048]{1,0:T(8,128)(2,1)}, bf16[128,2048]{1,0:T(8,128)(2,1)S(1)}, u32[]{:S(2)}, u32[]{:S(2)}) collective-permute-start(bf16[128,2048]{1,0:T(8,128)(2,1)} %get-tuple-element.9), channel_id=1, source_target_pairs={{0,1},{1,2},{2,3},{3,0},{4,5},{5,6},{6,7},{7,4},{8,9},{9,10},{10,1... | collective-permute-start | bytes 1572872 | tf_op jit(solution)/shard_map/ppermute | solution.py:129
  8.0 3.0 %collective-permute-start.1 = (bf16[128,2048]{1,0:T(8,128)(2,1)}, bf16[128,2048]{1,0:T(8,128)(2,1)S(1)}, u32[]{:S(2)}, u32[]{:S(2)}) collective-permute-start(bf16[128,2048]{1,0:T(8,128)(2,1)} %get-tuple-element.10), channel_id=1, source_target_pairs={{0,2},{1,3},{2,0},{3,1},{4,6},{5,7},{6,4},{7,5},{8,10},{9,11},{10,... | collective-permute-start | bytes 1572872 | tf_op jit(solution)/shard_map/ppermute | solution.py:129
  11.0 4.1 %collective-permute-start.2 = (bf16[128,2048]{1,0:T(8,128)(2,1)S(1)}, bf16[128,2048]{1,0:T(8,128)(2,1)S(1)}, u32[]{:S(2)}, u32[]{:S(2)}) collective-permute-start(bf16[128,2048]{1,0:T(8,128)(2,1)S(1)} %get-tuple-element.11), channel_id=1, source_target_pairs={{0,3},{1,0},{2,1},{3,2},{4,7},{5,4},{6,5},{7,6},{8,11},{9,8},{10,9... | collective-permute-start | bytes 1572872 | tf_op jit(solution)/shard_map/ppermute | solution.py:129
  15.1 1.4 fusion.6
  16.5 0.7 pad_add_fusion.where
  17.2 4.3 %collective-permute-done.refs_1_ = bf16[128,2048]{1,0:T(8,128)(2,1)S(1)} collective-permute-done((bf16[128,2048]{1,0:T(8,128)(2,1)}, bf16[128,2048]{1,0:T(8,128)(2,1)S(1)}, u32[]{:S(2)}, u32[]{:S(2)}) %collective-permute-start) | collective-permute-done | bytes 524320 | tf_op jit(solution)/shard_map/ppermute | solution.py:129
  21.5 5.0 %collective-permute-done.1.refs_2_ = bf16[128,2048]{1,0:T(8,128)(2,1)S(1)} collective-permute-done((bf16[128,2048]{1,0:T(8,128)(2,1)}, bf16[128,2048]{1,0:T(8,128)(2,1)S(1)}, u32[]{:S(2)}, u32[]{:S(2)}) %collective-permute-start.1) | collective-permute-done | bytes 524320 | tf_op jit(solution)/shard_map/ppermute | solution.py:129
  26.5 9.7 %collective-permute-done.2.refs_3_ = bf16[128,2048]{1,0:T(8,128)(2,1)S(1)} collective-permute-done((bf16[128,2048]{1,0:T(8,128)(2,1)S(1)}, bf16[128,2048]{1,0:T(8,128)(2,1)S(1)}, u32[]{:S(2)}, u32[]{:S(2)}) %collective-permute-start.2) | collective-permute-done | bytes 524320 | tf_op jit(solution)/shard_map/ppermute | solution.py:129
  36.2 1.2 copy-done.2
  37.4 2.7 %shard_map.87 = bf16[1024,1280]{1,0:T(8,128)(2,1)S(1)} custom-call(s32[3]{0:T(128)S(1)} %pad_add_fusion.where, bf16[128,2048]{1,0:T(8,128)(2,1)S(1)} %get-tuple-element.8.refs_0_, bf16[128,2048]{1,0:T(8,128)(2,1)S(1)} %collective-permute-done.refs_1_, bf16[128,2048]{1,0:T(8,128)(2,1)S(1)} %collective-permute-done.1.refs_2_, ...), custom_call_target="tpu_custom_call" | custom-call | tf_op jit(solution)/shard_map/pallas_call | solution.py:141
  40.1 0.0 copy-start
  40.1 1.5 copy-done
  41.6 11.9 %all-to-all-start = ((bf16[64,16,1280]{2,1,0:T(8,128)(2,1)}), bf16[64,16,1280]{2,1,0:T(8,128)(2,1)S(1)}, u32[]{:S(2)}, u32[]{:S(2)}) async-start(bf16[64,16,1280]{2,1,0:T(8,128)(2,1)} %bitcast.4), calls=%async_computation | async-start | bytes 5242880 | tf_op jit(solution)/shard_map/all_to_all | solution.py:151
  53.5 0.0 copy-done.8
  53.5 0.1 fusion.8.weights
  53.6 0.0 copy-start.5
  53.6 67.5 %all-to-all-done.got = bf16[64,16,1280]{2,1,0:T(8,128)(2,1)S(1)} async-done(((bf16[64,16,1280]{2,1,0:T(8,128)(2,1)}), bf16[64,16,1280]{2,1,0:T(8,128)(2,1)S(1)}, u32[]{:S(2)}, u32[]{:S(2)}) %all-to-all-start) | async-done | bytes 2621472 | tf_op jit(solution)/shard_map/all_to_all | solution.py:151
  121.1 2.0 %shard_map.89 = (f32[8,16,256]{2,1,0:T(8,128)S(1)}, bf16[4,8,16,256]{3,2,1,0:T(8,128)(2,1)}) custom-call(s32[2]{0:T(128)S(1)} %pad_add_fusion.1.where, f32[2,64]{1,0:T(2,128)S(1)} %fusion.8.weights, s32[2,64]{1,0:T(2,128)S(1)} %copy-done.8, bf16[64,16,1280]{2,1,0:T(8,128)(2,1)S(1)} %all-to-all-done.got), custom_call_target="tpu_custom_call" | custom-call | tf_op jit(solution)/shard_map/pallas_call | solution.py:154
  123.1 0.7 copy-done.6
  123.7 16.3 %all-to-all-start.1 = ((bf16[4,8,16,256]{3,2,1,0:T(8,128)(2,1)}), bf16[4,8,16,256]{3,2,1,0:T(8,128)(2,1)S(1)}, u32[]{:S(2)}, u32[]{:S(2)}) async-start(bf16[4,8,16,256]{3,2,1,0:T(8,128)(2,1)} %get-tuple-element.13), calls=%async_computation.1 | async-start | bytes 524288 | tf_op jit(solution)/shard_map/all_to_all | solution.py:165
  140.1 0.9 shard_map.88.average0
  140.9 20.0 %all-to-all-done.1.parts = bf16[4,8,16,256]{3,2,1,0:T(8,128)(2,1)S(1)} async-done(((bf16[4,8,16,256]{3,2,1,0:T(8,128)(2,1)}), bf16[4,8,16,256]{3,2,1,0:T(8,128)(2,1)S(1)}, u32[]{:S(2)}, u32[]{:S(2)}) %all-to-all-start.1) | async-done | bytes 262176 | tf_op jit(solution)/shard_map/all_to_all | solution.py:165
  160.9 0.0 copy-done.4
  160.9 0.0 copy-done.5
  160.9 0.9 copy-done.7
  161.8 0.9 shard_map.90
  (5 shorter events, 0.0 us)
Async XLA Ops:
  0.7 1.2 copy-start.1
  1.9 0.9 copy-start.3
  4.6 16.9 %collective-permute-start = (bf16[128,2048]{1,0:T(8,128)(2,1)}, bf16[128,2048]{1,0:T(8,128)(2,1)S(1)}, u32[]{:S(2)}, u32[]{:S(2)}) collective-permute-start(bf16[128,2048]{1,0:T(8,128)(2,1)} %get-tuple-element.9), channel_id=1, source_target_pairs={{0,1},{1,2},{2,3},{3,0},{4,5},{5,6},{6,7},{7,4},{8,9},{9,10},{10,1... | collective-permute-start | bytes 1572872 | tf_op jit(solution)/shard_map/ppermute | solution.py:129
  8.0 18.5 %collective-permute-start.1 = (bf16[128,2048]{1,0:T(8,128)(2,1)}, bf16[128,2048]{1,0:T(8,128)(2,1)S(1)}, u32[]{:S(2)}, u32[]{:S(2)}) collective-permute-start(bf16[128,2048]{1,0:T(8,128)(2,1)} %get-tuple-element.10), channel_id=1, source_target_pairs={{0,2},{1,3},{2,0},{3,1},{4,6},{5,7},{6,4},{7,5},{8,10},{9,11},{10,... | collective-permute-start | bytes 1572872 | tf_op jit(solution)/shard_map/ppermute | solution.py:129
  11.0 25.2 %collective-permute-start.2 = (bf16[128,2048]{1,0:T(8,128)(2,1)S(1)}, bf16[128,2048]{1,0:T(8,128)(2,1)S(1)}, u32[]{:S(2)}, u32[]{:S(2)}) collective-permute-start(bf16[128,2048]{1,0:T(8,128)(2,1)S(1)} %get-tuple-element.11), channel_id=1, source_target_pairs={{0,3},{1,0},{2,1},{3,2},{4,7},{5,4},{6,5},{7,6},{8,11},{9,8},{10,9... | collective-permute-start | bytes 1572872 | tf_op jit(solution)/shard_map/ppermute | solution.py:129
  36.2 1.2 copy-start.2
  40.1 1.5 copy-start
  41.6 11.9 %copy-start.8 = (s32[2,64]{1,0:T(2,128)S(1)}, s32[2,64]{1,0:T(2,128)}, u32[]{:S(2)}) copy-start(s32[2,64]{1,0:T(2,128)} %modules.3) | copy-start | bytes 1540
  41.6 79.5 %all-to-all-start = ((bf16[64,16,1280]{2,1,0:T(8,128)(2,1)}), bf16[64,16,1280]{2,1,0:T(8,128)(2,1)S(1)}, u32[]{:S(2)}, u32[]{:S(2)}) async-start(bf16[64,16,1280]{2,1,0:T(8,128)(2,1)} %bitcast.4), calls=%async_computation | async-start | bytes 5242880 | tf_op jit(solution)/shard_map/all_to_all | solution.py:151
  53.6 107.3 %copy-start.4 = (f32[2,8,16,256]{3,2,1,0:T(8,128)S(1)}, f32[2,8,16,256]{3,2,1,0:T(8,128)}, u32[]{:S(2)}) copy-start(f32[2,8,16,256]{3,2,1,0:T(8,128)} %outer_params.1) | copy-start | bytes 786436
  53.6 107.3 %copy-start.5 = (f32[2,8,16,256]{3,2,1,0:T(8,128)S(1)}, f32[2,8,16,256]{3,2,1,0:T(8,128)}, u32[]{:S(2)}) copy-start(f32[2,8,16,256]{3,2,1,0:T(8,128)} %outer_moment.1) | copy-start | bytes 786436
  123.1 0.7 copy-start.6
  123.7 37.2 %all-to-all-start.1 = ((bf16[4,8,16,256]{3,2,1,0:T(8,128)(2,1)}), bf16[4,8,16,256]{3,2,1,0:T(8,128)(2,1)S(1)}, u32[]{:S(2)}, u32[]{:S(2)}) async-start(bf16[4,8,16,256]{3,2,1,0:T(8,128)(2,1)} %get-tuple-element.13), calls=%async_computation.1 | async-start | bytes 524288 | tf_op jit(solution)/shard_map/all_to_all | solution.py:165
  160.9 0.9 copy-start.7

commit v3 on v2

--- a/solution.py
+++ b/solution.py
@@ -56,50 +56,55 @@
     )
 
 
-def grad_kernel(where, *refs):
-    *pieces, drift, out = refs
+def foreign_kernel(where, *refs):
+    *pieces, out = refs
+    block, wide = out.shape
+    at = pl.multiple_of(pl.program_id(0) * block, block)
+    last = pieces[0].shape[1]
+    out[...] = masked_product(where, pieces, at, block, last - wide, last).astype(out.dtype)
+
+
+def own_kernel(where, *refs):
+    *pieces, drift, _, out = refs
     block, cols = drift.shape[2:]
     at = pl.multiple_of(pl.program_id(0) * block, block)
     first = pieces[0].shape[1] - NZ * cols
-    part = masked_product(where, pieces, at, block, first, first + NZ * cols)
-    out[:, :cols] = (part[:, :cols] + drift[1, 0].astype(jnp.float32)).astype(out.dtype)
-    out[:, cols : NZ * cols] = part[:, cols:].astype(out.dtype)
-    out[:, NZ * cols :] = drift[0, 0]
-
-
-def add_paths(weights, modules, level, got, at, total):
-    wide = total.shape[2]
+    part = masked_product(where, pieces, at, block, first, first + cols)
+    out[:, :cols] = (part + drift[1, 0].astype(jnp.float32)).astype(out.dtype)
+    out[:, cols:] = drift[0, 0]
+
+
+def module_kernel(weights, modules, got, *refs):
+    *outs, total = refs
+    cols = outs[0].shape[2]
+    total[...] = jnp.zeros_like(total)
 
     def add(p, carry):
-        m = modules[level, p]
-        total[m] = total[m] + weights[level, p] * got[p, :, at : at + wide].astype(jnp.float32)
+        m = modules[1, p]
+        total[m] = total[m] + weights[1, p] * got[p].astype(jnp.float32)
         return carry
 
     lax.fori_loop(0, got.shape[0], add, 0, unroll=4)
-
-
-def level1_kernel(where, weights, modules, got, own, out, total):
-    cols = out.shape[3]
-    total[...] = jnp.zeros_like(total)
-    add_paths(weights, modules, 1, got, 0, total)
-    own[...] = total[:, :, :cols]
-    out[where[0]] = jnp.zeros(out.shape[1:], out.dtype)
-    for k in range(1, NZ):
-        out[(where[0] + k) % NZ] = total[:, :, k * cols : (k + 1) * cols].astype(out.dtype)
-
-
-def level0_kernel(weights, modules, got, out):
-    out[...] = jnp.zeros_like(out)
-    add_paths(weights, modules, 0, got, got.shape[2] - out.shape[2], out)
-
-
-def update_kernel(average0, own, parts, outer_params, outer_moment, new_params, new_moment):
+    for k, out in enumerate(outs):
+        out[...] = total[:, :, k * cols : (k + 1) * cols].astype(out.dtype)
+
+
+def update_kernel(weights, modules, got, *refs):
+    *parts, outer_params, outer_moment, new_params, new_moment, total = refs
+    cols = outer_params.shape[3]
+    total[0] = jnp.zeros(total.shape[1:], jnp.float32)
+    total[1] = functools.reduce(lambda a, b: a + b, [part[...].astype(jnp.float32) for part in parts])
+
+    def add(p, carry):
+        for level in range(2):
+            m = modules[level, p]
+            value = got[p, :, (1 - level) * cols : (2 - level) * cols].astype(jnp.float32)
+            total[level, m] = total[level, m] + weights[level, p] * value
+        return carry
+
+    lax.fori_loop(0, got.shape[0], add, 0, unroll=4)
     for level in range(2):
-        if level == 0:
-            average = average0[...]
-        else:
-            average = functools.reduce(lambda a, b: a + b, [parts[k].astype(jnp.float32) for k in range(NZ)])
-            average = average + own[...]
+        average = total[level]
         moment = momentum_rate * outer_moment[level] + average
         new_moment[level] = moment
         new_params[level] = outer_params[level] - outer_rate * (average + momentum_rate * moment)
@@ -116,6 +121,7 @@
     rows = cotangent.shape[1]
     width = cotangent.shape[2]
     packed_shape = (rows, width + NZ * cols)
+    foreign_cols = (NZ - 1) * cols
     bf16, f32 = jnp.bfloat16, jnp.float32
 
     place = jnp.stack([zh, x]).astype(jnp.int32)
@@ -137,46 +143,47 @@
 
     block = 256
     whole = pl.BlockSpec(packed_shape, lambda r: (0, 0))
-    wide = (NZ + 1) * cols
-    send = pl.pallas_call(
-        grad_kernel,
-        out_shape=jax.ShapeDtypeStruct((width, wide), bf16),
+    foreign = pl.pallas_call(
+        foreign_kernel,
+        out_shape=jax.ShapeDtypeStruct((width, foreign_cols), bf16),
+        grid=(width // block,),
+        in_specs=[SMEM] + [whole] * NX,
+        out_specs=pl.BlockSpec((block, foreign_cols), lambda r: (r, 0)),
+        compiler_params=params(),
+    )(where, *pieces)
+    got_foreign = lax.all_to_all(
+        foreign.reshape(paths, owner_rows, foreign_cols), PATH, split_axis=0, concat_axis=0, tiled=True
+    )
+    own = pl.pallas_call(
+        own_kernel,
+        out_shape=jax.ShapeDtypeStruct((width, 2 * cols), bf16),
         grid=(width // block,),
         in_specs=[SMEM]
         + [whole] * NX
-        + [pl.BlockSpec((2, 1, block, cols), lambda r: (0, 0, r, 0))],
-        out_specs=pl.BlockSpec((block, wide), lambda r: (r, 0)),
-        compiler_params=params(),
-    )(where, *pieces, drift)
-    got = lax.all_to_all(
-        send.reshape(paths, owner_rows, wide), PATH, split_axis=0, concat_axis=0, tiled=True
-    )
-    own, sums = pl.pallas_call(
-        level1_kernel,
-        out_shape=[
-            jax.ShapeDtypeStruct((modules, owner_rows, cols), f32),
-            jax.ShapeDtypeStruct((NZ, modules, owner_rows, cols), bf16),
-        ],
-        in_specs=[SMEM, SMEM, SMEM, VMEM],
-        out_specs=[VMEM, VMEM],
-        scratch_shapes=[pltpu.VMEM((modules, owner_rows, NZ * cols), f32)],
-        compiler_params=params(),
-    )(place, weights, assignment, got)
-    parts = lax.all_to_all(sums, "zh", split_axis=0, concat_axis=0, tiled=True)
-    average0 = pl.pallas_call(
-        level0_kernel,
-        out_shape=jax.ShapeDtypeStruct((modules, owner_rows, cols), f32),
+        + [pl.BlockSpec((2, 1, block, cols), lambda r: (0, 0, r, 0)), pl.BlockSpec(memory_space=pl.ANY)],
+        out_specs=pl.BlockSpec((block, 2 * cols), lambda r: (r, 0)),
+        compiler_params=params(),
+    )(where, *pieces, drift, foreign)
+    got_own = lax.all_to_all(
+        own.reshape(paths, owner_rows, 2 * cols), PATH, split_axis=0, concat_axis=0, tiled=True
+    )
+    sums = pl.pallas_call(
+        module_kernel,
+        out_shape=[jax.ShapeDtypeStruct((modules, owner_rows, cols), bf16)] * (NZ - 1),
         in_specs=[SMEM, SMEM, VMEM],
-        out_specs=VMEM,
-        compiler_params=params(),
-    )(weights, assignment, got)
+        out_specs=[VMEM] * (NZ - 1),
+        scratch_shapes=[pltpu.VMEM((modules, owner_rows, foreign_cols), f32)],
+        compiler_params=params(),
+    )(weights, assignment, got_foreign)
+    parts = [lax.ppermute(sums[k - 1], "zh", shift("zh", NZ, k)) for k in range(1, NZ)]
     return pl.pallas_call(
         update_kernel,
         out_shape=[jax.ShapeDtypeStruct(outer_params.shape, f32)] * 2,
-        in_specs=[VMEM] * 5,
+        in_specs=[SMEM, SMEM] + [VMEM] * (NZ + 2),
         out_specs=[VMEM] * 2,
-        compiler_params=params(),
-    )(average0, own, parts, outer_params, outer_moment)
+        scratch_shapes=[pltpu.VMEM((2, modules, owner_rows, cols), f32)],
+        compiler_params=params(),
+    )(weights, assignment, got_own, *parts, outer_params, outer_moment)
 
 
 def solution(mesh):

time: 163 us -> 152 us (0.933)
  the two profiles are of different devices: /device:TPU:146 before, /device:TPU:75 now
where the time goes in v3:
time: 152 us; the launch traced here: 151 us
  waiting for transfers between devices  75.2 us (49%)
  starting transfers between devices  57.3 us (38%)
  Pallas kernels  10 us (7%)
  local copies, waits for them, and re-layouts  5.42 us (4%)
  other arithmetic  2.26 us (1%)
    all_to_all x1, waiting for transfers between devices, body(): lax.all_to_all(foreign.reshape(paths, owner_rows, foreign_cols), PATH, sp...  34.1 us
    ppermute x3, starting transfers between devices, body(): lax.ppermute(sums[k - 1], 'zh', shift('zh', NZ, k))  25.4 us
    ppermute x3, waiting for transfers between devices, body(): lax.ppermute(packed[k], 'x', shift('x', NX, k))  19.8 us
    ppermute x3, waiting for transfers between devices, body(): lax.ppermute(sums[k - 1], 'zh', shift('zh', NZ, k))  19.6 us
    all_to_all x1, starting transfers between devices, body(): lax.all_to_all(foreign.reshape(paths, owner_rows, foreign_cols), PATH, sp...  12.8 us
    ppermute x3, starting transfers between devices, body(): lax.ppermute(packed[k], 'x', shift('x', NX, k))  9.63 us
    all_to_all x1, starting transfers between devices, body(): lax.all_to_all(own.reshape(paths, owner_rows, 2 * cols), PATH, split_axis...  9.53 us
    unnamed x18, local copies, waits for them, and re-layouts  5.42 us
  transfers between devices with their start and end apart: 8, of which 6 were waited for; matrix products, arithmetic and copies ran while one was open for 1% of the time, Pallas kernels for 2%

profile of v3, /device:TPU:75, one launch (start us, length us, event | category | flops | bytes accessed | tf_op | source)
XLA Modules:
  0.0 151.0 jit_solution(83002199241654931)
XLA Ops:
  0.6 0.1 pad_add_fusion.1.where
  0.7 1.2 copy-done.3
  1.9 0.9 copy-done.5
  2.9 1.5 %shard_map.86 = (bf16[128,2048]{1,0:T(8,128)(2,1)S(1)}, bf16[128,2048]{1,0:T(8,128)(2,1)}, bf16[128,2048]{1,0:T(8,128)(2,1)S(1)}, bf16[128,2048]{1,0:T(8,128)(2,1)S(1)}) custom-call(s32[2]{0:T(128)S(1)} %pad_add_fusion.1.where, bf16[1,128,1024]{2,1,0:T(8,128)(2,1)S(1)} %copy-done.5, bf16[1,128,4096]{2,1,0:T(8,128)(2,1)S(1)} %copy-done.3), custom_call_target="tpu_custom_call" | custom-call | tf_op jit(solution)/shard_map/pallas_call | solution.py:128
  4.4 3.1 %collective-permute-start = (bf16[128,2048]{1,0:T(8,128)(2,1)}, bf16[128,2048]{1,0:T(8,128)(2,1)S(1)}, u32[]{:S(2)}, u32[]{:S(2)}) collective-permute-start(bf16[128,2048]{1,0:T(8,128)(2,1)} %get-tuple-element.10), channel_id=1, source_target_pairs={{0,1},{1,2},{2,3},{3,0},{4,5},{5,6},{6,7},{7,4},{8,9},{9,10},{10,1... | collective-permute-start | bytes 1572872 | tf_op jit(solution)/shard_map/ppermute | solution.py:135
  7.5 2.7 %collective-permute-start.1 = (bf16[128,2048]{1,0:T(8,128)(2,1)S(1)}, bf16[128,2048]{1,0:T(8,128)(2,1)S(1)}, u32[]{:S(2)}, u32[]{:S(2)}) collective-permute-start(bf16[128,2048]{1,0:T(8,128)(2,1)S(1)} %get-tuple-element.11), channel_id=1, source_target_pairs={{0,2},{1,3},{2,0},{3,1},{4,6},{5,7},{6,4},{7,5},{8,10},{9,11},{10,... | collective-permute-start | bytes 1572872 | tf_op jit(solution)/shard_map/ppermute | solution.py:135
  10.3 3.8 %collective-permute-start.2 = (bf16[128,2048]{1,0:T(8,128)(2,1)S(1)}, bf16[128,2048]{1,0:T(8,128)(2,1)S(1)}, u32[]{:S(2)}, u32[]{:S(2)}) collective-permute-start(bf16[128,2048]{1,0:T(8,128)(2,1)S(1)} %get-tuple-element.12), channel_id=1, source_target_pairs={{0,3},{1,0},{2,1},{3,2},{4,7},{5,4},{6,5},{7,6},{8,11},{9,8},{10,9... | collective-permute-start | bytes 1572872 | tf_op jit(solution)/shard_map/ppermute | solution.py:135
  14.1 1.4 fusion.6
  15.4 0.7 pad_add_fusion.where
  16.2 3.1 %collective-permute-done.refs_1_ = bf16[128,2048]{1,0:T(8,128)(2,1)S(1)} collective-permute-done((bf16[128,2048]{1,0:T(8,128)(2,1)}, bf16[128,2048]{1,0:T(8,128)(2,1)S(1)}, u32[]{:S(2)}, u32[]{:S(2)}) %collective-permute-start) | collective-permute-done | bytes 524320 | tf_op jit(solution)/shard_map/ppermute | solution.py:135
  19.3 4.1 %collective-permute-done.1.refs_2_ = bf16[128,2048]{1,0:T(8,128)(2,1)S(1)} collective-permute-done((bf16[128,2048]{1,0:T(8,128)(2,1)S(1)}, bf16[128,2048]{1,0:T(8,128)(2,1)S(1)}, u32[]{:S(2)}, u32[]{:S(2)}) %collective-permute-start.1) | collective-permute-done | bytes 524320 | tf_op jit(solution)/shard_map/ppermute | solution.py:135
  23.4 12.6 %collective-permute-done.2.refs_3_ = bf16[128,2048]{1,0:T(8,128)(2,1)S(1)} collective-permute-done((bf16[128,2048]{1,0:T(8,128)(2,1)S(1)}, bf16[128,2048]{1,0:T(8,128)(2,1)S(1)}, u32[]{:S(2)}, u32[]{:S(2)}) %collective-permute-start.2) | collective-permute-done | bytes 524320 | tf_op jit(solution)/shard_map/ppermute | solution.py:135
  36.0 3.4 %shard_map.87.refs_5_ = bf16[1024,768]{1,0:T(8,128)(2,1)} custom-call(s32[3]{0:T(128)S(1)} %pad_add_fusion.where, bf16[128,2048]{1,0:T(8,128)(2,1)S(1)} %get-tuple-element.9.refs_0_, bf16[128,2048]{1,0:T(8,128)(2,1)S(1)} %collective-permute-done.refs_1_, bf16[128,2048]{1,0:T(8,128)(2,1)S(1)} %collective-permute-done.1.refs_2_, ...), custom_call_target="tpu_custom_call" | custom-call | tf_op jit(solution)/shard_map/pallas_call | solution.py:146
  39.4 12.8 %all-to-all-start.1 = ((bf16[64,16,768]{2,1,0:T(8,128)(2,1)}), bf16[64,16,768]{2,1,0:T(8,128)(2,1)S(1)}, u32[]{:S(2)}, u32[]{:S(2)}) async-start(bf16[64,16,768]{2,1,0:T(8,128)(2,1)} %bitcast.4), calls=%async_computation.1 | async-start | bytes 3145728 | tf_op jit(solution)/shard_map/all_to_all | solution.py:154
  52.2 1.0 copy-done.2
  53.3 1.2 copy-done.4
  54.5 1.9 %shard_map.88 = bf16[1024,512]{1,0:T(8,128)(2,1)S(1)} custom-call(s32[3]{0:T(128)S(1)} %pad_add_fusion.where, bf16[128,2048]{1,0:T(8,128)(2,1)S(1)} %get-tuple-element.9.refs_0_, bf16[128,2048]{1,0:T(8,128)(2,1)S(1)} %collective-permute-done.refs_1_, bf16[128,2048]{1,0:T(8,128)(2,1)S(1)} %collective-permute-done.1.refs_2_, bf16[128,2048]{1,0:T(8,128)(2,1)S(1)} %copy-done.2, ...), custom_call_target="tpu_custom_call" | custom-call | tf_op jit(solution)/shard_map/pallas_call | solution.py:157
  56.4 0.0 copy-start
  56.4 1.0 copy-done
  57.4 34.1 %all-to-all-done.1.got = bf16[64,16,768]{2,1,0:T(8,128)(2,1)S(1)} async-done(((bf16[64,16,768]{2,1,0:T(8,128)(2,1)}), bf16[64,16,768]{2,1,0:T(8,128)(2,1)S(1)}, u32[]{:S(2)}, u32[]{:S(2)}) %all-to-all-start.1) | async-done | bytes 1572896 | tf_op jit(solution)/shard_map/all_to_all | solution.py:154
  91.5 9.5 %all-to-all-start = ((bf16[64,16,512]{2,1,0:T(8,128)(2,1)}), bf16[64,16,512]{2,1,0:T(8,128)(2,1)S(1)}, u32[]{:S(2)}, u32[]{:S(2)}) async-start(bf16[64,16,512]{2,1,0:T(8,128)(2,1)} %bitcast.5), calls=%async_computation | async-start | bytes 2097152 | tf_op jit(solution)/shard_map/all_to_all | solution.py:167
  101.1 0.1 fusion.8.weights
  101.2 1.1 shard_map.89
  102.3 10.6 %collective-permute-start.3 = (bf16[8,16,256]{2,1,0:T(8,128)(2,1)S(1)}, bf16[8,16,256]{2,1,0:T(8,128)(2,1)S(1)}, u32[]{:S(2)}, u32[]{:S(2)}) collective-permute-start(bf16[8,16,256]{2,1,0:T(8,128)(2,1)S(1)} %get-tuple-element.13), channel_id=1, source_target_pairs={{0,4},{4,8},{8,12},{12,0},{1,5},{5,9},{9,13},{13,1},{2,6},{6,10},{... | collective-permute-start | bytes 196616 | tf_op jit(solution)/shard_map/ppermute | solution.py:178
  113.0 11.6 %collective-permute-start.4 = (bf16[8,16,256]{2,1,0:T(8,128)(2,1)S(1)}, bf16[8,16,256]{2,1,0:T(8,128)(2,1)S(1)}, u32[]{:S(2)}, u32[]{:S(2)}) collective-permute-start(bf16[8,16,256]{2,1,0:T(8,128)(2,1)S(1)} %get-tuple-element.14), channel_id=1, source_target_pairs={{0,8},{4,12},{8,0},{12,4},{1,9},{5,13},{9,1},{13,5},{2,10},{6,14},... | collective-permute-start | bytes 196616 | tf_op jit(solution)/shard_map/ppermute | solution.py:178
  124.5 3.2 %collective-permute-start.5 = (bf16[8,16,256]{2,1,0:T(8,128)(2,1)S(1)}, bf16[8,16,256]{2,1,0:T(8,128)(2,1)S(1)}, u32[]{:S(2)}, u32[]{:S(2)}) collective-permute-start(bf16[8,16,256]{2,1,0:T(8,128)(2,1)S(1)} %get-tuple-element.15), channel_id=1, source_target_pairs={{0,12},{4,0},{8,4},{12,8},{1,13},{5,1},{9,5},{13,9},{2,14},{6,2},{... | collective-permute-start | bytes 196616 | tf_op jit(solution)/shard_map/ppermute | solution.py:178
  127.7 1.7 %all-to-all-done.got = bf16[64,16,512]{2,1,0:T(8,128)(2,1)S(1)} async-done(((bf16[64,16,512]{2,1,0:T(8,128)(2,1)}), bf16[64,16,512]{2,1,0:T(8,128)(2,1)S(1)}, u32[]{:S(2)}, u32[]{:S(2)}) %all-to-all-start) | async-done | bytes 1048608 | tf_op jit(solution)/shard_map/all_to_all | solution.py:167
  129.4 19.6 %collective-permute-done.3.refs_0_ = bf16[8,16,256]{2,1,0:T(8,128)(2,1)S(1)} collective-permute-done((bf16[8,16,256]{2,1,0:T(8,128)(2,1)S(1)}, bf16[8,16,256]{2,1,0:T(8,128)(2,1)S(1)}, u32[]{:S(2)}, u32[]{:S(2)}) %collective-permute-start.3) | collective-permute-done | bytes 65568 | tf_op jit(solution)/shard_map/ppermute | solution.py:178
  149.0 0.0 collective-permute-done.4.refs_1_
  149.0 0.0 collective-permute-done.5.refs_2_
  149.0 0.0 copy-done.7
  149.0 2.0 %shard_map.90 = (f32[2,8,16,256]{3,2,1,0:T(8,128)}, f32[2,8,16,256]{3,2,1,0:T(8,128)}) custom-call(f32[2,64]{1,0:T(2,128)S(1)} %fusion.8.weights, s32[2,64]{1,0:T(2,128)S(1)} %copy-done.8, bf16[64,16,512]{2,1,0:T(8,128)(2,1)S(1)} %all-to-all-done.got, bf16[8,16,256]{2,1,0:T(8,128)(2,1)S(1)} %collective-permute-done.3.refs_0_, ...), custom_call_target="tpu_custom_call" | custom-call | tf_op jit(solution)/shard_map/pallas_call | solution.py:179
  (11 shorter events, 0.0 us)
Async XLA Ops:
  0.7 1.2 copy-start.3
  1.9 0.9 copy-start.5
  4.4 14.9 %collective-permute-start = (bf16[128,2048]{1,0:T(8,128)(2,1)}, bf16[128,2048]{1,0:T(8,128)(2,1)S(1)}, u32[]{:S(2)}, u32[]{:S(2)}) collective-permute-start(bf16[128,2048]{1,0:T(8,128)(2,1)} %get-tuple-element.10), channel_id=1, source_target_pairs={{0,1},{1,2},{2,3},{3,0},{4,5},{5,6},{6,7},{7,4},{8,9},{9,10},{10,1... | collective-permute-start | bytes 1572872 | tf_op jit(solution)/shard_map/ppermute | solution.py:135
  7.5 15.9 %collective-permute-start.1 = (bf16[128,2048]{1,0:T(8,128)(2,1)S(1)}, bf16[128,2048]{1,0:T(8,128)(2,1)S(1)}, u32[]{:S(2)}, u32[]{:S(2)}) collective-permute-start(bf16[128,2048]{1,0:T(8,128)(2,1)S(1)} %get-tuple-element.11), channel_id=1, source_target_pairs={{0,2},{1,3},{2,0},{3,1},{4,6},{5,7},{6,4},{7,5},{8,10},{9,11},{10,... | collective-permute-start | bytes 1572872 | tf_op jit(solution)/shard_map/ppermute | solution.py:135
  10.3 25.7 %collective-permute-start.2 = (bf16[128,2048]{1,0:T(8,128)(2,1)S(1)}, bf16[128,2048]{1,0:T(8,128)(2,1)S(1)}, u32[]{:S(2)}, u32[]{:S(2)}) collective-permute-start(bf16[128,2048]{1,0:T(8,128)(2,1)S(1)} %get-tuple-element.12), channel_id=1, source_target_pairs={{0,3},{1,0},{2,1},{3,2},{4,7},{5,4},{6,5},{7,6},{8,11},{9,8},{10,9... | collective-permute-start | bytes 1572872 | tf_op jit(solution)/shard_map/ppermute | solution.py:135
  36.0 3.4 %copy-start.1 = (bf16[128,2048]{1,0:T(8,128)(2,1)}, bf16[128,2048]{1,0:T(8,128)(2,1)S(1)}, u32[]{:S(2)}) copy-start(bf16[128,2048]{1,0:T(8,128)(2,1)S(1)} %collective-permute-done.2.refs_3_) | copy-start | bytes 1572868
  39.4 52.1 %all-to-all-start.1 = ((bf16[64,16,768]{2,1,0:T(8,128)(2,1)}), bf16[64,16,768]{2,1,0:T(8,128)(2,1)S(1)}, u32[]{:S(2)}, u32[]{:S(2)}) async-start(bf16[64,16,768]{2,1,0:T(8,128)(2,1)} %bitcast.4), calls=%async_computation.1 | async-start | bytes 3145728 | tf_op jit(solution)/shard_map/all_to_all | solution.py:154
  52.2 1.0 copy-start.2
  53.3 1.2 copy-start.4
  56.4 1.0 copy-start
  57.4 43.6 %copy-start.8 = (s32[2,64]{1,0:T(2,128)S(1)}, s32[2,64]{1,0:T(2,128)}, u32[]{:S(2)}) copy-start(s32[2,64]{1,0:T(2,128)} %modules.3) | copy-start | bytes 1540
  91.5 57.5 %copy-start.6 = (f32[2,8,16,256]{3,2,1,0:T(8,128)S(1)}, f32[2,8,16,256]{3,2,1,0:T(8,128)}, u32[]{:S(2)}) copy-start(f32[2,8,16,256]{3,2,1,0:T(8,128)} %refs_3_.1) | copy-start | bytes 786436
  91.5 57.5 %copy-start.7 = (f32[2,8,16,256]{3,2,1,0:T(8,128)S(1)}, f32[2,8,16,256]{3,2,1,0:T(8,128)}, u32[]{:S(2)}) copy-start(f32[2,8,16,256]{3,2,1,0:T(8,128)} %refs_4_.3) | copy-start | bytes 786436
  91.5 37.9 %all-to-all-start = ((bf16[64,16,512]{2,1,0:T(8,128)(2,1)}), bf16[64,16,512]{2,1,0:T(8,128)(2,1)S(1)}, u32[]{:S(2)}, u32[]{:S(2)}) async-start(bf16[64,16,512]{2,1,0:T(8,128)(2,1)} %bitcast.5), calls=%async_computation | async-start | bytes 2097152 | tf_op jit(solution)/shard_map/all_to_all | solution.py:167
  102.3 46.7 %collective-permute-start.3 = (bf16[8,16,256]{2,1,0:T(8,128)(2,1)S(1)}, bf16[8,16,256]{2,1,0:T(8,128)(2,1)S(1)}, u32[]{:S(2)}, u32[]{:S(2)}) collective-permute-start(bf16[8,16,256]{2,1,0:T(8,128)(2,1)S(1)} %get-tuple-element.13), channel_id=1, source_target_pairs={{0,4},{4,8},{8,12},{12,0},{1,5},{5,9},{9,13},{13,1},{2,6},{6,10},{... | collective-permute-start | bytes 196616 | tf_op jit(solution)/shard_map/ppermute | solution.py:178
  113.0 36.0 %collective-permute-start.4 = (bf16[8,16,256]{2,1,0:T(8,128)(2,1)S(1)}, bf16[8,16,256]{2,1,0:T(8,128)(2,1)S(1)}, u32[]{:S(2)}, u32[]{:S(2)}) collective-permute-start(bf16[8,16,256]{2,1,0:T(8,128)(2,1)S(1)} %get-tuple-element.14), channel_id=1, source_target_pairs={{0,8},{4,12},{8,0},{12,4},{1,9},{5,13},{9,1},{13,5},{2,10},{6,14},... | collective-permute-start | bytes 196616 | tf_op jit(solution)/shard_map/ppermute | solution.py:178
  124.5 24.5 %collective-permute-start.5 = (bf16[8,16,256]{2,1,0:T(8,128)(2,1)S(1)}, bf16[8,16,256]{2,1,0:T(8,128)(2,1)S(1)}, u32[]{:S(2)}, u32[]{:S(2)}) collective-permute-start(bf16[8,16,256]{2,1,0:T(8,128)(2,1)S(1)} %get-tuple-element.15), channel_id=1, source_target_pairs={{0,12},{4,0},{8,4},{12,8},{1,13},{5,1},{9,5},{13,9},{2,14},{6,2},{... | collective-permute-start | bytes 196616 | tf_op jit(solution)/shard_map/ppermute | solution.py:178

commit v4 on v3

--- a/solution.py
+++ b/solution.py
@@ -66,12 +66,15 @@
 
 def own_kernel(where, *refs):
     *pieces, drift, _, out = refs
-    block, cols = drift.shape[2:]
+    block, cols = out.shape
     at = pl.multiple_of(pl.program_id(0) * block, block)
     first = pieces[0].shape[1] - NZ * cols
     part = masked_product(where, pieces, at, block, first, first + cols)
-    out[:, :cols] = (part + drift[1, 0].astype(jnp.float32)).astype(out.dtype)
-    out[:, cols:] = drift[0, 0]
+    out[...] = (part + drift[0, 0].astype(jnp.float32)).astype(out.dtype)
+
+
+def copy_kernel(source, _, out):
+    out[...] = source[0, 0]
 
 
 def module_kernel(weights, modules, got, *refs):
@@ -89,20 +92,18 @@
         out[...] = total[:, :, k * cols : (k + 1) * cols].astype(out.dtype)
 
 
-def update_kernel(weights, modules, got, *refs):
+def update_kernel(weights, modules, got0, got1, *refs):
     *parts, outer_params, outer_moment, new_params, new_moment, total = refs
-    cols = outer_params.shape[3]
     total[0] = jnp.zeros(total.shape[1:], jnp.float32)
     total[1] = functools.reduce(lambda a, b: a + b, [part[...].astype(jnp.float32) for part in parts])
 
     def add(p, carry):
-        for level in range(2):
+        for level, got in ((0, got0), (1, got1)):
             m = modules[level, p]
-            value = got[p, :, (1 - level) * cols : (2 - level) * cols].astype(jnp.float32)
-            total[level, m] = total[level, m] + weights[level, p] * value
+            total[level, m] = total[level, m] + weights[level, p] * got[p].astype(jnp.float32)
         return carry
 
-    lax.fori_loop(0, got.shape[0], add, 0, unroll=4)
+    lax.fori_loop(0, got0.shape[0], add, 0, unroll=4)
     for level in range(2):
         average = total[level]
         moment = momentum_rate * outer_moment[level] + average
@@ -134,6 +135,21 @@
     )(place, cotangent, hidden)
     pieces = [packed[0]] + [lax.ppermute(packed[k], "x", shift("x", NX, k)) for k in range(1, NX)]
 
+    send0 = pl.pallas_call(
+        copy_kernel,
+        out_shape=jax.ShapeDtypeStruct((width, cols), bf16),
+        grid=(1,),
+        in_specs=[
+            pl.BlockSpec((1, 1, width, cols), lambda r: (0, 0, 0, 0)),
+            pl.BlockSpec(memory_space=pl.ANY),
+        ],
+        out_specs=pl.BlockSpec((width, cols), lambda r: (0, 0)),
+        compiler_params=params(),
+    )(drift, packed[1])
+    got0 = lax.all_to_all(
+        send0.reshape(paths, owner_rows, cols), PATH, split_axis=0, concat_axis=0, tiled=True
+    )
+
     member = (assignment[:, None, :] == jnp.arange(modules, dtype=jnp.int32)[None, :, None]).astype(f32)
     weighted = member * counts[None, None, :].astype(f32)
     shares = weighted / jnp.sum(weighted, axis=-1, keepdims=True)
@@ -150,22 +166,24 @@
         in_specs=[SMEM] + [whole] * NX,
         out_specs=pl.BlockSpec((block, foreign_cols), lambda r: (r, 0)),
         compiler_params=params(),
+        cost_estimate=pl.CostEstimate(flops=30 * 10**9, bytes_accessed=4 * 10**6, transcendentals=0),
     )(where, *pieces)
+    foreign, got0 = lax.optimization_barrier((foreign, got0))
     got_foreign = lax.all_to_all(
         foreign.reshape(paths, owner_rows, foreign_cols), PATH, split_axis=0, concat_axis=0, tiled=True
     )
     own = pl.pallas_call(
         own_kernel,
-        out_shape=jax.ShapeDtypeStruct((width, 2 * cols), bf16),
+        out_shape=jax.ShapeDtypeStruct((width, cols), bf16),
         grid=(width // block,),
         in_specs=[SMEM]
         + [whole] * NX
-        + [pl.BlockSpec((2, 1, block, cols), lambda r: (0, 0, r, 0)), pl.BlockSpec(memory_space=pl.ANY)],
-        out_specs=pl.BlockSpec((block, 2 * cols), lambda r: (r, 0)),
+        + [pl.BlockSpec((1, 1, block, cols), lambda r: (1, 0, r, 0)), pl.BlockSpec(memory_space=pl.ANY)],
+        out_specs=pl.BlockSpec((block, cols), lambda r: (r, 0)),
         compiler_params=params(),
     )(where, *pieces, drift, foreign)
     got_own = lax.all_to_all(
-        own.reshape(paths, owner_rows, 2 * cols), PATH, split_axis=0, concat_axis=0, tiled=True
+        own.reshape(paths, owner_rows, cols), PATH, split_axis=0, concat_axis=0, tiled=True
     )
     sums = pl.pallas_call(
         module_kernel,
@@ -179,11 +197,11 @@
     return pl.pallas_call(
         update_kernel,
         out_shape=[jax.ShapeDtypeStruct(outer_params.shape, f32)] * 2,
-        in_specs=[SMEM, SMEM] + [VMEM] * (NZ + 2),
+        in_specs=[SMEM, SMEM] + [VMEM] * (NZ + 3),
         out_specs=[VMEM] * 2,
         scratch_shapes=[pltpu.VMEM((2, modules, owner_rows, cols), f32)],
         compiler_params=params(),
-    )(weights, assignment, got_own, *parts, outer_params, outer_moment)
+    )(weights, assignment, got0, got_own, *parts, outer_params, outer_moment)
 
 
 def solution(mesh):

time: 152 us -> 142 us (0.934)
  the two profiles are of different devices: /device:TPU:75 before, /device:TPU:8 now
where the time goes in v4:
time: 142 us; the launch traced here: 141 us
  starting transfers between devices  67.9 us (48%)
  waiting for transfers between devices  52.6 us (37%)
  Pallas kernels  12.9 us (9%)
  local copies, waits for them, and re-layouts  5.16 us (4%)
  other arithmetic  1.53 us (1%)
    all_to_all x1, waiting for transfers between devices, body(): lax.all_to_all(foreign.reshape(paths, owner_rows, foreign_cols), PATH, sp...  32.9 us
    ppermute x3, starting transfers between devices, body(): lax.ppermute(sums[k - 1], 'zh', shift('zh', NZ, k))  25.5 us
    all_to_all x1, starting transfers between devices, body(): lax.all_to_all(send0.reshape(paths, owner_rows, cols), PATH, split_axis=0...  14.2 us
    ppermute x3, starting transfers between devices, body(): lax.ppermute(packed[k], 'x', shift('x', NX, k))  10.8 us
    all_to_all x1, starting transfers between devices, body(): lax.all_to_all(own.reshape(paths, owner_rows, cols), PATH, split_axis=0,...  10.4 us
    all_to_all x1, waiting for transfers between devices, body(): lax.all_to_all(send0.reshape(paths, owner_rows, cols), PATH, split_axis=0...  9.17 us
    ppermute x3, waiting for transfers between devices, body(): lax.ppermute(sums[k - 1], 'zh', shift('zh', NZ, k))  9.03 us
    all_to_all x1, starting transfers between devices, body(): lax.all_to_all(foreign.reshape(paths, owner_rows, foreign_cols), PATH, sp...  7.16 us
  transfers between devices with their start and end apart: 9, of which 5 were waited for; matrix products, arithmetic and copies ran while one was open for 1% of the time, Pallas kernels for 7%

profile of v4, /device:TPU:8, one launch (start us, length us, event | category | flops | bytes accessed | tf_op | source)
XLA Modules:
  0.0 141.0 jit_solution(3296994698685408647)
XLA Ops:
  0.6 0.1 pad_add_fusion.1.where
  0.7 1.3 copy-done.2
  2.0 0.9 copy-done.7
  3.0 1.7 %shard_map.86 = (bf16[128,2048]{1,0:T(8,128)(2,1)S(1)}, bf16[128,2048]{1,0:T(8,128)(2,1)S(1)}, bf16[128,2048]{1,0:T(8,128)(2,1)}, bf16[128,2048]{1,0:T(8,128)(2,1)}) custom-call(s32[2]{0:T(128)S(1)} %pad_add_fusion.1.where, bf16[1,128,1024]{2,1,0:T(8,128)(2,1)S(1)} %copy-done.7, bf16[1,128,4096]{2,1,0:T(8,128)(2,1)S(1)} %copy-done.2), custom_call_target="tpu_custom_call" | custom-call | tf_op jit(solution)/shard_map/pallas_call | solution.py:129
  4.7 4.9 %collective-permute-start.1 = (bf16[128,2048]{1,0:T(8,128)(2,1)}, bf16[128,2048]{1,0:T(8,128)(2,1)S(1)}, u32[]{:S(2)}, u32[]{:S(2)}) collective-permute-start(bf16[128,2048]{1,0:T(8,128)(2,1)} %get-tuple-element.13), channel_id=1, source_target_pairs={{0,2},{1,3},{2,0},{3,1},{4,6},{5,7},{6,4},{7,5},{8,10},{9,11},{10,... | collective-permute-start | bytes 1572872 | tf_op jit(solution)/shard_map/ppermute | solution.py:136
  9.6 3.0 %collective-permute-start.2 = (bf16[128,2048]{1,0:T(8,128)(2,1)}, bf16[128,2048]{1,0:T(8,128)(2,1)}, u32[]{:S(2)}, u32[]{:S(2)}) collective-permute-start(bf16[128,2048]{1,0:T(8,128)(2,1)} %get-tuple-element.14), channel_id=1, source_target_pairs={{0,3},{1,0},{2,1},{3,2},{4,7},{5,4},{6,5},{7,6},{8,11},{9,8},{10,9... | collective-permute-start | bytes 1572872 | tf_op jit(solution)/shard_map/ppermute | solution.py:136
  12.7 0.0 copy-start.11
  12.7 2.8 %collective-permute-start = (bf16[128,2048]{1,0:T(8,128)(2,1)S(1)}, bf16[128,2048]{1,0:T(8,128)(2,1)}, u32[]{:S(2)}, u32[]{:S(2)}) collective-permute-start(bf16[128,2048]{1,0:T(8,128)(2,1)S(1)} %get-tuple-element.12._), channel_id=1, source_target_pairs={{0,1},{1,2},{2,3},{3,0},{4,5},{5,6},{6,7},{7,4},{8,9},{9,10},{10,1... | collective-permute-start | bytes 1572872 | tf_op jit(solution)/shard_map/ppermute | solution.py:136
  15.5 0.8 shard_map.88
  16.3 14.2 %all-to-all-start = ((bf16[64,16,256]{2,1,0:T(8,128)(2,1)}), bf16[64,16,256]{2,1,0:T(8,128)(2,1)S(1)}, u32[]{:S(2)}, u32[]{:S(2)}) async-start(bf16[64,16,256]{2,1,0:T(8,128)(2,1)} %bitcast.3), calls=%async_computation | async-start | bytes 1048576 | tf_op jit(solution)/shard_map/all_to_all | solution.py:149
  30.5 0.6 fusion.6
  31.1 0.7 pad_add_fusion.where
  31.9 0.0 collective-permute-done.1.refs_2_
  31.9 1.5 %collective-permute-done.2.refs_3_ = bf16[128,2048]{1,0:T(8,128)(2,1)} collective-permute-done((bf16[128,2048]{1,0:T(8,128)(2,1)}, bf16[128,2048]{1,0:T(8,128)(2,1)}, u32[]{:S(2)}, u32[]{:S(2)}) %collective-permute-start.2) | collective-permute-done | bytes 524320 | tf_op jit(solution)/shard_map/ppermute | solution.py:136
  33.4 4.1 %shard_map.87.refs_5_ = bf16[1024,768]{1,0:T(8,128)(2,1)} custom-call(s32[3]{0:T(128)S(1)} %pad_add_fusion.where, bf16[128,2048]{1,0:T(8,128)(2,1)S(1)} %get-tuple-element.11.refs_0_, bf16[128,2048]{1,0:T(8,128)(2,1)} %collective-permute-done.refs_1_, bf16[128,2048]{1,0:T(8,128)(2,1)S(1)} %collective-permute-done.1.refs_2_, ...), custom_call_target="tpu_custom_call" | custom-call | flops 30000001024 | bytes 4000000 | tf_op jit(solution)/shard_map/pallas_call | solution.py:162
  37.5 9.2 %all-to-all-done.got0 = bf16[64,16,256]{2,1,0:T(8,128)(2,1)S(1)} async-done(((bf16[64,16,256]{2,1,0:T(8,128)(2,1)}), bf16[64,16,256]{2,1,0:T(8,128)(2,1)S(1)}, u32[]{:S(2)}, u32[]{:S(2)}) %all-to-all-start) | async-done | bytes 524320 | tf_op jit(solution)/shard_map/all_to_all | solution.py:149
  46.7 7.2 %all-to-all-start.2 = ((bf16[64,16,768]{2,1,0:T(8,128)(2,1)}), bf16[64,16,768]{2,1,0:T(8,128)(2,1)S(1)}, u32[]{:S(2)}, u32[]{:S(2)}) async-start(bf16[64,16,768]{2,1,0:T(8,128)(2,1)} %bitcast.5), calls=%async_computation.2 | async-start | bytes 3145728 | tf_op jit(solution)/shard_map/all_to_all | solution.py:172
  53.9 1.0 copy-done.4
  54.9 1.0 copy-done.6
  55.9 2.5 %shard_map.89 = bf16[1024,256]{1,0:T(8,128)(2,1)S(1)} custom-call(s32[3]{0:T(128)S(1)} %pad_add_fusion.where, bf16[128,2048]{1,0:T(8,128)(2,1)S(1)} %copy-done.4, bf16[128,2048]{1,0:T(8,128)(2,1)} %collective-permute-done.refs_1_, bf16[128,2048]{1,0:T(8,128)(2,1)S(1)} %copy-done.6, bf16[128,2048]{1,0:T(8,128)(2,1)} %collective-permute-done.2.refs_3_, ...), custom_call_target="tpu_custom_call" | custom-call | tf_op jit(solution)/shard_map/pallas_call | solution.py:175
  58.5 0.8 copy-done.1
  59.3 32.9 %all-to-all-done.2.got = bf16[64,16,768]{2,1,0:T(8,128)(2,1)S(1)} async-done(((bf16[64,16,768]{2,1,0:T(8,128)(2,1)}), bf16[64,16,768]{2,1,0:T(8,128)(2,1)S(1)}, u32[]{:S(2)}, u32[]{:S(2)}) %all-to-all-start.2) | async-done | bytes 1572896 | tf_op jit(solution)/shard_map/all_to_all | solution.py:172
  92.2 10.4 %all-to-all-start.1 = ((bf16[64,16,256]{2,1,0:T(8,128)(2,1)}), bf16[64,16,256]{2,1,0:T(8,128)(2,1)S(1)}, u32[]{:S(2)}, u32[]{:S(2)}) async-start(bf16[64,16,256]{2,1,0:T(8,128)(2,1)} %bitcast.6), calls=%async_computation.1 | async-start | bytes 1048576 | tf_op jit(solution)/shard_map/all_to_all | solution.py:185
  102.6 0.1 fusion.8.weights
  102.7 1.7 %shard_map.90 = (bf16[8,16,256]{2,1,0:T(8,128)(2,1)}, bf16[8,16,256]{2,1,0:T(8,128)(2,1)S(1)}, bf16[8,16,256]{2,1,0:T(8,128)(2,1)S(1)}) custom-call(f32[2,64]{1,0:T(2,128)S(1)} %fusion.8.weights, s32[2,64]{1,0:T(2,128)S(1)} %copy-done.10, bf16[64,16,768]{2,1,0:T(8,128)(2,1)S(1)} %all-to-all-done.2.got), custom_call_target="tpu_custom_call" | custom-call | tf_op jit(solution)/shard_map/pallas_call | solution.py:188
  104.4 10.2 %collective-permute-start.3 = (bf16[8,16,256]{2,1,0:T(8,128)(2,1)}, bf16[8,16,256]{2,1,0:T(8,128)(2,1)S(1)}, u32[]{:S(2)}, u32[]{:S(2)}) collective-permute-start(bf16[8,16,256]{2,1,0:T(8,128)(2,1)} %get-tuple-element.17), channel_id=1, source_target_pairs={{0,4},{4,8},{8,12},{12,0},{1,5},{5,9},{9,13},{13,1},{2,6},{6,10},{... | collective-permute-start | bytes 196616 | tf_op jit(solution)/shard_map/ppermute | solution.py:196
  114.6 11.9 %collective-permute-start.4 = (bf16[8,16,256]{2,1,0:T(8,128)(2,1)S(1)}, bf16[8,16,256]{2,1,0:T(8,128)(2,1)S(1)}, u32[]{:S(2)}, u32[]{:S(2)}) collective-permute-start(bf16[8,16,256]{2,1,0:T(8,128)(2,1)S(1)} %get-tuple-element.18), channel_id=1, source_target_pairs={{0,8},{4,12},{8,0},{12,4},{1,9},{5,13},{9,1},{13,5},{2,10},{6,14},... | collective-permute-start | bytes 196616 | tf_op jit(solution)/shard_map/ppermute | solution.py:196
  126.5 3.4 %collective-permute-start.5 = (bf16[8,16,256]{2,1,0:T(8,128)(2,1)S(1)}, bf16[8,16,256]{2,1,0:T(8,128)(2,1)S(1)}, u32[]{:S(2)}, u32[]{:S(2)}) collective-permute-start(bf16[8,16,256]{2,1,0:T(8,128)(2,1)S(1)} %get-tuple-element.19), channel_id=1, source_target_pairs={{0,12},{4,0},{8,4},{12,8},{1,13},{5,1},{9,5},{13,9},{2,14},{6,2},{... | collective-permute-start | bytes 196616 | tf_op jit(solution)/shard_map/ppermute | solution.py:196
  129.9 0.0 collective-permute-done.3.refs_0_
  129.9 1.9 %collective-permute-done.4.refs_1_ = bf16[8,16,256]{2,1,0:T(8,128)(2,1)S(1)} collective-permute-done((bf16[8,16,256]{2,1,0:T(8,128)(2,1)S(1)}, bf16[8,16,256]{2,1,0:T(8,128)(2,1)S(1)}, u32[]{:S(2)}, u32[]{:S(2)}) %collective-permute-start.4) | collective-permute-done | bytes 65568 | tf_op jit(solution)/shard_map/ppermute | solution.py:196
  131.8 7.1 %collective-permute-done.5.refs_2_ = bf16[8,16,256]{2,1,0:T(8,128)(2,1)S(1)} collective-permute-done((bf16[8,16,256]{2,1,0:T(8,128)(2,1)S(1)}, bf16[8,16,256]{2,1,0:T(8,128)(2,1)S(1)}, u32[]{:S(2)}, u32[]{:S(2)}) %collective-permute-start.5) | collective-permute-done | bytes 65568 | tf_op jit(solution)/shard_map/ppermute | solution.py:196
  139.0 2.0 %shard_map.91 = (f32[2,8,16,256]{3,2,1,0:T(8,128)}, f32[2,8,16,256]{3,2,1,0:T(8,128)}) custom-call(f32[2,64]{1,0:T(2,128)S(1)} %fusion.8.weights, s32[2,64]{1,0:T(2,128)S(1)} %copy-done.10, bf16[64,16,256]{2,1,0:T(8,128)(2,1)S(1)} %all-to-all-done.got0, bf16[64,16,256]{2,1,0:T(8,128)(2,1)S(1)} %all-to-all-done.1.got1, ...), custom_call_target="tpu_custom_call" | custom-call | tf_op jit(solution)/shard_map/pallas_call | solution.py:197
  (20 shorter events, 0.0 us)
Async XLA Ops:
  0.6 14.9 %copy-start = (bf16[2,1,1024,256]{3,2,1,0:T(8,128)(2,1)S(1)}, bf16[2,1,1024,256]{3,2,1,0:T(8,128)(2,1)}, u32[]{:S(2)}) copy-start(bf16[2,1,1024,256]{3,2,1,0:T(8,128)(2,1)} %refs_4_.2) | copy-start | bytes 3145732
  0.7 1.3 copy-start.2
  2.0 0.9 copy-start.7
  4.7 28.7 %copy-start.3 = (bf16[128,2048]{1,0:T(8,128)(2,1)}, bf16[128,2048]{1,0:T(8,128)(2,1)S(1)}, u32[]{:S(2)}) copy-start(bf16[128,2048]{1,0:T(8,128)(2,1)S(1)} %get-tuple-element.11.refs_0_) | copy-start | bytes 1572868
  4.7 27.2 %collective-permute-start.1 = (bf16[128,2048]{1,0:T(8,128)(2,1)}, bf16[128,2048]{1,0:T(8,128)(2,1)S(1)}, u32[]{:S(2)}, u32[]{:S(2)}) collective-permute-start(bf16[128,2048]{1,0:T(8,128)(2,1)} %get-tuple-element.13), channel_id=1, source_target_pairs={{0,2},{1,3},{2,0},{3,1},{4,6},{5,7},{6,4},{7,5},{8,10},{9,11},{10,... | collective-permute-start | bytes 1572872 | tf_op jit(solution)/shard_map/ppermute | solution.py:136
  9.6 23.8 %collective-permute-start.2 = (bf16[128,2048]{1,0:T(8,128)(2,1)}, bf16[128,2048]{1,0:T(8,128)(2,1)}, u32[]{:S(2)}, u32[]{:S(2)}) collective-permute-start(bf16[128,2048]{1,0:T(8,128)(2,1)} %get-tuple-element.14), channel_id=1, source_target_pairs={{0,3},{1,0},{2,1},{3,2},{4,7},{5,4},{6,5},{7,6},{8,11},{9,8},{10,9... | collective-permute-start | bytes 1572872 | tf_op jit(solution)/shard_map/ppermute | solution.py:136
  12.7 17.8 %copy-start.11 = (s32[64]{0:T(128)S(1)}, s32[64]{0:T(128)}, u32[]{:S(2)}) copy-start(s32[64]{0:T(128)} %param.10) | copy-start | bytes 772
  12.7 20.7 %collective-permute-start = (bf16[128,2048]{1,0:T(8,128)(2,1)S(1)}, bf16[128,2048]{1,0:T(8,128)(2,1)}, u32[]{:S(2)}, u32[]{:S(2)}) collective-permute-start(bf16[128,2048]{1,0:T(8,128)(2,1)S(1)} %get-tuple-element.12._), channel_id=1, source_target_pairs={{0,1},{1,2},{2,3},{3,0},{4,5},{5,6},{6,7},{7,4},{8,9},{9,10},{10,1... | collective-permute-start | bytes 1572872 | tf_op jit(solution)/shard_map/ppermute | solution.py:136
  16.3 30.4 %all-to-all-start = ((bf16[64,16,256]{2,1,0:T(8,128)(2,1)}), bf16[64,16,256]{2,1,0:T(8,128)(2,1)S(1)}, u32[]{:S(2)}, u32[]{:S(2)}) async-start(bf16[64,16,256]{2,1,0:T(8,128)(2,1)} %bitcast.3), calls=%async_computation | async-start | bytes 1048576 | tf_op jit(solution)/shard_map/all_to_all | solution.py:149
  31.9 5.6 %copy-start.5 = (bf16[128,2048]{1,0:T(8,128)(2,1)}, bf16[128,2048]{1,0:T(8,128)(2,1)S(1)}, u32[]{:S(2)}) copy-start(bf16[128,2048]{1,0:T(8,128)(2,1)S(1)} %collective-permute-done.1.refs_2_) | copy-start | bytes 1572868
  46.7 45.5 %all-to-all-start.2 = ((bf16[64,16,768]{2,1,0:T(8,128)(2,1)}), bf16[64,16,768]{2,1,0:T(8,128)(2,1)S(1)}, u32[]{:S(2)}, u32[]{:S(2)}) async-start(bf16[64,16,768]{2,1,0:T(8,128)(2,1)} %bitcast.5), calls=%async_computation.2 | async-start | bytes 3145728 | tf_op jit(solution)/shard_map/all_to_all | solution.py:172
  53.8 1.0 copy-start.4
  54.9 1.0 copy-start.6
  55.9 46.6 %copy-start.10 = (s32[2,64]{1,0:T(2,128)S(1)}, s32[2,64]{1,0:T(2,128)}, u32[]{:S(2)}) copy-start(s32[2,64]{1,0:T(2,128)} %modules.3) | copy-start | bytes 1540
  58.5 0.8 copy-start.1
  59.3 79.7 %copy-start.8 = (f32[2,8,16,256]{3,2,1,0:T(8,128)S(1)}, f32[2,8,16,256]{3,2,1,0:T(8,128)}, u32[]{:S(2)}) copy-start(f32[2,8,16,256]{3,2,1,0:T(8,128)} %refs_3_.1) | copy-start | bytes 786436
  59.3 79.7 %copy-start.9 = (f32[2,8,16,256]{3,2,1,0:T(8,128)S(1)}, f32[2,8,16,256]{3,2,1,0:T(8,128)}, u32[]{:S(2)}) copy-start(f32[2,8,16,256]{3,2,1,0:T(8,128)} %refs_4_.3) | copy-start | bytes 786436
  92.2 37.7 %all-to-all-start.1 = ((bf16[64,16,256]{2,1,0:T(8,128)(2,1)}), bf16[64,16,256]{2,1,0:T(8,128)(2,1)S(1)}, u32[]{:S(2)}, u32[]{:S(2)}) async-start(bf16[64,16,256]{2,1,0:T(8,128)(2,1)} %bitcast.6), calls=%async_computation.1 | async-start | bytes 1048576 | tf_op jit(solution)/shard_map/all_to_all | solution.py:185
  104.4 25.5 %collective-permute-start.3 = (bf16[8,16,256]{2,1,0:T(8,128)(2,1)}, bf16[8,16,256]{2,1,0:T(8,128)(2,1)S(1)}, u32[]{:S(2)}, u32[]{:S(2)}) collective-permute-start(bf16[8,16,256]{2,1,0:T(8,128)(2,1)} %get-tuple-element.17), channel_id=1, source_target_pairs={{0,4},{4,8},{8,12},{12,0},{1,5},{5,9},{9,13},{13,1},{2,6},{6,10},{... | collective-permute-start | bytes 196616 | tf_op jit(solution)/shard_map/ppermute | solution.py:196
  114.6 17.3 %collective-permute-start.4 = (bf16[8,16,256]{2,1,0:T(8,128)(2,1)S(1)}, bf16[8,16,256]{2,1,0:T(8,128)(2,1)S(1)}, u32[]{:S(2)}, u32[]{:S(2)}) collective-permute-start(bf16[8,16,256]{2,1,0:T(8,128)(2,1)S(1)} %get-tuple-element.18), channel_id=1, source_target_pairs={{0,8},{4,12},{8,0},{12,4},{1,9},{5,13},{9,1},{13,5},{2,10},{6,14},... | collective-permute-start | bytes 196616 | tf_op jit(solution)/shard_map/ppermute | solution.py:196
  126.5 12.5 %collective-permute-start.5 = (bf16[8,16,256]{2,1,0:T(8,128)(2,1)S(1)}, bf16[8,16,256]{2,1,0:T(8,128)(2,1)S(1)}, u32[]{:S(2)}, u32[]{:S(2)}) collective-permute-start(bf16[8,16,256]{2,1,0:T(8,128)(2,1)S(1)} %get-tuple-element.19), channel_id=1, source_target_pairs={{0,12},{4,0},{8,4},{12,8},{1,13},{5,1},{9,5},{13,9},{2,14},{6,2},{... | collective-permute-start | bytes 196616 | tf_op jit(solution)/shard_map/ppermute | solution.py:196

commit v5 on v3

v5 whole, which is shorter than its diff:
```python
import functools

import jax
import jax.numpy as jnp
from jax import lax
from jax.experimental import pallas as pl
from jax.experimental.pallas import tpu as pltpu
from jax.sharding import Mesh, PartitionSpec as P

inner_step = 0.02
momentum_rate = 0.9
outer_rate = 0.7

PATH = ("zl", "y", "core")
FSDP = ("zh", "x")
NX = 4
NZ = 4
LIMIT = 24 * 2**20
LARGE = 56 * 2**20
SMEM = pl.BlockSpec(memory_space=pltpu.SMEM)
VMEM = pl.BlockSpec(memory_space=pltpu.VMEM)
HBM = pl.BlockSpec(memory_space=pltpu.HBM)


def shift(axis, size, by):
    return [(i, (i + by) % size) for i in range(size)]


def params(limit=LIMIT):
    return pltpu.CompilerParams(vmem_limit_bytes=limit)


def pieces_to(where, shift_x, cot, hid, out):
    width = cot.shape[2]
    cols = hid.shape[2] // (NX * NZ)
    to = (where[1] + shift_x) % NX
    pairs = [(cot.at[0], out.at[:, pl.ds(0, width)])]
    for j in range(NZ):
        z = (where[0] + j) % NZ
        start = pl.multiple_of((z * NX + to) * cols, cols)
        pairs.append((hid.at[0, :, pl.ds(start, cols)], out.at[:, pl.ds(width + j * cols, cols)]))
    return pairs


def copy_all(pairs, sems):
    copies = [pltpu.make_async_copy(a, b, sems.at[i]) for i, (a, b) in enumerate(pairs)]
    for copy in copies:
        copy.start()
    for copy in copies:
        copy.wait()


def pack_kernel(where, cot, hid, *refs):
    *outs, sems = refs
    copy_all([pair for k, out in enumerate(outs) for pair in pieces_to(where, k + 1, cot, hid, out)], sems)


def local_kernel(where, cot, hid, drift, _, own, send0, sems):
    copy_all(pieces_to(where, 0, cot, hid, own) + [(drift.at[0, 0], send0)], sems)


def masked_product(where, pieces, at, block, first, last):
    rows = pieces[0].shape[0]
    left = []
    for k, piece in enumerate(pieces):
        source = (where[1] - k + NX) % NX
        token = (where[0] * NX + source) * rows + lax.broadcasted_iota(jnp.int32, (rows, block), 0)
        value = piece[:, pl.ds(at, block)].astype(jnp.float32)
        left.append(jnp.where(token < where[2], value, 0.0).astype(jnp.bfloat16))
    return inner_step * lax.dot_general(
        jnp.concatenate(left, axis=0),
        jnp.concatenate([piece[:, first:last] for piece in pieces], axis=0),
        (((0,), (0,)), ((), ())),
        preferred_element_type=jnp.float32,
    )


def grad_kernel(where, *refs):
    *pieces, drift, foreign, own = refs
    block, cols = own.shape
    at = pl.multiple_of(pl.program_id(0) * block, block)
    last = pieces[0].shape[1]
    part = masked_product(where, pieces, at, block, last - NZ * cols, last)
    own[...] = (part[:, :cols] + drift[0, 0].astype(jnp.float32)).astype(own.dtype)
    foreign[...] = part[:, cols:].astype(foreign.dtype)


def add_paths(weights, modules, level, got, total):
    def add(p, carry):
        m = modules[level, p]
        total[m] = total[m] + weights[level, p] * got[p].astype(jnp.float32)
        return carry

    lax.fori_loop(0, got.shape[0], add, 0, unroll=4)


def module_kernel(weights, modules, got, *refs):
    *outs, total = refs
    cols = outs[0].shape[2]
    total[...] = jnp.zeros_like(total)
    add_paths(weights, modules, 1, got, total)
    for k, out in enumerate(outs):
        out[...] = total[:, :, k * cols : (k + 1) * cols].astype(out.dtype)


def level0_kernel(weights, modules, got, out):
    out[...] = jnp.zeros_like(out)
    add_paths(weights, modules, 0, got, out)


def update_kernel(weights, modules, average0, got, *refs):
    *parts, outer_params, outer_moment, new_params, new_moment, total = refs
    total[...] = functools.reduce(lambda a, b: a + b, [part[...].astype(jnp.float32) for part in parts])
    add_paths(weights, modules, 1, got, total)
    for level, average in ((0, average0[...]), (1, total[...])):
        moment = momentum_rate * outer_moment[level] + average
        new_moment[level] = moment
        new_params[level] = outer_params[level] - outer_rate * (average + momentum_rate * moment)


def body(cotangent, hidden, drift, counts, assignment, outer_params, outer_moment):
    path_index = lax.axis_index(PATH)
    zh = lax.axis_index("zh")
    x = lax.axis_index("x")
    paths = counts.shape[0]
    modules = outer_params.shape[1]
    owner_rows = outer_params.shape[2]
    cols = outer_params.shape[3]
    rows = cotangent.shape[1]
    width = cotangent.shape[2]
    packed_shape = (rows, width + NZ * cols)
    foreign_cols = (NZ - 1) * cols
    bf16, f32 = jnp.bfloat16, jnp.float32

    place = jnp.stack([zh, x]).astype(jnp.int32)
    packed = pl.pallas_call(
        pack_kernel,
        out_shape=[jax.ShapeDtypeStruct(packed_shape, bf16)] * (NX - 1),
        in_specs=[SMEM, HBM, HBM],
        out_specs=[HBM] * (NX - 1),
        scratch_shapes=[pltpu.SemaphoreType.DMA(((NX - 1) * (1 + NZ),))],
        compiler_params=params(LARGE),
    )(place, cotangent, hidden)
    pieces = [lax.ppermute(packed[k - 1], "x", shift("x", NX, k)) for k in range(1, NX)]
    piece0, send0 = pl.pallas_call(
        local_kernel,
        out_shape=[jax.ShapeDtypeStruct(packed_shape, bf16), jax.ShapeDtypeStruct((width, cols), bf16)],
        in_specs=[SMEM, HBM, HBM, HBM, HBM],
        out_specs=[HBM, HBM],
        scratch_shapes=[pltpu.SemaphoreType.DMA((2 + NZ,))],
        compiler_params=params(LARGE),
    )(place, cotangent, hidden, drift, packed[0])
    pieces = [piece0] + pieces
    got0 = lax.all_to_all(
        send0.reshape(paths, owner_rows, cols), PATH, split_axis=0, concat_axis=0, tiled=True
    )

    member = (assignment[:, None, :] == jnp.arange(modules, dtype=jnp.int32)[None, :, None]).astype(f32)
    weighted = member * counts[None, None, :].astype(f32)
    shares = weighted / jnp.sum(weighted, axis=-1, keepdims=True)
    weights = jnp.sum(shares, axis=1)
    my_count = jnp.sum(jnp.where(jnp.arange(paths, dtype=jnp.int32) == path_index, counts, 0))
    where = jnp.stack([zh, x, my_count]).astype(jnp.int32)

    block = 256
    foreign, own = pl.pallas_call(
        grad_kernel,
        out_shape=[
            jax.ShapeDtypeStruct((width, foreign_cols), bf16),
            jax.ShapeDtypeStruct((width, cols), bf16),
        ],
        grid=(width // block,),
        in_specs=[SMEM] + [VMEM] * NX + [pl.BlockSpec((1, 1, block, cols), lambda r: (1, 0, r, 0))],
        out_specs=[
            pl.BlockSpec((block, foreign_cols), lambda r: (r, 0)),
            pl.BlockSpec((block, cols), lambda r: (r, 0)),
        ],
        compiler_params=params(),
        cost_estimate=pl.CostEstimate(flops=30 * 10**9, bytes_accessed=4 * 10**6, transcendentals=0),
    )(where, *pieces, drift)
    foreign, got0 = lax.optimization_barrier((foreign, got0))
    got_foreign = lax.all_to_all(
        foreign.reshape(paths, owner_rows, foreign_cols), PATH, split_axis=0, concat_axis=0, tiled=True
    )
    got_own = lax.all_to_all(
        own.reshape(paths, owner_rows, cols), PATH, split_axis=0, concat_axis=0, tiled=True
    )
    sums = pl.pallas_call(
        module_kernel,
        out_shape=[jax.ShapeDtypeStruct((modules, owner_rows, cols), bf16)] * (NZ - 1),
        in_specs=[SMEM, SMEM, VMEM],
        out_specs=[VMEM] * (NZ - 1),
        scratch_shapes=[pltpu.VMEM((modules, owner_rows, foreign_cols), f32)],
        compiler_params=params(),
    )(weights, assignment, got_foreign)
    parts = [lax.ppermute(sums[k - 1], "zh", shift("zh", NZ, k)) for k in range(1, NZ)]
    average0 = pl.pallas_call(
        level0_kernel,
        out_shape=jax.ShapeDtypeStruct((modules, owner_rows, cols), f32),
        in_specs=[SMEM, SMEM, VMEM],
        out_specs=VMEM,
        compiler_params=params(),
    )(weights, assignment, got0)
    return pl.pallas_call(
        update_kernel,
        out_shape=[jax.ShapeDtypeStruct(outer_params.shape, f32)] * 2,
        in_specs=[SMEM, SMEM] + [VMEM] * (NZ + 3),
        out_specs=[VMEM] * 2,
        scratch_shapes=[pltpu.VMEM((modules, owner_rows, cols), f32)],
        compiler_params=params(),
    )(weights, assignment, average0, got_own, *parts, outer_params, outer_moment)


def solution(mesh):
    fine = Mesh(mesh.devices.reshape(4, 8, 2, 4, 4), ("zl", "y", "core", "zh", "x"))
    placed = (
        P(PATH, FSDP, None),
        P(PATH, FSDP, None),
        P(None, PATH, None, FSDP),
        P(),
        P(),
        P(None, None, PATH, FSDP),
        P(None, None, PATH, FSDP),
    )
    return jax.shard_map(
        lambda *a: tuple(body(*a)),
        mesh=fine,
        in_specs=placed,
        out_specs=(P(None, None, PATH, FSDP), P(None, None, PATH, FSDP)),
        check_vma=False,
    )
```

time: 152 us -> 221 us (1.45)
  the two profiles are of different devices: /device:TPU:75 before, /device:TPU:8 now
where the time goes in v5:
time: 221 us; the launch traced here: 220 us
  Pallas kernels  90.1 us (41%)
  starting transfers between devices  61.7 us (28%)
  blocking collectives  45.6 us (21%)
  waiting for transfers between devices  17.6 us (8%)
  local copies, waits for them, and re-layouts  2.22 us (1%)
    pallas_call x1, Pallas kernels, body(): pl.pallas_call(pack_kernel, out_shape=[jax.ShapeDtypeStruct(packed_shape,...  49.5 us
    all_to_all x1, blocking collectives, body(): lax.all_to_all(foreign.reshape(paths, owner_rows, foreign_cols), PATH, sp...  45.6 us
    pallas_call x1, Pallas kernels, body(): pl.pallas_call(local_kernel, out_shape=[jax.ShapeDtypeStruct(packed_shape...  33.6 us
    ppermute x3, starting transfers between devices, body(): lax.ppermute(sums[k - 1], 'zh', shift('zh', NZ, k))  24.9 us
    all_to_all x1, starting transfers between devices, body(): lax.all_to_all(send0.reshape(paths, owner_rows, cols), PATH, split_axis=0...  14.8 us
    ppermute x3, starting transfers between devices, body(): lax.ppermute(packed[k - 1], 'x', shift('x', NX, k))  11.5 us
    all_to_all x1, starting transfers between devices, body(): lax.all_to_all(own.reshape(paths, owner_rows, cols), PATH, split_axis=0,...  10.5 us
    all_to_all x1, waiting for transfers between devices, body(): lax.all_to_all(send0.reshape(paths, owner_rows, cols), PATH, split_axis=0...  9.47 us
  transfers between devices with their start and end apart: 8, of which 3 were waited for; matrix products, arithmetic and copies ran while one was open for 1% of the time, Pallas kernels for 18%

profile of v5, /device:TPU:8, one launch (start us, length us, event | category | flops | bytes accessed | tf_op | source)
XLA Modules:
  0.0 220.0 jit_solution(5660857421266688013)
XLA Ops:
  0.6 0.6 pad_add_fusion.1.where
  1.2 49.5 %shard_map.86 = (bf16[128,2048]{1,0:T(8,128)(2,1)}, bf16[128,2048]{1,0:T(8,128)(2,1)}, bf16[128,2048]{1,0:T(8,128)(2,1)}) custom-call(s32[2]{0:T(128)} %pad_add_fusion.1.where, bf16[1,128,1024]{2,1,0:T(8,128)(2,1)} %cot.3, bf16[1,128,4096]{2,1,0:T(8,128)(2,1)} %hid.3), custom_call_target="tpu_custom_call" | custom-call | tf_op jit(solution)/shard_map/pallas_call | solution.py:136
  50.8 3.4 %collective-permute-start = (bf16[128,2048]{1,0:T(8,128)(2,1)}, bf16[128,2048]{1,0:T(8,128)(2,1)S(1)}, u32[]{:S(2)}, u32[]{:S(2)}) collective-permute-start(bf16[128,2048]{1,0:T(8,128)(2,1)} %get-tuple-element.14._), channel_id=1, source_target_pairs={{0,1},{1,2},{2,3},{3,0},{4,5},{5,6},{6,7},{7,4},{8,9},{9,10},{10,1... | collective-permute-start | bytes 1572872 | tf_op jit(solution)/shard_map/ppermute | solution.py:144
  54.2 4.6 %collective-permute-start.1 = (bf16[128,2048]{1,0:T(8,128)(2,1)}, bf16[128,2048]{1,0:T(8,128)(2,1)S(1)}, u32[]{:S(2)}, u32[]{:S(2)}) collective-permute-start(bf16[128,2048]{1,0:T(8,128)(2,1)} %get-tuple-element.16), channel_id=1, source_target_pairs={{0,2},{1,3},{2,0},{3,1},{4,6},{5,7},{6,4},{7,5},{8,10},{9,11},{10,... | collective-permute-start | bytes 1572872 | tf_op jit(solution)/shard_map/ppermute | solution.py:144
  58.8 0.0 copy-start.6
  58.8 0.0 copy-start.1
  58.8 3.5 %collective-permute-start.2 = (bf16[128,2048]{1,0:T(8,128)(2,1)}, bf16[128,2048]{1,0:T(8,128)(2,1)S(1)}, u32[]{:S(2)}, u32[]{:S(2)}) collective-permute-start(bf16[128,2048]{1,0:T(8,128)(2,1)} %get-tuple-element.17), channel_id=1, source_target_pairs={{0,3},{1,0},{2,1},{3,2},{4,7},{5,4},{6,5},{7,6},{8,11},{9,8},{10,9... | collective-permute-start | bytes 1572872 | tf_op jit(solution)/shard_map/ppermute | solution.py:144
  62.3 33.6 %shard_map.87 = (bf16[128,2048]{1,0:T(8,128)(2,1)}, bf16[1024,256]{1,0:T(8,128)(2,1)}) custom-call(s32[2]{0:T(128)} %pad_add_fusion.1.where, bf16[1,128,1024]{2,1,0:T(8,128)(2,1)} %cot.3, bf16[1,128,4096]{2,1,0:T(8,128)(2,1)} %hid.3, bf16[2,1,1024,256]{3,2,1,0:T(8,128)(2,1)} %refs_4_.2, bf16[128,2048]{1,0:T(8,128)(2,1)} %get-tuple-element.14._), custom_call_target="tpu_custom_call" | custom-call | tf_op jit(solution)/shard_map/pallas_call | solution.py:145
  95.9 14.8 %all-to-all-start = ((bf16[64,16,256]{2,1,0:T(8,128)(2,1)}), bf16[64,16,256]{2,1,0:T(8,128)(2,1)S(1)}, u32[]{:S(2)}, u32[]{:S(2)}) async-start(bf16[64,16,256]{2,1,0:T(8,128)(2,1)} %bitcast.7), calls=%async_computation | async-start | bytes 1048576 | tf_op jit(solution)/shard_map/all_to_all | solution.py:154
  110.7 0.0 copy-done.6
  110.7 0.6 fusion.6
  111.4 0.7 pad_add_fusion.where
  112.1 0.0 collective-permute-done.refs_1_
  112.1 0.0 collective-permute-done.1.refs_2_
  112.1 0.0 collective-permute-done.2.refs_3_
  112.1 1.0 copy-done.5
  113.1 3.1 %shard_map.88 = (bf16[1024,768]{1,0:T(8,128)(2,1)S(1)}, bf16[1024,256]{1,0:T(8,128)(2,1)}) custom-call(s32[3]{0:T(128)S(1)} %pad_add_fusion.where, bf16[128,2048]{1,0:T(8,128)(2,1)S(1)} %copy-done.5, bf16[128,2048]{1,0:T(8,128)(2,1)S(1)} %collective-permute-done.refs_1_, bf16[128,2048]{1,0:T(8,128)(2,1)S(1)} %collective-permute-done.1.refs_2_, ...), custom_call_target="tpu_custom_call" | custom-call | flops 30000001024 | bytes 4000000 | tf_op jit(solution)/shard_map/pallas_call | solution.py:166
  116.3 1.2 copy-done
  117.4 9.5 %all-to-all-done.got = bf16[64,16,256]{2,1,0:T(8,128)(2,1)S(1)} async-done(((bf16[64,16,256]{2,1,0:T(8,128)(2,1)}), bf16[64,16,256]{2,1,0:T(8,128)(2,1)S(1)}, u32[]{:S(2)}, u32[]{:S(2)}) %all-to-all-start) | async-done | bytes 524320 | tf_op jit(solution)/shard_map/all_to_all | solution.py:154
  126.9 45.6 %all_to_all.15.got = bf16[64,16,768]{2,1,0:T(8,128)(2,1)S(1)} all-to-all(bf16[64,16,768]{2,1,0:T(8,128)(2,1)} %bitcast.6), channel_id=1, replica_groups=mesh['zl'=4,'y'=8,'core'=2,'zh'=4,'x'=4] {'zl','y','core'}, dimensions={0} | all-to-all | bytes 3145728 | tf_op jit(solution)/shard_map/all_to_all | solution.py:182
  172.5 10.5 %all-to-all-start.1 = ((bf16[64,16,256]{2,1,0:T(8,128)(2,1)}), bf16[64,16,256]{2,1,0:T(8,128)(2,1)S(1)}, u32[]{:S(2)}, u32[]{:S(2)}) async-start(bf16[64,16,256]{2,1,0:T(8,128)(2,1)} %bitcast.4), calls=%async_computation.1 | async-start | bytes 1048576 | tf_op jit(solution)/shard_map/all_to_all | solution.py:185
  183.1 0.1 fusion.8.weights
  183.2 1.1 shard_map.90
  184.3 9.6 %collective-permute-start.3 = (bf16[8,16,256]{2,1,0:T(8,128)(2,1)S(1)}, bf16[8,16,256]{2,1,0:T(8,128)(2,1)S(1)}, u32[]{:S(2)}, u32[]{:S(2)}) collective-permute-start(bf16[8,16,256]{2,1,0:T(8,128)(2,1)S(1)} %get-tuple-element.23), channel_id=1, source_target_pairs={{0,4},{4,8},{8,12},{12,0},{1,5},{5,9},{9,13},{13,1},{2,6},{6,10},{... | collective-permute-start | bytes 196616 | tf_op jit(solution)/shard_map/ppermute | solution.py:196
  193.9 11.9 %collective-permute-start.4 = (bf16[8,16,256]{2,1,0:T(8,128)(2,1)S(1)}, bf16[8,16,256]{2,1,0:T(8,128)(2,1)S(1)}, u32[]{:S(2)}, u32[]{:S(2)}) collective-permute-start(bf16[8,16,256]{2,1,0:T(8,128)(2,1)S(1)} %get-tuple-element.24), channel_id=1, source_target_pairs={{0,8},{4,12},{8,0},{12,4},{1,9},{5,13},{9,1},{13,5},{2,10},{6,14},... | collective-permute-start | bytes 196616 | tf_op jit(solution)/shard_map/ppermute | solution.py:196
  205.7 3.5 %collective-permute-start.5 = (bf16[8,16,256]{2,1,0:T(8,128)(2,1)S(1)}, bf16[8,16,256]{2,1,0:T(8,128)(2,1)S(1)}, u32[]{:S(2)}, u32[]{:S(2)}) collective-permute-start(bf16[8,16,256]{2,1,0:T(8,128)(2,1)S(1)} %get-tuple-element.25), channel_id=1, source_target_pairs={{0,12},{4,0},{8,4},{12,8},{1,13},{5,1},{9,5},{13,9},{2,14},{6,2},{... | collective-permute-start | bytes 196616 | tf_op jit(solution)/shard_map/ppermute | solution.py:196
  209.2 0.9 shard_map.89.average0
  210.0 0.0 all-to-all-done.1.got
  210.0 1.3 collective-permute-done.3.refs_0_
  211.3 0.0 collective-permute-done.4.refs_1_
  211.3 6.9 %collective-permute-done.5.refs_2_ = bf16[8,16,256]{2,1,0:T(8,128)(2,1)S(1)} collective-permute-done((bf16[8,16,256]{2,1,0:T(8,128)(2,1)S(1)}, bf16[8,16,256]{2,1,0:T(8,128)(2,1)S(1)}, u32[]{:S(2)}, u32[]{:S(2)}) %collective-permute-start.5) | collective-permute-done | bytes 65568 | tf_op jit(solution)/shard_map/ppermute | solution.py:196
  218.2 1.9 shard_map.91
  (9 shorter events, 0.0 us)
Async XLA Ops:
  50.8 61.3 %collective-permute-start = (bf16[128,2048]{1,0:T(8,128)(2,1)}, bf16[128,2048]{1,0:T(8,128)(2,1)S(1)}, u32[]{:S(2)}, u32[]{:S(2)}) collective-permute-start(bf16[128,2048]{1,0:T(8,128)(2,1)} %get-tuple-element.14._), channel_id=1, source_target_pairs={{0,1},{1,2},{2,3},{3,0},{4,5},{5,6},{6,7},{7,4},{8,9},{9,10},{10,1... | collective-permute-start | bytes 1572872 | tf_op jit(solution)/shard_map/ppermute | solution.py:144
  54.2 57.9 %collective-permute-start.1 = (bf16[128,2048]{1,0:T(8,128)(2,1)}, bf16[128,2048]{1,0:T(8,128)(2,1)S(1)}, u32[]{:S(2)}, u32[]{:S(2)}) collective-permute-start(bf16[128,2048]{1,0:T(8,128)(2,1)} %get-tuple-element.16), channel_id=1, source_target_pairs={{0,2},{1,3},{2,0},{3,1},{4,6},{5,7},{6,4},{7,5},{8,10},{9,11},{10,... | collective-permute-start | bytes 1572872 | tf_op jit(solution)/shard_map/ppermute | solution.py:144
  58.8 51.9 %copy-start.6 = (s32[64]{0:T(128)S(1)}, s32[64]{0:T(128)}, u32[]{:S(2)}) copy-start(s32[64]{0:T(128)} %param.10) | copy-start | bytes 772
  58.8 53.3 %copy-start.1 = (bf16[2,1,1024,256]{3,2,1,0:T(8,128)(2,1)S(1)}, bf16[2,1,1024,256]{3,2,1,0:T(8,128)(2,1)}, u32[]{:S(2)}) copy-start(bf16[2,1,1024,256]{3,2,1,0:T(8,128)(2,1)} %refs_4_.2) | copy-start | bytes 3145732
  58.8 53.2 %collective-permute-start.2 = (bf16[128,2048]{1,0:T(8,128)(2,1)}, bf16[128,2048]{1,0:T(8,128)(2,1)S(1)}, u32[]{:S(2)}, u32[]{:S(2)}) collective-permute-start(bf16[128,2048]{1,0:T(8,128)(2,1)} %get-tuple-element.17), channel_id=1, source_target_pairs={{0,3},{1,0},{2,1},{3,2},{4,7},{5,4},{6,5},{7,6},{8,11},{9,8},{10,9... | collective-permute-start | bytes 1572872 | tf_op jit(solution)/shard_map/ppermute | solution.py:144
  95.9 31.0 %all-to-all-start = ((bf16[64,16,256]{2,1,0:T(8,128)(2,1)}), bf16[64,16,256]{2,1,0:T(8,128)(2,1)S(1)}, u32[]{:S(2)}, u32[]{:S(2)}) async-start(bf16[64,16,256]{2,1,0:T(8,128)(2,1)} %bitcast.7), calls=%async_computation | async-start | bytes 1048576 | tf_op jit(solution)/shard_map/all_to_all | solution.py:154
  112.1 1.0 copy-start.5
  116.3 1.2 copy-start
  126.9 56.1 %copy-start.4 = (s32[2,64]{1,0:T(2,128)S(1)}, s32[2,64]{1,0:T(2,128)}, u32[]{:S(2)}) copy-start(s32[2,64]{1,0:T(2,128)} %modules.5) | copy-start | bytes 1540
  172.5 45.6 %copy-start.2 = (f32[2,8,16,256]{3,2,1,0:T(8,128)S(1)}, f32[2,8,16,256]{3,2,1,0:T(8,128)}, u32[]{:S(2)}) copy-start(f32[2,8,16,256]{3,2,1,0:T(8,128)} %refs_3_.1) | copy-start | bytes 786436
  172.5 45.6 %copy-start.3 = (f32[2,8,16,256]{3,2,1,0:T(8,128)S(1)}, f32[2,8,16,256]{3,2,1,0:T(8,128)}, u32[]{:S(2)}) copy-start(f32[2,8,16,256]{3,2,1,0:T(8,128)} %refs_4_.3) | copy-start | bytes 786436
  172.5 37.5 %all-to-all-start.1 = ((bf16[64,16,256]{2,1,0:T(8,128)(2,1)}), bf16[64,16,256]{2,1,0:T(8,128)(2,1)S(1)}, u32[]{:S(2)}, u32[]{:S(2)}) async-start(bf16[64,16,256]{2,1,0:T(8,128)(2,1)} %bitcast.4), calls=%async_computation.1 | async-start | bytes 1048576 | tf_op jit(solution)/shard_map/all_to_all | solution.py:185
  184.3 27.0 %collective-permute-start.3 = (bf16[8,16,256]{2,1,0:T(8,128)(2,1)S(1)}, bf16[8,16,256]{2,1,0:T(8,128)(2,1)S(1)}, u32[]{:S(2)}, u32[]{:S(2)}) collective-permute-start(bf16[8,16,256]{2,1,0:T(8,128)(2,1)S(1)} %get-tuple-element.23), channel_id=1, source_target_pairs={{0,4},{4,8},{8,12},{12,0},{1,5},{5,9},{9,13},{13,1},{2,6},{6,10},{... | collective-permute-start | bytes 196616 | tf_op jit(solution)/shard_map/ppermute | solution.py:196
  193.9 17.5 %collective-permute-start.4 = (bf16[8,16,256]{2,1,0:T(8,128)(2,1)S(1)}, bf16[8,16,256]{2,1,0:T(8,128)(2,1)S(1)}, u32[]{:S(2)}, u32[]{:S(2)}) collective-permute-start(bf16[8,16,256]{2,1,0:T(8,128)(2,1)S(1)} %get-tuple-element.24), channel_id=1, source_target_pairs={{0,8},{4,12},{8,0},{12,4},{1,9},{5,13},{9,1},{13,5},{2,10},{6,14},... | collective-permute-start | bytes 196616 | tf_op jit(solution)/shard_map/ppermute | solution.py:196
  205.7 12.5 %collective-permute-start.5 = (bf16[8,16,256]{2,1,0:T(8,128)(2,1)S(1)}, bf16[8,16,256]{2,1,0:T(8,128)(2,1)S(1)}, u32[]{:S(2)}, u32[]{:S(2)}) collective-permute-start(bf16[8,16,256]{2,1,0:T(8,128)(2,1)S(1)} %get-tuple-element.25), channel_id=1, source_target_pairs={{0,12},{4,0},{8,4},{12,8},{1,13},{5,1},{9,5},{13,9},{2,14},{6,2},{... | collective-permute-start | bytes 196616 | tf_op jit(solution)/shard_map/ppermute | solution.py:196

commit v6 on v5

--- a/solution.py
+++ b/solution.py
@@ -11,6 +11,7 @@
 momentum_rate = 0.9
 outer_rate = 0.7
 
+CHIPS = ("zl", "y")
 PATH = ("zl", "y", "core")
 FSDP = ("zh", "x")
 NX = 4
@@ -55,8 +56,12 @@
     copy_all([pair for k, out in enumerate(outs) for pair in pieces_to(where, k + 1, cot, hid, out)], sems)
 
 
-def local_kernel(where, cot, hid, drift, _, own, send0, sems):
-    copy_all(pieces_to(where, 0, cot, hid, own) + [(drift.at[0, 0], send0)], sems)
+def local_kernel(where, cot, hid, _, own, sems):
+    copy_all(pieces_to(where, 0, cot, hid, own), sems)
+
+
+def copy_kernel(source, _, out):
+    out[...] = source[0, 0]
 
 
 def masked_product(where, pieces, at, block, first, last):
@@ -103,16 +108,26 @@
         out[...] = total[:, :, k * cols : (k + 1) * cols].astype(out.dtype)
 
 
-def level0_kernel(weights, modules, got, out):
-    out[...] = jnp.zeros_like(out)
-    add_paths(weights, modules, 0, got, out)
-
-
-def update_kernel(weights, modules, average0, got, *refs):
+def level0_kernel(where, weights, modules, got, mine, other, total):
+    core, rows = where[2], mine.shape[1]
+    total[...] = jnp.zeros_like(total)
+
+    def add(i, carry):
+        p = 2 * i + core
+        m = modules[0, p]
+        total[m] = total[m] + weights[0, p] * got[i].astype(jnp.float32)
+        return carry
+
+    lax.fori_loop(0, got.shape[0], add, 0, unroll=4)
+    mine[...] = total[:, pl.ds(pl.multiple_of(core * rows, rows), rows)]
+    other[...] = total[:, pl.ds(pl.multiple_of((1 - core) * rows, rows), rows)]
+
+
+def update_kernel(weights, modules, mine0, other0, got, *refs):
     *parts, outer_params, outer_moment, new_params, new_moment, total = refs
     total[...] = functools.reduce(lambda a, b: a + b, [part[...].astype(jnp.float32) for part in parts])
     add_paths(weights, modules, 1, got, total)
-    for level, average in ((0, average0[...]), (1, total[...])):
+    for level, average in ((0, mine0[...] + other0[...]), (1, total[...])):
         moment = momentum_rate * outer_moment[level] + average
         new_moment[level] = moment
         new_params[level] = outer_params[level] - outer_rate * (average + momentum_rate * moment)
@@ -132,27 +147,36 @@
     foreign_cols = (NZ - 1) * cols
     bf16, f32 = jnp.bfloat16, jnp.float32
 
-    place = jnp.stack([zh, x]).astype(jnp.int32)
+    place = jnp.stack([zh, x, lax.axis_index("core")]).astype(jnp.int32)
     packed = pl.pallas_call(
         pack_kernel,
         out_shape=[jax.ShapeDtypeStruct(packed_shape, bf16)] * (NX - 1),
         in_specs=[SMEM, HBM, HBM],
-        out_specs=[HBM] * (NX - 1),
+        out_specs=[VMEM] * (NX - 1),
         scratch_shapes=[pltpu.SemaphoreType.DMA(((NX - 1) * (1 + NZ),))],
         compiler_params=params(LARGE),
     )(place, cotangent, hidden)
     pieces = [lax.ppermute(packed[k - 1], "x", shift("x", NX, k)) for k in range(1, NX)]
-    piece0, send0 = pl.pallas_call(
+    send0 = pl.pallas_call(
+        copy_kernel,
+        out_shape=jax.ShapeDtypeStruct((width, cols), bf16),
+        grid=(1,),
+        in_specs=[pl.BlockSpec((1, 1, width, cols), lambda r: (0, 0, 0, 0)), HBM],
+        out_specs=pl.BlockSpec((width, cols), lambda r: (0, 0)),
+        compiler_params=params(LARGE),
+    )(drift, packed[0])
+    piece0 = pl.pallas_call(
         local_kernel,
-        out_shape=[jax.ShapeDtypeStruct(packed_shape, bf16), jax.ShapeDtypeStruct((width, cols), bf16)],
-        in_specs=[SMEM, HBM, HBM, HBM, HBM],
-        out_specs=[HBM, HBM],
-        scratch_shapes=[pltpu.SemaphoreType.DMA((2 + NZ,))],
+        out_shape=jax.ShapeDtypeStruct(packed_shape, bf16),
+        in_specs=[SMEM, HBM, HBM, HBM],
+        out_specs=VMEM,
+        scratch_shapes=[pltpu.SemaphoreType.DMA((1 + NZ,))],
         compiler_params=params(LARGE),
-    )(place, cotangent, hidden, drift, packed[0])
+    )(place, cotangent, hidden, send0)
     pieces = [piece0] + pieces
+    chips = paths // 2
     got0 = lax.all_to_all(
-        send0.reshape(paths, owner_rows, cols), PATH, split_axis=0, concat_axis=0, tiled=True
+        send0.reshape(chips, 2 * owner_rows, cols), CHIPS, split_axis=0, concat_axis=0, tiled=True
     )
 
     member = (assignment[:, None, :] == jnp.arange(modules, dtype=jnp.int32)[None, :, None]).astype(f32)
@@ -182,6 +206,16 @@
     got_foreign = lax.all_to_all(
         foreign.reshape(paths, owner_rows, foreign_cols), PATH, split_axis=0, concat_axis=0, tiled=True
     )
+    mine0, other0 = pl.pallas_call(
+        level0_kernel,
+        out_shape=[jax.ShapeDtypeStruct((modules, owner_rows, cols), f32)] * 2,
+        in_specs=[SMEM, SMEM, SMEM, VMEM],
+        out_specs=[VMEM, VMEM],
+        scratch_shapes=[pltpu.VMEM((modules, 2 * owner_rows, cols), f32)],
+        compiler_params=params(),
+    )(place, weights, assignment, got0)
+    other0 = lax.ppermute(other0, "core", shift("core", 2, 1))
+    own, other0 = lax.optimization_barrier((own, other0))
     got_own = lax.all_to_all(
         own.reshape(paths, owner_rows, cols), PATH, split_axis=0, concat_axis=0, tiled=True
     )
@@ -194,21 +228,14 @@
         compiler_params=params(),
     )(weights, assignment, got_foreign)
     parts = [lax.ppermute(sums[k - 1], "zh", shift("zh", NZ, k)) for k in range(1, NZ)]
-    average0 = pl.pallas_call(
-        level0_kernel,
-        out_shape=jax.ShapeDtypeStruct((modules, owner_rows, cols), f32),
-        in_specs=[SMEM, SMEM, VMEM],
-        out_specs=VMEM,
-        compiler_params=params(),
-    )(weights, assignment, got0)
     return pl.pallas_call(
         update_kernel,
         out_shape=[jax.ShapeDtypeStruct(outer_params.shape, f32)] * 2,
-        in_specs=[SMEM, SMEM] + [VMEM] * (NZ + 3),
+        in_specs=[SMEM, SMEM] + [VMEM] * (NZ + 4),
         out_specs=[VMEM] * 2,
         scratch_shapes=[pltpu.VMEM((modules, owner_rows, cols), f32)],
         compiler_params=params(),
-    )(weights, assignment, average0, got_own, *parts, outer_params, outer_moment)
+    )(weights, assignment, mine0, other0, got_own, *parts, outer_params, outer_moment)
 
 
 def solution(mesh):

time: 221 us -> 143 us (0.65)
  the two profiles are of different devices: /device:TPU:8 before, /device:TPU:2 now
where the time goes in v6:
time: 143 us; the launch traced here: 142 us
  starting transfers between devices  70.9 us (50%)
  waiting for transfers between devices  51.6 us (36%)
  Pallas kernels  14.6 us (10%)
  local copies, waits for them, and re-layouts  2.24 us (2%)
  other arithmetic  2.1 us (1%)
    all_to_all x1, waiting for transfers between devices, body(): lax.all_to_all(foreign.reshape(paths, owner_rows, foreign_cols), PATH, sp...  35.3 us
    ppermute x3, starting transfers between devices, body(): lax.ppermute(sums[k - 1], 'zh', shift('zh', NZ, k))  26.2 us
    ppermute x3, starting transfers between devices, body(): lax.ppermute(packed[k - 1], 'x', shift('x', NX, k))  21 us
    all_to_all x1, starting transfers between devices, body(): lax.all_to_all(own.reshape(paths, owner_rows, cols), PATH, split_axis=0,...  9.24 us
    ppermute x3, waiting for transfers between devices, body(): lax.ppermute(sums[k - 1], 'zh', shift('zh', NZ, k))  9.06 us
    all_to_all x1, starting transfers between devices, body(): lax.all_to_all(foreign.reshape(paths, owner_rows, foreign_cols), PATH, sp...  8.49 us
    all_to_all x1, waiting for transfers between devices, body(): lax.all_to_all(send0.reshape(chips, 2 * owner_rows, cols), CHIPS, split_a...  4.77 us
    all_to_all x1, starting transfers between devices, body(): lax.all_to_all(send0.reshape(chips, 2 * owner_rows, cols), CHIPS, split_a...  4.02 us
  transfers between devices with their start and end apart: 10, of which 7 were waited for; matrix products, arithmetic and copies ran while one was open for 1% of the time, Pallas kernels for 7%

profile of v6, /device:TPU:2, one launch (start us, length us, event | category | flops | bytes accessed | tf_op | source)
XLA Modules:
  0.0 142.3 jit_solution(5905610061687777489)
XLA Ops:
  0.6 0.6 pad_add_fusion.where
  1.3 3.3 %shard_map.86 = (bf16[128,2048]{1,0:T(8,128)(2,1)}, bf16[128,2048]{1,0:T(8,128)(2,1)}, bf16[128,2048]{1,0:T(8,128)(2,1)}) custom-call(s32[3]{0:T(128)} %pad_add_fusion.where, bf16[1,128,1024]{2,1,0:T(8,128)(2,1)} %cot.3, bf16[1,128,4096]{2,1,0:T(8,128)(2,1)} %hid.3), custom_call_target="tpu_custom_call" | custom-call | tf_op jit(solution)/shard_map/pallas_call | solution.py:151
  4.6 3.4 %collective-permute-start = (bf16[128,2048]{1,0:T(8,128)(2,1)}, bf16[128,2048]{1,0:T(8,128)(2,1)S(1)}, u32[]{:S(2)}, u32[]{:S(2)}) collective-permute-start(bf16[128,2048]{1,0:T(8,128)(2,1)} %get-tuple-element.16._), channel_id=1, source_target_pairs={{0,1},{1,2},{2,3},{3,0},{4,5},{5,6},{6,7},{7,4},{8,9},{9,10},{10,1... | collective-permute-start | bytes 1572872 | tf_op jit(solution)/shard_map/ppermute | solution.py:159
  8.0 15.7 %collective-permute-start.1 = (bf16[128,2048]{1,0:T(8,128)(2,1)}, bf16[128,2048]{1,0:T(8,128)(2,1)S(1)}, u32[]{:S(2)}, u32[]{:S(2)}) collective-permute-start(bf16[128,2048]{1,0:T(8,128)(2,1)} %get-tuple-element.17), channel_id=1, source_target_pairs={{0,2},{1,3},{2,0},{3,1},{4,6},{5,7},{6,4},{7,5},{8,10},{9,11},{10,... | collective-permute-start | bytes 1572872 | tf_op jit(solution)/shard_map/ppermute | solution.py:159
  23.7 1.9 %collective-permute-start.2 = (bf16[128,2048]{1,0:T(8,128)(2,1)}, bf16[128,2048]{1,0:T(8,128)(2,1)S(1)}, u32[]{:S(2)}, u32[]{:S(2)}) collective-permute-start(bf16[128,2048]{1,0:T(8,128)(2,1)} %get-tuple-element.18), channel_id=1, source_target_pairs={{0,3},{1,0},{2,1},{3,2},{4,7},{5,4},{6,5},{7,6},{8,11},{9,8},{10,9... | collective-permute-start | bytes 1572872 | tf_op jit(solution)/shard_map/ppermute | solution.py:159
  25.6 1.9 %shard_map.87._ = bf16[1024,256]{1,0:T(8,128)(2,1)} custom-call(bf16[2,1,1024,256]{3,2,1,0:T(8,128)(2,1)} %refs_4_.2, bf16[128,2048]{1,0:T(8,128)(2,1)} %get-tuple-element.16._), custom_call_target="tpu_custom_call" | custom-call | tf_op jit(solution)/shard_map/pallas_call | solution.py:160
  27.5 4.0 %all-to-all-start = ((bf16[32,32,256]{2,1,0:T(8,128)(2,1)}), bf16[32,32,256]{2,1,0:T(8,128)(2,1)S(1)}, u32[]{:S(2)}, u32[]{:S(2)}) async-start(bf16[32,32,256]{2,1,0:T(8,128)(2,1)} %bitcast.8), calls=%async_computation | async-start | bytes 1048576 | tf_op jit(solution)/shard_map/all_to_all | solution.py:178
  31.5 2.5 %shard_map.88.refs_0_ = bf16[128,2048]{1,0:T(8,128)(2,1)} custom-call(s32[3]{0:T(128)} %pad_add_fusion.where, bf16[1,128,1024]{2,1,0:T(8,128)(2,1)} %cot.3, bf16[1,128,4096]{2,1,0:T(8,128)(2,1)} %hid.3, bf16[1024,256]{1,0:T(8,128)(2,1)} %shard_map.87._), custom_call_target="tpu_custom_call" | custom-call | tf_op jit(solution)/shard_map/pallas_call | solution.py:168
  34.1 0.6 fusion.6
  34.7 0.7 pad_add_fusion.2.where
  35.5 1.2 collective-permute-done.2.refs_3_
  36.7 1.0 copy-done.2
  37.7 3.1 %shard_map.89 = (bf16[1024,768]{1,0:T(8,128)(2,1)S(1)}, bf16[1024,256]{1,0:T(8,128)(2,1)}) custom-call(s32[3]{0:T(128)S(1)} %pad_add_fusion.2.where, bf16[128,2048]{1,0:T(8,128)(2,1)S(1)} %copy-done.2, bf16[128,2048]{1,0:T(8,128)(2,1)S(1)} %collective-permute-done.refs_1_, bf16[128,2048]{1,0:T(8,128)(2,1)S(1)} %collective-permute-done.1.refs_2_, ...), custom_call_target="tpu_custom_call" | custom-call | flops 30000001024 | bytes 4000000 | tf_op jit(solution)/shard_map/pallas_call | solution.py:190
  40.8 1.2 copy-done
  42.0 4.8 %all-to-all-done.got = bf16[32,32,256]{2,1,0:T(8,128)(2,1)S(1)} async-done(((bf16[32,32,256]{2,1,0:T(8,128)(2,1)}), bf16[32,32,256]{2,1,0:T(8,128)(2,1)S(1)}, u32[]{:S(2)}, u32[]{:S(2)}) %all-to-all-start) | async-done | bytes 524320 | tf_op jit(solution)/shard_map/all_to_all | solution.py:178
  46.8 8.5 %all-to-all-start.2 = ((bf16[64,16,768]{2,1,0:T(8,128)(2,1)}), bf16[64,16,768]{2,1,0:T(8,128)(2,1)S(1)}, u32[]{:S(2)}, u32[]{:S(2)}) async-start(bf16[64,16,768]{2,1,0:T(8,128)(2,1)} %bitcast.7), calls=%async_computation.2 | async-start | bytes 3145728 | tf_op jit(solution)/shard_map/all_to_all | solution.py:206
  55.3 0.1 fusion.8.weights
  55.4 0.0 copy-start.3
  55.4 0.0 copy-start.4
  55.4 0.8 shard_map.90
  56.2 2.0 %collective-permute-start.3 = (f32[8,16,256]{2,1,0:T(8,128)S(1)}, f32[8,16,256]{2,1,0:T(8,128)S(1)}, u32[]{:S(2)}, u32[]{:S(2)}) collective-permute-start(f32[8,16,256]{2,1,0:T(8,128)S(1)} %get-tuple-element.23), channel_id=1, source_target_pairs={{0,16},{16,0},{1,17},{17,1},{2,18},{18,2},{3,19},{19,3},{4,20},{20... | collective-permute-start | bytes 393224 | tf_op jit(solution)/shard_map/ppermute | solution.py:217
  58.2 1.3 collective-permute-done.3.other0
  59.4 35.3 %all-to-all-done.2.got = bf16[64,16,768]{2,1,0:T(8,128)(2,1)S(1)} async-done(((bf16[64,16,768]{2,1,0:T(8,128)(2,1)}), bf16[64,16,768]{2,1,0:T(8,128)(2,1)S(1)}, u32[]{:S(2)}, u32[]{:S(2)}) %all-to-all-start.2) | async-done | bytes 1572896 | tf_op jit(solution)/shard_map/all_to_all | solution.py:206
  94.7 9.2 %all-to-all-start.1 = ((bf16[64,16,256]{2,1,0:T(8,128)(2,1)}), bf16[64,16,256]{2,1,0:T(8,128)(2,1)S(1)}, u32[]{:S(2)}, u32[]{:S(2)}) async-start(bf16[64,16,256]{2,1,0:T(8,128)(2,1)} %bitcast.5), calls=%async_computation.1 | async-start | bytes 1048576 | tf_op jit(solution)/shard_map/all_to_all | solution.py:219
  104.0 1.1 shard_map.91
  105.1 10.9 %collective-permute-start.4 = (bf16[8,16,256]{2,1,0:T(8,128)(2,1)S(1)}, bf16[8,16,256]{2,1,0:T(8,128)(2,1)S(1)}, u32[]{:S(2)}, u32[]{:S(2)}) collective-permute-start(bf16[8,16,256]{2,1,0:T(8,128)(2,1)S(1)} %get-tuple-element.27), channel_id=1, source_target_pairs={{0,4},{4,8},{8,12},{12,0},{1,5},{5,9},{9,13},{13,1},{2,6},{6,10},{... | collective-permute-start | bytes 196616 | tf_op jit(solution)/shard_map/ppermute | solution.py:230
  116.0 11.8 %collective-permute-start.5 = (bf16[8,16,256]{2,1,0:T(8,128)(2,1)S(1)}, bf16[8,16,256]{2,1,0:T(8,128)(2,1)S(1)}, u32[]{:S(2)}, u32[]{:S(2)}) collective-permute-start(bf16[8,16,256]{2,1,0:T(8,128)(2,1)S(1)} %get-tuple-element.28), channel_id=1, source_target_pairs={{0,8},{4,12},{8,0},{12,4},{1,9},{5,13},{9,1},{13,5},{2,10},{6,14},... | collective-permute-start | bytes 196616 | tf_op jit(solution)/shard_map/ppermute | solution.py:230
  127.9 3.5 %collective-permute-start.6 = (bf16[8,16,256]{2,1,0:T(8,128)(2,1)S(1)}, bf16[8,16,256]{2,1,0:T(8,128)(2,1)S(1)}, u32[]{:S(2)}, u32[]{:S(2)}) collective-permute-start(bf16[8,16,256]{2,1,0:T(8,128)(2,1)S(1)} %get-tuple-element.29), channel_id=1, source_target_pairs={{0,12},{4,0},{8,4},{12,8},{1,13},{5,1},{9,5},{13,9},{2,14},{6,2},{... | collective-permute-start | bytes 196616 | tf_op jit(solution)/shard_map/ppermute | solution.py:230
  131.4 0.5 collective-permute-done.4.refs_0_
  131.9 1.6 %collective-permute-done.5.refs_1_ = bf16[8,16,256]{2,1,0:T(8,128)(2,1)S(1)} collective-permute-done((bf16[8,16,256]{2,1,0:T(8,128)(2,1)S(1)}, bf16[8,16,256]{2,1,0:T(8,128)(2,1)S(1)}, u32[]{:S(2)}, u32[]{:S(2)}) %collective-permute-start.5) | collective-permute-done | bytes 65568 | tf_op jit(solution)/shard_map/ppermute | solution.py:230
  133.5 6.9 %collective-permute-done.6.refs_2_ = bf16[8,16,256]{2,1,0:T(8,128)(2,1)S(1)} collective-permute-done((bf16[8,16,256]{2,1,0:T(8,128)(2,1)S(1)}, bf16[8,16,256]{2,1,0:T(8,128)(2,1)S(1)}, u32[]{:S(2)}, u32[]{:S(2)}) %collective-permute-start.6) | collective-permute-done | bytes 65568 | tf_op jit(solution)/shard_map/ppermute | solution.py:230
  140.4 1.9 %shard_map.92 = (f32[2,8,16,256]{3,2,1,0:T(8,128)}, f32[2,8,16,256]{3,2,1,0:T(8,128)}) custom-call(f32[2,64]{1,0:T(2,128)S(1)} %fusion.8.weights, s32[2,64]{1,0:T(2,128)S(1)} %copy-done.5, f32[8,16,256]{2,1,0:T(8,128)S(1)} %get-tuple-element.21.mine0, f32[8,16,256]{2,1,0:T(8,128)S(1)} %collective-permute-done.3.other0, ...), custom_call_target="tpu_custom_call" | custom-call | tf_op jit(solution)/shard_map/pallas_call | solution.py:231
  (15 shorter events, 0.0 us)
Async XLA Ops:
  4.6 30.9 %collective-permute-start = (bf16[128,2048]{1,0:T(8,128)(2,1)}, bf16[128,2048]{1,0:T(8,128)(2,1)S(1)}, u32[]{:S(2)}, u32[]{:S(2)}) collective-permute-start(bf16[128,2048]{1,0:T(8,128)(2,1)} %get-tuple-element.16._), channel_id=1, source_target_pairs={{0,1},{1,2},{2,3},{3,0},{4,5},{5,6},{6,7},{7,4},{8,9},{9,10},{10,1... | collective-permute-start | bytes 1572872 | tf_op jit(solution)/shard_map/ppermute | solution.py:159
  8.0 27.5 %collective-permute-start.1 = (bf16[128,2048]{1,0:T(8,128)(2,1)}, bf16[128,2048]{1,0:T(8,128)(2,1)S(1)}, u32[]{:S(2)}, u32[]{:S(2)}) collective-permute-start(bf16[128,2048]{1,0:T(8,128)(2,1)} %get-tuple-element.17), channel_id=1, source_target_pairs={{0,2},{1,3},{2,0},{3,1},{4,6},{5,7},{6,4},{7,5},{8,10},{9,11},{10,... | collective-permute-start | bytes 1572872 | tf_op jit(solution)/shard_map/ppermute | solution.py:159
  23.7 13.0 %collective-permute-start.2 = (bf16[128,2048]{1,0:T(8,128)(2,1)}, bf16[128,2048]{1,0:T(8,128)(2,1)S(1)}, u32[]{:S(2)}, u32[]{:S(2)}) collective-permute-start(bf16[128,2048]{1,0:T(8,128)(2,1)} %get-tuple-element.18), channel_id=1, source_target_pairs={{0,3},{1,0},{2,1},{3,2},{4,7},{5,4},{6,5},{7,6},{8,11},{9,8},{10,9... | collective-permute-start | bytes 1572872 | tf_op jit(solution)/shard_map/ppermute | solution.py:159
  27.5 6.6 %copy-start.7 = (s32[64]{0:T(128)S(1)}, s32[64]{0:T(128)}, u32[]{:S(2)}) copy-start(s32[64]{0:T(128)} %param.10) | copy-start | bytes 772
  27.5 9.1 %copy-start.1 = (bf16[2,1,1024,256]{3,2,1,0:T(8,128)(2,1)S(1)}, bf16[2,1,1024,256]{3,2,1,0:T(8,128)(2,1)}, u32[]{:S(2)}) copy-start(bf16[2,1,1024,256]{3,2,1,0:T(8,128)(2,1)} %refs_4_.2) | copy-start | bytes 3145732
  27.5 19.3 %all-to-all-start = ((bf16[32,32,256]{2,1,0:T(8,128)(2,1)}), bf16[32,32,256]{2,1,0:T(8,128)(2,1)S(1)}, u32[]{:S(2)}, u32[]{:S(2)}) async-start(bf16[32,32,256]{2,1,0:T(8,128)(2,1)} %bitcast.8), calls=%async_computation | async-start | bytes 1048576 | tf_op jit(solution)/shard_map/all_to_all | solution.py:178
  36.7 1.0 copy-start.2
  40.8 1.2 copy-start
  46.8 8.5 %copy-start.5 = (s32[2,64]{1,0:T(2,128)S(1)}, s32[2,64]{1,0:T(2,128)}, u32[]{:S(2)}) copy-start(s32[2,64]{1,0:T(2,128)} %modules.5) | copy-start | bytes 1540
  46.8 8.6 %copy-start.6 = (s32[3]{0:T(128)S(1)}, s32[3]{0:T(128)}, u32[]{:S(2)}) copy-start(s32[3]{0:T(128)} %pad_add_fusion.where) | copy-start | bytes 40
  46.8 48.0 %all-to-all-start.2 = ((bf16[64,16,768]{2,1,0:T(8,128)(2,1)}), bf16[64,16,768]{2,1,0:T(8,128)(2,1)S(1)}, u32[]{:S(2)}, u32[]{:S(2)}) async-start(bf16[64,16,768]{2,1,0:T(8,128)(2,1)} %bitcast.7), calls=%async_computation.2 | async-start | bytes 3145728 | tf_op jit(solution)/shard_map/all_to_all | solution.py:206
  55.4 85.0 %copy-start.3 = (f32[2,8,16,256]{3,2,1,0:T(8,128)S(1)}, f32[2,8,16,256]{3,2,1,0:T(8,128)}, u32[]{:S(2)}) copy-start(f32[2,8,16,256]{3,2,1,0:T(8,128)} %refs_3_.1) | copy-start | bytes 786436
  55.4 85.0 %copy-start.4 = (f32[2,8,16,256]{3,2,1,0:T(8,128)S(1)}, f32[2,8,16,256]{3,2,1,0:T(8,128)}, u32[]{:S(2)}) copy-start(f32[2,8,16,256]{3,2,1,0:T(8,128)} %refs_4_.3) | copy-start | bytes 786436
  56.2 3.2 %collective-permute-start.3 = (f32[8,16,256]{2,1,0:T(8,128)S(1)}, f32[8,16,256]{2,1,0:T(8,128)S(1)}, u32[]{:S(2)}, u32[]{:S(2)}) collective-permute-start(f32[8,16,256]{2,1,0:T(8,128)S(1)} %get-tuple-element.23), channel_id=1, source_target_pairs={{0,16},{16,0},{1,17},{17,1},{2,18},{18,2},{3,19},{19,3},{4,20},{20... | collective-permute-start | bytes 393224 | tf_op jit(solution)/shard_map/ppermute | solution.py:217
  94.7 36.6 %all-to-all-start.1 = ((bf16[64,16,256]{2,1,0:T(8,128)(2,1)}), bf16[64,16,256]{2,1,0:T(8,128)(2,1)S(1)}, u32[]{:S(2)}, u32[]{:S(2)}) async-start(bf16[64,16,256]{2,1,0:T(8,128)(2,1)} %bitcast.5), calls=%async_computation.1 | async-start | bytes 1048576 | tf_op jit(solution)/shard_map/all_to_all | solution.py:219
  105.1 26.8 %collective-permute-start.4 = (bf16[8,16,256]{2,1,0:T(8,128)(2,1)S(1)}, bf16[8,16,256]{2,1,0:T(8,128)(2,1)S(1)}, u32[]{:S(2)}, u32[]{:S(2)}) collective-permute-start(bf16[8,16,256]{2,1,0:T(8,128)(2,1)S(1)} %get-tuple-element.27), channel_id=1, source_target_pairs={{0,4},{4,8},{8,12},{12,0},{1,5},{5,9},{9,13},{13,1},{2,6},{6,10},{... | collective-permute-start | bytes 196616 | tf_op jit(solution)/shard_map/ppermute | solution.py:230
  116.0 17.5 %collective-permute-start.5 = (bf16[8,16,256]{2,1,0:T(8,128)(2,1)S(1)}, bf16[8,16,256]{2,1,0:T(8,128)(2,1)S(1)}, u32[]{:S(2)}, u32[]{:S(2)}) collective-permute-start(bf16[8,16,256]{2,1,0:T(8,128)(2,1)S(1)} %get-tuple-element.28), channel_id=1, source_target_pairs={{0,8},{4,12},{8,0},{12,4},{1,9},{5,13},{9,1},{13,5},{2,10},{6,14},... | collective-permute-start | bytes 196616 | tf_op jit(solution)/shard_map/ppermute | solution.py:230
  127.9 12.5 %collective-permute-start.6 = (bf16[8,16,256]{2,1,0:T(8,128)(2,1)S(1)}, bf16[8,16,256]{2,1,0:T(8,128)(2,1)S(1)}, u32[]{:S(2)}, u32[]{:S(2)}) collective-permute-start(bf16[8,16,256]{2,1,0:T(8,128)(2,1)S(1)} %get-tuple-element.29), channel_id=1, source_target_pairs={{0,12},{4,0},{8,4},{12,8},{1,13},{5,1},{9,5},{13,9},{2,14},{6,2},{... | collective-permute-start | bytes 196616 | tf_op jit(solution)/shard_map/ppermute | solution.py:230

commit v7 on v6

--- a/solution.py
+++ b/solution.py
@@ -15,6 +15,7 @@
 PATH = ("zl", "y", "core")
 FSDP = ("zh", "x")
 NX = 4
+SHIFTS = (0, 2, 3, 1)
 NZ = 4
 LIMIT = 24 * 2**20
 LARGE = 56 * 2**20
@@ -51,9 +52,19 @@
         copy.wait()
 
 
-def pack_kernel(where, cot, hid, *refs):
-    *outs, sems = refs
-    copy_all([pair for k, out in enumerate(outs) for pair in pieces_to(where, k + 1, cot, hid, out)], sems)
+def pack_kernel(cot, hid, *refs):
+    *outs, packed = refs
+    packed[...] = jnp.zeros_like(packed)
+    zh, x = lax.axis_index("zh"), lax.axis_index("x")
+    width = cot.shape[2]
+    cols = hid.shape[2] // (NX * NZ)
+    for k, out in enumerate(outs):
+        to = (x + k + 1) % NX
+        out[:, :width] = cot[0]
+        for j in range(NZ):
+            z = (zh + j) % NZ
+            start = pl.multiple_of((z * NX + to) * cols, cols)
+            out[:, width + j * cols : width + (j + 1) * cols] = hid[0, :, pl.ds(start, cols)]
 
 
 def local_kernel(where, cot, hid, _, own, sems):
@@ -67,8 +78,8 @@
 def masked_product(where, pieces, at, block, first, last):
     rows = pieces[0].shape[0]
     left = []
-    for k, piece in enumerate(pieces):
-        source = (where[1] - k + NX) % NX
+    for by, piece in zip(SHIFTS, pieces):
+        source = (where[1] - by + NX) % NX
         token = (where[0] * NX + source) * rows + lax.broadcasted_iota(jnp.int32, (rows, block), 0)
         value = piece[:, pl.ds(at, block)].astype(jnp.float32)
         left.append(jnp.where(token < where[2], value, 0.0).astype(jnp.bfloat16))
@@ -148,23 +159,28 @@
     bf16, f32 = jnp.bfloat16, jnp.float32
 
     place = jnp.stack([zh, x, lax.axis_index("core")]).astype(jnp.int32)
-    packed = pl.pallas_call(
+    step = 32
+    *packed, after = pl.pallas_call(
         pack_kernel,
-        out_shape=[jax.ShapeDtypeStruct(packed_shape, bf16)] * (NX - 1),
-        in_specs=[SMEM, HBM, HBM],
-        out_specs=[VMEM] * (NX - 1),
-        scratch_shapes=[pltpu.SemaphoreType.DMA(((NX - 1) * (1 + NZ),))],
+        out_shape=[jax.ShapeDtypeStruct(packed_shape, bf16)] * (NX - 1) + [jax.ShapeDtypeStruct((8, 128), f32)],
+        grid=(rows // step,),
+        in_specs=[
+            pl.BlockSpec((1, step, width), lambda r: (0, r, 0)),
+            pl.BlockSpec((1, step, hidden.shape[2]), lambda r: (0, r, 0)),
+        ],
+        out_specs=[pl.BlockSpec((step, packed_shape[1]), lambda r: (r, 0))] * (NX - 1)
+        + [pl.BlockSpec((8, 128), lambda r: (0, 0))],
         compiler_params=params(LARGE),
-    )(place, cotangent, hidden)
-    pieces = [lax.ppermute(packed[k - 1], "x", shift("x", NX, k)) for k in range(1, NX)]
+    )(cotangent, hidden)
+    pieces = [lax.ppermute(packed[k - 1], "x", shift("x", NX, k)) for k in SHIFTS[1:]]
     send0 = pl.pallas_call(
         copy_kernel,
         out_shape=jax.ShapeDtypeStruct((width, cols), bf16),
         grid=(1,),
         in_specs=[pl.BlockSpec((1, 1, width, cols), lambda r: (0, 0, 0, 0)), HBM],
         out_specs=pl.BlockSpec((width, cols), lambda r: (0, 0)),
-        compiler_params=params(LARGE),
-    )(drift, packed[0])
+        compiler_params=params(),
+    )(drift, after)
     piece0 = pl.pallas_call(
         local_kernel,
         out_shape=jax.ShapeDtypeStruct(packed_shape, bf16),
@@ -227,7 +243,7 @@
         scratch_shapes=[pltpu.VMEM((modules, owner_rows, foreign_cols), f32)],
         compiler_params=params(),
     )(weights, assignment, got_foreign)
-    parts = [lax.ppermute(sums[k - 1], "zh", shift("zh", NZ, k)) for k in range(1, NZ)]
+    parts = [lax.ppermute(sums[k - 1], "zh", shift("zh", NZ, k)) for k in SHIFTS[1:]]
     return pl.pallas_call(
         update_kernel,
         out_shape=[jax.ShapeDtypeStruct(outer_params.shape, f32)] * 2,

time: 143 us -> 137 us (0.958)
  the two profiles are of different devices: /device:TPU:2 before, /device:TPU:81 now
where the time goes in v7:
time: 137 us; the launch traced here: 136 us
  starting transfers between devices  68.3 us (50%)
  waiting for transfers between devices  48.5 us (35%)
  Pallas kernels  13.9 us (10%)
  local copies, waits for them, and re-layouts  2.93 us (2%)
  other arithmetic  1.96 us (1%)
    all_to_all x1, waiting for transfers between devices, body(): lax.all_to_all(foreign.reshape(paths, owner_rows, foreign_cols), PATH, sp...  35 us
    ppermute x3, starting transfers between devices, body(): lax.ppermute(sums[k - 1], 'zh', shift('zh', NZ, k))  25.4 us
    all_to_all x1, starting transfers between devices, body(): lax.all_to_all(send0.reshape(chips, 2 * owner_rows, cols), CHIPS, split_a...  11.6 us
    ppermute x3, starting transfers between devices, body(): lax.ppermute(packed[k - 1], 'x', shift('x', NX, k))  10.1 us
    all_to_all x1, starting transfers between devices, body(): lax.all_to_all(foreign.reshape(paths, owner_rows, foreign_cols), PATH, sp...  9.55 us
    all_to_all x1, starting transfers between devices, body(): lax.all_to_all(own.reshape(paths, owner_rows, cols), PATH, split_axis=0,...  9.53 us
    ppermute x3, waiting for transfers between devices, body(): lax.ppermute(sums[k - 1], 'zh', shift('zh', NZ, k))  7.91 us
    pallas_call x1, Pallas kernels, body(): pl.pallas_call(pack_kernel, out_shape=[jax.ShapeDtypeStruct(packed_shape,...  3.68 us
  transfers between devices with their start and end apart: 10, of which 7 were waited for; matrix products, arithmetic and copies ran while one was open for 1% of the time, Pallas kernels for 6%

profile of v7, /device:TPU:81, one launch (start us, length us, event | category | flops | bytes accessed | tf_op | source)
XLA Modules:
  0.0 136.4 jit_solution(3789360993423876516)
XLA Ops:
  0.6 3.7 %shard_map.86 = (bf16[128,2048]{1,0:T(8,128)(2,1)}, bf16[128,2048]{1,0:T(8,128)(2,1)}, bf16[128,2048]{1,0:T(8,128)(2,1)}, f32[8,128]{1,0:T(8,128)}) custom-call(bf16[1,128,1024]{2,1,0:T(8,128)(2,1)} %cot.3, bf16[1,128,4096]{2,1,0:T(8,128)(2,1)} %hid.3), custom_call_target="tpu_custom_call" | custom-call | tf_op jit(solution)/shard_map/pallas_call | solution.py:163
  4.3 4.8 %collective-permute-start = (bf16[128,2048]{1,0:T(8,128)(2,1)}, bf16[128,2048]{1,0:T(8,128)(2,1)S(1)}, u32[]{:S(2)}, u32[]{:S(2)}) collective-permute-start(bf16[128,2048]{1,0:T(8,128)(2,1)} %get-tuple-element.18), channel_id=1, source_target_pairs={{0,2},{1,3},{2,0},{3,1},{4,6},{5,7},{6,4},{7,5},{8,10},{9,11},{10,... | collective-permute-start | bytes 1572872 | tf_op jit(solution)/shard_map/ppermute | solution.py:175
  9.1 2.8 %collective-permute-start.1 = (bf16[128,2048]{1,0:T(8,128)(2,1)}, bf16[128,2048]{1,0:T(8,128)(2,1)S(1)}, u32[]{:S(2)}, u32[]{:S(2)}) collective-permute-start(bf16[128,2048]{1,0:T(8,128)(2,1)} %get-tuple-element.19), channel_id=1, source_target_pairs={{0,3},{1,0},{2,1},{3,2},{4,7},{5,4},{6,5},{7,6},{8,11},{9,8},{10,9... | collective-permute-start | bytes 1572872 | tf_op jit(solution)/shard_map/ppermute | solution.py:175
  11.9 2.5 %collective-permute-start.2 = (bf16[128,2048]{1,0:T(8,128)(2,1)}, bf16[128,2048]{1,0:T(8,128)(2,1)S(1)}, u32[]{:S(2)}, u32[]{:S(2)}) collective-permute-start(bf16[128,2048]{1,0:T(8,128)(2,1)} %get-tuple-element.20), channel_id=1, source_target_pairs={{0,1},{1,2},{2,3},{3,0},{4,5},{5,6},{6,7},{7,4},{8,9},{9,10},{10,1... | collective-permute-start | bytes 1572872 | tf_op jit(solution)/shard_map/ppermute | solution.py:175
  14.4 0.7 copy-done.7
  15.1 0.9 shard_map.87._
  16.0 11.6 %all-to-all-start = ((bf16[32,32,256]{2,1,0:T(8,128)(2,1)}), bf16[32,32,256]{2,1,0:T(8,128)(2,1)S(1)}, u32[]{:S(2)}, u32[]{:S(2)}) async-start(bf16[32,32,256]{2,1,0:T(8,128)(2,1)} %bitcast.4), calls=%async_computation | async-start | bytes 1048576 | tf_op jit(solution)/shard_map/all_to_all | solution.py:194
  27.5 0.6 fusion.6
  28.2 1.2 pad_add_fusion
  29.4 2.5 %shard_map.88.refs_0_ = bf16[128,2048]{1,0:T(8,128)(2,1)} custom-call(s32[3]{0:T(128)} %get-tuple-element.34.where, bf16[1,128,1024]{2,1,0:T(8,128)(2,1)} %cot.3, bf16[1,128,4096]{2,1,0:T(8,128)(2,1)} %hid.3, bf16[1024,256]{1,0:T(8,128)(2,1)} %shard_map.87._), custom_call_target="tpu_custom_call" | custom-call | tf_op jit(solution)/shard_map/pallas_call | solution.py:184
  31.9 0.4 collective-permute-done.1.refs_2_
  32.3 0.8 collective-permute-done.2.refs_3_
  33.1 1.0 copy-done.2
  34.2 3.1 %shard_map.89 = (bf16[1024,768]{1,0:T(8,128)(2,1)S(1)}, bf16[1024,256]{1,0:T(8,128)(2,1)}) custom-call(s32[3]{0:T(128)S(1)} %get-tuple-element.35.where, bf16[128,2048]{1,0:T(8,128)(2,1)S(1)} %copy-done.2, bf16[128,2048]{1,0:T(8,128)(2,1)S(1)} %collective-permute-done.refs_1_, bf16[128,2048]{1,0:T(8,128)(2,1)S(1)} %collective-permute-done.1.refs_2_, ...), custom_call_target="tpu_custom_call" | custom-call | flops 30000001024 | bytes 4000000 | tf_op jit(solution)/shard_map/pallas_call | solution.py:206
  37.3 1.2 copy-done
  38.4 3.4 %all-to-all-done.got = bf16[32,32,256]{2,1,0:T(8,128)(2,1)S(1)} async-done(((bf16[32,32,256]{2,1,0:T(8,128)(2,1)}), bf16[32,32,256]{2,1,0:T(8,128)(2,1)S(1)}, u32[]{:S(2)}, u32[]{:S(2)}) %all-to-all-start) | async-done | bytes 524320 | tf_op jit(solution)/shard_map/all_to_all | solution.py:194
  41.8 9.5 %all-to-all-start.2 = ((bf16[64,16,768]{2,1,0:T(8,128)(2,1)}), bf16[64,16,768]{2,1,0:T(8,128)(2,1)S(1)}, u32[]{:S(2)}, u32[]{:S(2)}) async-start(bf16[64,16,768]{2,1,0:T(8,128)(2,1)} %bitcast.7), calls=%async_computation.2 | async-start | bytes 3145728 | tf_op jit(solution)/shard_map/all_to_all | solution.py:222
  51.4 0.1 fusion.8.weights
  51.5 0.0 copy-start.3
  51.5 0.0 copy-start.4
  51.5 0.8 shard_map.90
  52.3 2.3 %collective-permute-start.3 = (f32[8,16,256]{2,1,0:T(8,128)S(1)}, f32[8,16,256]{2,1,0:T(8,128)S(1)}, u32[]{:S(2)}, u32[]{:S(2)}) collective-permute-start(f32[8,16,256]{2,1,0:T(8,128)S(1)} %get-tuple-element.25), channel_id=1, source_target_pairs={{0,16},{16,0},{1,17},{17,1},{2,18},{18,2},{3,19},{19,3},{4,20},{20... | collective-permute-start | bytes 393224 | tf_op jit(solution)/shard_map/ppermute | solution.py:233
  54.6 1.0 collective-permute-done.3.other0
  55.6 35.0 %all-to-all-done.2.got = bf16[64,16,768]{2,1,0:T(8,128)(2,1)S(1)} async-done(((bf16[64,16,768]{2,1,0:T(8,128)(2,1)}), bf16[64,16,768]{2,1,0:T(8,128)(2,1)S(1)}, u32[]{:S(2)}, u32[]{:S(2)}) %all-to-all-start.2) | async-done | bytes 1572896 | tf_op jit(solution)/shard_map/all_to_all | solution.py:222
  90.6 9.5 %all-to-all-start.1 = ((bf16[64,16,256]{2,1,0:T(8,128)(2,1)}), bf16[64,16,256]{2,1,0:T(8,128)(2,1)S(1)}, u32[]{:S(2)}, u32[]{:S(2)}) async-start(bf16[64,16,256]{2,1,0:T(8,128)(2,1)} %bitcast.5), calls=%async_computation.1 | async-start | bytes 1048576 | tf_op jit(solution)/shard_map/all_to_all | solution.py:235
  100.1 1.1 shard_map.91
  101.2 16.2 %collective-permute-start.4 = (bf16[8,16,256]{2,1,0:T(8,128)(2,1)S(1)}, bf16[8,16,256]{2,1,0:T(8,128)(2,1)S(1)}, u32[]{:S(2)}, u32[]{:S(2)}) collective-permute-start(bf16[8,16,256]{2,1,0:T(8,128)(2,1)S(1)} %get-tuple-element.29), channel_id=1, source_target_pairs={{0,8},{4,12},{8,0},{12,4},{1,9},{5,13},{9,1},{13,5},{2,10},{6,14},... | collective-permute-start | bytes 196616 | tf_op jit(solution)/shard_map/ppermute | solution.py:246
  117.4 1.9 %collective-permute-start.5 = (bf16[8,16,256]{2,1,0:T(8,128)(2,1)S(1)}, bf16[8,16,256]{2,1,0:T(8,128)(2,1)S(1)}, u32[]{:S(2)}, u32[]{:S(2)}) collective-permute-start(bf16[8,16,256]{2,1,0:T(8,128)(2,1)S(1)} %get-tuple-element.30), channel_id=1, source_target_pairs={{0,12},{4,0},{8,4},{12,8},{1,13},{5,1},{9,5},{13,9},{2,14},{6,2},{... | collective-permute-start | bytes 196616 | tf_op jit(solution)/shard_map/ppermute | solution.py:246
  119.3 7.3 %collective-permute-start.6 = (bf16[8,16,256]{2,1,0:T(8,128)(2,1)S(1)}, bf16[8,16,256]{2,1,0:T(8,128)(2,1)S(1)}, u32[]{:S(2)}, u32[]{:S(2)}) collective-permute-start(bf16[8,16,256]{2,1,0:T(8,128)(2,1)S(1)} %get-tuple-element.31), channel_id=1, source_target_pairs={{0,4},{4,8},{8,12},{12,0},{1,5},{5,9},{9,13},{13,1},{2,6},{6,10},{... | collective-permute-start | bytes 196616 | tf_op jit(solution)/shard_map/ppermute | solution.py:246
  126.6 1.2 collective-permute-done.5.refs_1_
  127.8 6.7 %collective-permute-done.6.refs_2_ = bf16[8,16,256]{2,1,0:T(8,128)(2,1)S(1)} collective-permute-done((bf16[8,16,256]{2,1,0:T(8,128)(2,1)S(1)}, bf16[8,16,256]{2,1,0:T(8,128)(2,1)S(1)}, u32[]{:S(2)}, u32[]{:S(2)}) %collective-permute-start.6) | collective-permute-done | bytes 65568 | tf_op jit(solution)/shard_map/ppermute | solution.py:246
  134.5 1.9 %shard_map.92 = (f32[2,8,16,256]{3,2,1,0:T(8,128)}, f32[2,8,16,256]{3,2,1,0:T(8,128)}) custom-call(f32[2,64]{1,0:T(2,128)S(1)} %fusion.8.weights, s32[2,64]{1,0:T(2,128)S(1)} %copy-done.5, f32[8,16,256]{2,1,0:T(8,128)S(1)} %get-tuple-element.23.mine0, f32[8,16,256]{2,1,0:T(8,128)S(1)} %collective-permute-done.3.other0, ...), custom_call_target="tpu_custom_call" | custom-call | tf_op jit(solution)/shard_map/pallas_call | solution.py:247
  (16 shorter events, 0.0 us)
Async XLA Ops:
  0.6 13.8 %copy-start.1 = (bf16[2,1,1024,256]{3,2,1,0:T(8,128)(2,1)S(1)}, bf16[2,1,1024,256]{3,2,1,0:T(8,128)(2,1)}, u32[]{:S(2)}) copy-start(bf16[2,1,1024,256]{3,2,1,0:T(8,128)(2,1)} %refs_4_.2) | copy-start | bytes 3145732
  4.3 23.2 %copy-start.8 = (s32[64]{0:T(128)S(1)}, s32[64]{0:T(128)}, u32[]{:S(2)}) copy-start(s32[64]{0:T(128)} %param.10) | copy-start | bytes 772
  4.3 27.6 %collective-permute-start = (bf16[128,2048]{1,0:T(8,128)(2,1)}, bf16[128,2048]{1,0:T(8,128)(2,1)S(1)}, u32[]{:S(2)}, u32[]{:S(2)}) collective-permute-start(bf16[128,2048]{1,0:T(8,128)(2,1)} %get-tuple-element.18), channel_id=1, source_target_pairs={{0,2},{1,3},{2,0},{3,1},{4,6},{5,7},{6,4},{7,5},{8,10},{9,11},{10,... | collective-permute-start | bytes 1572872 | tf_op jit(solution)/shard_map/ppermute | solution.py:175
  9.1 23.2 %collective-permute-start.1 = (bf16[128,2048]{1,0:T(8,128)(2,1)}, bf16[128,2048]{1,0:T(8,128)(2,1)S(1)}, u32[]{:S(2)}, u32[]{:S(2)}) collective-permute-start(bf16[128,2048]{1,0:T(8,128)(2,1)} %get-tuple-element.19), channel_id=1, source_target_pairs={{0,3},{1,0},{2,1},{3,2},{4,7},{5,4},{6,5},{7,6},{8,11},{9,8},{10,9... | collective-permute-start | bytes 1572872 | tf_op jit(solution)/shard_map/ppermute | solution.py:175
  11.9 21.3 %collective-permute-start.2 = (bf16[128,2048]{1,0:T(8,128)(2,1)}, bf16[128,2048]{1,0:T(8,128)(2,1)S(1)}, u32[]{:S(2)}, u32[]{:S(2)}) collective-permute-start(bf16[128,2048]{1,0:T(8,128)(2,1)} %get-tuple-element.20), channel_id=1, source_target_pairs={{0,1},{1,2},{2,3},{3,0},{4,5},{5,6},{6,7},{7,4},{8,9},{9,10},{10,1... | collective-permute-start | bytes 1572872 | tf_op jit(solution)/shard_map/ppermute | solution.py:175
  14.4 0.7 copy-start.7
  16.0 25.9 %all-to-all-start = ((bf16[32,32,256]{2,1,0:T(8,128)(2,1)}), bf16[32,32,256]{2,1,0:T(8,128)(2,1)S(1)}, u32[]{:S(2)}, u32[]{:S(2)}) async-start(bf16[32,32,256]{2,1,0:T(8,128)(2,1)} %bitcast.4), calls=%async_computation | async-start | bytes 1048576 | tf_op jit(solution)/shard_map/all_to_all | solution.py:194
  33.1 1.0 copy-start.2
  37.2 1.2 copy-start
  41.8 9.6 %copy-start.5 = (s32[2,64]{1,0:T(2,128)S(1)}, s32[2,64]{1,0:T(2,128)}, u32[]{:S(2)}) copy-start(s32[2,64]{1,0:T(2,128)} %modules.5) | copy-start | bytes 1540
  41.8 9.7 %copy-start.6 = (s32[3]{0:T(128)S(1)}, s32[3]{0:T(128)}, u32[]{:S(2)}) copy-start(s32[3]{0:T(128)} %get-tuple-element.34.where) | copy-start | bytes 40
  41.8 48.7 %all-to-all-start.2 = ((bf16[64,16,768]{2,1,0:T(8,128)(2,1)}), bf16[64,16,768]{2,1,0:T(8,128)(2,1)S(1)}, u32[]{:S(2)}, u32[]{:S(2)}) async-start(bf16[64,16,768]{2,1,0:T(8,128)(2,1)} %bitcast.7), calls=%async_computation.2 | async-start | bytes 3145728 | tf_op jit(solution)/shard_map/all_to_all | solution.py:222
  51.5 83.0 %copy-start.3 = (f32[2,8,16,256]{3,2,1,0:T(8,128)S(1)}, f32[2,8,16,256]{3,2,1,0:T(8,128)}, u32[]{:S(2)}) copy-start(f32[2,8,16,256]{3,2,1,0:T(8,128)} %refs_3_.1) | copy-start | bytes 786436
  51.5 83.0 %copy-start.4 = (f32[2,8,16,256]{3,2,1,0:T(8,128)S(1)}, f32[2,8,16,256]{3,2,1,0:T(8,128)}, u32[]{:S(2)}) copy-start(f32[2,8,16,256]{3,2,1,0:T(8,128)} %refs_4_.3) | copy-start | bytes 786436
  52.3 3.2 %collective-permute-start.3 = (f32[8,16,256]{2,1,0:T(8,128)S(1)}, f32[8,16,256]{2,1,0:T(8,128)S(1)}, u32[]{:S(2)}, u32[]{:S(2)}) collective-permute-start(f32[8,16,256]{2,1,0:T(8,128)S(1)} %get-tuple-element.25), channel_id=1, source_target_pairs={{0,16},{16,0},{1,17},{17,1},{2,18},{18,2},{3,19},{19,3},{4,20},{20... | collective-permute-start | bytes 393224 | tf_op jit(solution)/shard_map/ppermute | solution.py:233
  90.6 36.1 %all-to-all-start.1 = ((bf16[64,16,256]{2,1,0:T(8,128)(2,1)}), bf16[64,16,256]{2,1,0:T(8,128)(2,1)S(1)}, u32[]{:S(2)}, u32[]{:S(2)}) async-start(bf16[64,16,256]{2,1,0:T(8,128)(2,1)} %bitcast.5), calls=%async_computation.1 | async-start | bytes 1048576 | tf_op jit(solution)/shard_map/all_to_all | solution.py:235
  101.2 25.4 %collective-permute-start.4 = (bf16[8,16,256]{2,1,0:T(8,128)(2,1)S(1)}, bf16[8,16,256]{2,1,0:T(8,128)(2,1)S(1)}, u32[]{:S(2)}, u32[]{:S(2)}) collective-permute-start(bf16[8,16,256]{2,1,0:T(8,128)(2,1)S(1)} %get-tuple-element.29), channel_id=1, source_target_pairs={{0,8},{4,12},{8,0},{12,4},{1,9},{5,13},{9,1},{13,5},{2,10},{6,14},... | collective-permute-start | bytes 196616 | tf_op jit(solution)/shard_map/ppermute | solution.py:246
  117.4 10.4 %collective-permute-start.5 = (bf16[8,16,256]{2,1,0:T(8,128)(2,1)S(1)}, bf16[8,16,256]{2,1,0:T(8,128)(2,1)S(1)}, u32[]{:S(2)}, u32[]{:S(2)}) collective-permute-start(bf16[8,16,256]{2,1,0:T(8,128)(2,1)S(1)} %get-tuple-element.30), channel_id=1, source_target_pairs={{0,12},{4,0},{8,4},{12,8},{1,13},{5,1},{9,5},{13,9},{2,14},{6,2},{... | collective-permute-start | bytes 196616 | tf_op jit(solution)/shard_map/ppermute | solution.py:246
  119.3 15.2 %collective-permute-start.6 = (bf16[8,16,256]{2,1,0:T(8,128)(2,1)S(1)}, bf16[8,16,256]{2,1,0:T(8,128)(2,1)S(1)}, u32[]{:S(2)}, u32[]{:S(2)}) collective-permute-start(bf16[8,16,256]{2,1,0:T(8,128)(2,1)S(1)} %get-tuple-element.31), channel_id=1, source_target_pairs={{0,4},{4,8},{8,12},{12,0},{1,5},{5,9},{9,13},{13,1},{2,6},{6,10},{... | collective-permute-start | bytes 196616 | tf_op jit(solution)/shard_map/ppermute | solution.py:246

commit v8 on v7

--- a/solution.py
+++ b/solution.py
@@ -52,9 +52,9 @@
         copy.wait()
 
 
-def pack_kernel(cot, hid, *refs):
-    *outs, packed = refs
-    packed[...] = jnp.zeros_like(packed)
+def pack_kernel(cot, hid, drift, *refs):
+    *outs, send0 = refs
+    send0[...] = drift[0, 0]
     zh, x = lax.axis_index("zh"), lax.axis_index("x")
     width = cot.shape[2]
     cols = hid.shape[2] // (NX * NZ)
@@ -69,10 +69,6 @@
 
 def local_kernel(where, cot, hid, _, own, sems):
     copy_all(pieces_to(where, 0, cot, hid, own), sems)
-
-
-def copy_kernel(source, _, out):
-    out[...] = source[0, 0]
 
 
 def masked_product(where, pieces, at, block, first, last):
@@ -159,28 +155,23 @@
     bf16, f32 = jnp.bfloat16, jnp.float32
 
     place = jnp.stack([zh, x, lax.axis_index("core")]).astype(jnp.int32)
-    step = 32
-    *packed, after = pl.pallas_call(
+    step = 64
+    part = width // (rows // step)
+    *packed, send0 = pl.pallas_call(
         pack_kernel,
-        out_shape=[jax.ShapeDtypeStruct(packed_shape, bf16)] * (NX - 1) + [jax.ShapeDtypeStruct((8, 128), f32)],
+        out_shape=[jax.ShapeDtypeStruct(packed_shape, bf16)] * (NX - 1)
+        + [jax.ShapeDtypeStruct((width, cols), bf16)],
         grid=(rows // step,),
         in_specs=[
             pl.BlockSpec((1, step, width), lambda r: (0, r, 0)),
             pl.BlockSpec((1, step, hidden.shape[2]), lambda r: (0, r, 0)),
+            pl.BlockSpec((1, 1, part, cols), lambda r: (0, 0, r, 0)),
         ],
         out_specs=[pl.BlockSpec((step, packed_shape[1]), lambda r: (r, 0))] * (NX - 1)
-        + [pl.BlockSpec((8, 128), lambda r: (0, 0))],
+        + [pl.BlockSpec((part, cols), lambda r: (r, 0))],
         compiler_params=params(LARGE),
-    )(cotangent, hidden)
+    )(cotangent, hidden, drift)
     pieces = [lax.ppermute(packed[k - 1], "x", shift("x", NX, k)) for k in SHIFTS[1:]]
-    send0 = pl.pallas_call(
-        copy_kernel,
-        out_shape=jax.ShapeDtypeStruct((width, cols), bf16),
-        grid=(1,),
-        in_specs=[pl.BlockSpec((1, 1, width, cols), lambda r: (0, 0, 0, 0)), HBM],
-        out_specs=pl.BlockSpec((width, cols), lambda r: (0, 0)),
-        compiler_params=params(),
-    )(drift, after)
     piece0 = pl.pallas_call(
         local_kernel,
         out_shape=jax.ShapeDtypeStruct(packed_shape, bf16),

time: 137 us -> 136 us (level)
  Pallas kernels: 13.9 us -> 12 us
  starting transfers between devices: 68.3 us -> 69.8 us
    all_to_all x1, waiting for transfers between devices: 3.39 us -> 1.94 us  [body(): lax.all_to_all(send0.reshape(chips, 2 * owner_rows, cols), CHIPS, split_a...]
    all_to_all x1, starting transfers between devices: 9.55 us -> 11 us  [body(): lax.all_to_all(foreign.reshape(paths, owner_rows, foreign_cols), PATH, sp...]
    ppermute x3, waiting for transfers between devices: 1.2 us -> 2.57 us  [body(): lax.ppermute(packed[k - 1], 'x', shift('x', NX, k))]
    unnamed x18 -> x16, local copies, waits for them, and re-layouts: 2.93 us -> 2.24 us
where the time goes in v8:
time: 136 us; the launch traced here: 135 us
  starting transfers between devices  69.8 us (51%)
  waiting for transfers between devices  48.4 us (36%)
  Pallas kernels  12 us (9%)
  local copies, waits for them, and re-layouts  2.24 us (2%)
  other arithmetic  1.98 us (1%)
    all_to_all x1, waiting for transfers between devices, body(): lax.all_to_all(foreign.reshape(paths, owner_rows, foreign_cols), PATH, sp...  35 us
    ppermute x3, starting transfers between devices, body(): lax.ppermute(sums[k - 1], 'zh', shift('zh', NZ, k))  25.4 us
    all_to_all x1, starting transfers between devices, body(): lax.all_to_all(send0.reshape(chips, 2 * owner_rows, cols), CHIPS, split_a...  11.7 us
    all_to_all x1, starting transfers between devices, body(): lax.all_to_all(foreign.reshape(paths, owner_rows, foreign_cols), PATH, sp...  11 us
    ppermute x3, starting transfers between devices, body(): lax.ppermute(packed[k - 1], 'x', shift('x', NX, k))  9.92 us
    all_to_all x1, starting transfers between devices, body(): lax.all_to_all(own.reshape(paths, owner_rows, cols), PATH, split_axis=0,...  9.53 us
    ppermute x3, waiting for transfers between devices, body(): lax.ppermute(sums[k - 1], 'zh', shift('zh', NZ, k))  7.9 us
    pallas_call x1, Pallas kernels, body(): pl.pallas_call(grad_kernel, out_shape=[jax.ShapeDtypeStruct((width, forei...  3.13 us
  transfers between devices with their start and end apart: 10, of which 7 were waited for; matrix products, arithmetic and copies ran while one was open for 1% of the time, Pallas kernels for 6%

profile of v8, /device:TPU:81, one launch (start us, length us, event | category | flops | bytes accessed | tf_op | source)
XLA Modules:
  0.0 135.2 jit_solution(11760483423448921748)
XLA Ops:
  0.6 2.5 %shard_map.86 = (bf16[128,2048]{1,0:T(8,128)(2,1)}, bf16[128,2048]{1,0:T(8,128)(2,1)}, bf16[128,2048]{1,0:T(8,128)(2,1)}, bf16[1024,256]{1,0:T(8,128)(2,1)}) custom-call(bf16[1,128,1024]{2,1,0:T(8,128)(2,1)} %cot.3, bf16[1,128,4096]{2,1,0:T(8,128)(2,1)} %hid.3, bf16[2,1,1024,256]{3,2,1,0:T(8,128)(2,1)} %refs_4_.2), custom_call_target="tpu_custom_call" | custom-call | tf_op jit(solution)/shard_map/pallas_call | solution.py:160
  3.2 4.6 %collective-permute-start = (bf16[128,2048]{1,0:T(8,128)(2,1)}, bf16[128,2048]{1,0:T(8,128)(2,1)S(1)}, u32[]{:S(2)}, u32[]{:S(2)}) collective-permute-start(bf16[128,2048]{1,0:T(8,128)(2,1)} %get-tuple-element.18), channel_id=1, source_target_pairs={{0,2},{1,3},{2,0},{3,1},{4,6},{5,7},{6,4},{7,5},{8,10},{9,11},{10,... | collective-permute-start | bytes 1572872 | tf_op jit(solution)/shard_map/ppermute | solution.py:174
  7.8 2.8 %collective-permute-start.1 = (bf16[128,2048]{1,0:T(8,128)(2,1)}, bf16[128,2048]{1,0:T(8,128)(2,1)S(1)}, u32[]{:S(2)}, u32[]{:S(2)}) collective-permute-start(bf16[128,2048]{1,0:T(8,128)(2,1)} %get-tuple-element.19), channel_id=1, source_target_pairs={{0,3},{1,0},{2,1},{3,2},{4,7},{5,4},{6,5},{7,6},{8,11},{9,8},{10,9... | collective-permute-start | bytes 1572872 | tf_op jit(solution)/shard_map/ppermute | solution.py:174
  10.6 2.5 %collective-permute-start.2 = (bf16[128,2048]{1,0:T(8,128)(2,1)}, bf16[128,2048]{1,0:T(8,128)(2,1)S(1)}, u32[]{:S(2)}, u32[]{:S(2)}) collective-permute-start(bf16[128,2048]{1,0:T(8,128)(2,1)} %get-tuple-element.20), channel_id=1, source_target_pairs={{0,1},{1,2},{2,3},{3,0},{4,5},{5,6},{6,7},{7,4},{8,9},{9,10},{10,1... | collective-permute-start | bytes 1572872 | tf_op jit(solution)/shard_map/ppermute | solution.py:174
  13.1 0.0 copy-start.1
  13.1 11.7 %all-to-all-start = ((bf16[32,32,256]{2,1,0:T(8,128)(2,1)}), bf16[32,32,256]{2,1,0:T(8,128)(2,1)S(1)}, u32[]{:S(2)}, u32[]{:S(2)}) async-start(bf16[32,32,256]{2,1,0:T(8,128)(2,1)} %bitcast.8), calls=%async_computation | async-start | bytes 1048576 | tf_op jit(solution)/shard_map/all_to_all | solution.py:185
  24.9 0.6 fusion.6
  25.5 1.3 pad_add_fusion
  26.8 2.5 %shard_map.87.refs_0_ = bf16[128,2048]{1,0:T(8,128)(2,1)} custom-call(s32[3]{0:T(128)} %get-tuple-element.34.where, bf16[1,128,1024]{2,1,0:T(8,128)(2,1)} %cot.3, bf16[1,128,4096]{2,1,0:T(8,128)(2,1)} %hid.3, bf16[1024,256]{1,0:T(8,128)(2,1)} %get-tuple-element.17._), custom_call_target="tpu_custom_call" | custom-call | tf_op jit(solution)/shard_map/pallas_call | solution.py:175
  29.3 0.0 collective-permute-done.refs_1_
  29.3 1.7 %collective-permute-done.1.refs_2_ = bf16[128,2048]{1,0:T(8,128)(2,1)S(1)} collective-permute-done((bf16[128,2048]{1,0:T(8,128)(2,1)}, bf16[128,2048]{1,0:T(8,128)(2,1)S(1)}, u32[]{:S(2)}, u32[]{:S(2)}) %collective-permute-start.1) | collective-permute-done | bytes 524320 | tf_op jit(solution)/shard_map/ppermute | solution.py:174
  31.0 0.8 collective-permute-done.2.refs_3_
  31.9 1.0 copy-done.2
  32.9 3.1 %shard_map.88 = (bf16[1024,768]{1,0:T(8,128)(2,1)S(1)}, bf16[1024,256]{1,0:T(8,128)(2,1)}) custom-call(s32[3]{0:T(128)S(1)} %get-tuple-element.35.where, bf16[128,2048]{1,0:T(8,128)(2,1)S(1)} %copy-done.2, bf16[128,2048]{1,0:T(8,128)(2,1)S(1)} %collective-permute-done.refs_1_, bf16[128,2048]{1,0:T(8,128)(2,1)S(1)} %collective-permute-done.1.refs_2_, ...), custom_call_target="tpu_custom_call" | custom-call | flops 30000001024 | bytes 4000000 | tf_op jit(solution)/shard_map/pallas_call | solution.py:197
  36.0 1.2 copy-done
  37.2 1.9 %all-to-all-done.got = bf16[32,32,256]{2,1,0:T(8,128)(2,1)S(1)} async-done(((bf16[32,32,256]{2,1,0:T(8,128)(2,1)}), bf16[32,32,256]{2,1,0:T(8,128)(2,1)S(1)}, u32[]{:S(2)}, u32[]{:S(2)}) %all-to-all-start) | async-done | bytes 524320 | tf_op jit(solution)/shard_map/all_to_all | solution.py:185
  39.2 11.0 %all-to-all-start.2 = ((bf16[64,16,768]{2,1,0:T(8,128)(2,1)}), bf16[64,16,768]{2,1,0:T(8,128)(2,1)S(1)}, u32[]{:S(2)}, u32[]{:S(2)}) async-start(bf16[64,16,768]{2,1,0:T(8,128)(2,1)} %bitcast.7), calls=%async_computation.2 | async-start | bytes 3145728 | tf_op jit(solution)/shard_map/all_to_all | solution.py:213
  50.2 0.1 fusion.8.weights
  50.3 0.0 copy-start.3
  50.3 0.0 copy-start.4
  50.3 0.8 shard_map.89
  51.1 2.3 %collective-permute-start.3 = (f32[8,16,256]{2,1,0:T(8,128)S(1)}, f32[8,16,256]{2,1,0:T(8,128)S(1)}, u32[]{:S(2)}, u32[]{:S(2)}) collective-permute-start(f32[8,16,256]{2,1,0:T(8,128)S(1)} %get-tuple-element.25), channel_id=1, source_target_pairs={{0,16},{16,0},{1,17},{17,1},{2,18},{18,2},{3,19},{19,3},{4,20},{20... | collective-permute-start | bytes 393224 | tf_op jit(solution)/shard_map/ppermute | solution.py:224
  53.4 1.0 collective-permute-done.3.other0
  54.3 35.0 %all-to-all-done.2.got = bf16[64,16,768]{2,1,0:T(8,128)(2,1)S(1)} async-done(((bf16[64,16,768]{2,1,0:T(8,128)(2,1)}), bf16[64,16,768]{2,1,0:T(8,128)(2,1)S(1)}, u32[]{:S(2)}, u32[]{:S(2)}) %all-to-all-start.2) | async-done | bytes 1572896 | tf_op jit(solution)/shard_map/all_to_all | solution.py:213
  89.3 9.5 %all-to-all-start.1 = ((bf16[64,16,256]{2,1,0:T(8,128)(2,1)}), bf16[64,16,256]{2,1,0:T(8,128)(2,1)S(1)}, u32[]{:S(2)}, u32[]{:S(2)}) async-start(bf16[64,16,256]{2,1,0:T(8,128)(2,1)} %bitcast.5), calls=%async_computation.1 | async-start | bytes 1048576 | tf_op jit(solution)/shard_map/all_to_all | solution.py:226
  98.9 1.1 shard_map.90
  100.0 16.2 %collective-permute-start.4 = (bf16[8,16,256]{2,1,0:T(8,128)(2,1)S(1)}, bf16[8,16,256]{2,1,0:T(8,128)(2,1)S(1)}, u32[]{:S(2)}, u32[]{:S(2)}) collective-permute-start(bf16[8,16,256]{2,1,0:T(8,128)(2,1)S(1)} %get-tuple-element.29), channel_id=1, source_target_pairs={{0,8},{4,12},{8,0},{12,4},{1,9},{5,13},{9,1},{13,5},{2,10},{6,14},... | collective-permute-start | bytes 196616 | tf_op jit(solution)/shard_map/ppermute | solution.py:237
  116.2 1.9 %collective-permute-start.5 = (bf16[8,16,256]{2,1,0:T(8,128)(2,1)S(1)}, bf16[8,16,256]{2,1,0:T(8,128)(2,1)S(1)}, u32[]{:S(2)}, u32[]{:S(2)}) collective-permute-start(bf16[8,16,256]{2,1,0:T(8,128)(2,1)S(1)} %get-tuple-element.30), channel_id=1, source_target_pairs={{0,12},{4,0},{8,4},{12,8},{1,13},{5,1},{9,5},{13,9},{2,14},{6,2},{... | collective-permute-start | bytes 196616 | tf_op jit(solution)/shard_map/ppermute | solution.py:237
  118.1 7.3 %collective-permute-start.6 = (bf16[8,16,256]{2,1,0:T(8,128)(2,1)S(1)}, bf16[8,16,256]{2,1,0:T(8,128)(2,1)S(1)}, u32[]{:S(2)}, u32[]{:S(2)}) collective-permute-start(bf16[8,16,256]{2,1,0:T(8,128)(2,1)S(1)} %get-tuple-element.31), channel_id=1, source_target_pairs={{0,4},{4,8},{8,12},{12,0},{1,5},{5,9},{9,13},{13,1},{2,6},{6,10},{... | collective-permute-start | bytes 196616 | tf_op jit(solution)/shard_map/ppermute | solution.py:237
  125.4 1.2 collective-permute-done.5.refs_1_
  126.6 6.7 %collective-permute-done.6.refs_2_ = bf16[8,16,256]{2,1,0:T(8,128)(2,1)S(1)} collective-permute-done((bf16[8,16,256]{2,1,0:T(8,128)(2,1)S(1)}, bf16[8,16,256]{2,1,0:T(8,128)(2,1)S(1)}, u32[]{:S(2)}, u32[]{:S(2)}) %collective-permute-start.6) | collective-permute-done | bytes 65568 | tf_op jit(solution)/shard_map/ppermute | solution.py:237
  133.3 1.9 %shard_map.91 = (f32[2,8,16,256]{3,2,1,0:T(8,128)}, f32[2,8,16,256]{3,2,1,0:T(8,128)}) custom-call(f32[2,64]{1,0:T(2,128)S(1)} %fusion.8.weights, s32[2,64]{1,0:T(2,128)S(1)} %copy-done.5, f32[8,16,256]{2,1,0:T(8,128)S(1)} %get-tuple-element.23.mine0, f32[8,16,256]{2,1,0:T(8,128)S(1)} %collective-permute-done.3.other0, ...), custom_call_target="tpu_custom_call" | custom-call | tf_op jit(solution)/shard_map/pallas_call | solution.py:238
  (13 shorter events, 0.0 us)
Async XLA Ops:
  0.6 24.2 %copy-start.7 = (s32[64]{0:T(128)S(1)}, s32[64]{0:T(128)}, u32[]{:S(2)}) copy-start(s32[64]{0:T(128)} %param.10) | copy-start | bytes 772
  3.2 26.1 %collective-permute-start = (bf16[128,2048]{1,0:T(8,128)(2,1)}, bf16[128,2048]{1,0:T(8,128)(2,1)S(1)}, u32[]{:S(2)}, u32[]{:S(2)}) collective-permute-start(bf16[128,2048]{1,0:T(8,128)(2,1)} %get-tuple-element.18), channel_id=1, source_target_pairs={{0,2},{1,3},{2,0},{3,1},{4,6},{5,7},{6,4},{7,5},{8,10},{9,11},{10,... | collective-permute-start | bytes 1572872 | tf_op jit(solution)/shard_map/ppermute | solution.py:174
  7.8 23.2 %collective-permute-start.1 = (bf16[128,2048]{1,0:T(8,128)(2,1)}, bf16[128,2048]{1,0:T(8,128)(2,1)S(1)}, u32[]{:S(2)}, u32[]{:S(2)}) collective-permute-start(bf16[128,2048]{1,0:T(8,128)(2,1)} %get-tuple-element.19), channel_id=1, source_target_pairs={{0,3},{1,0},{2,1},{3,2},{4,7},{5,4},{6,5},{7,6},{8,11},{9,8},{10,9... | collective-permute-start | bytes 1572872 | tf_op jit(solution)/shard_map/ppermute | solution.py:174
  10.6 21.3 %collective-permute-start.2 = (bf16[128,2048]{1,0:T(8,128)(2,1)}, bf16[128,2048]{1,0:T(8,128)(2,1)S(1)}, u32[]{:S(2)}, u32[]{:S(2)}) collective-permute-start(bf16[128,2048]{1,0:T(8,128)(2,1)} %get-tuple-element.20), channel_id=1, source_target_pairs={{0,1},{1,2},{2,3},{3,0},{4,5},{5,6},{6,7},{7,4},{8,9},{9,10},{10,1... | collective-permute-start | bytes 1572872 | tf_op jit(solution)/shard_map/ppermute | solution.py:174
  13.1 18.7 %copy-start.1 = (bf16[2,1,1024,256]{3,2,1,0:T(8,128)(2,1)S(1)}, bf16[2,1,1024,256]{3,2,1,0:T(8,128)(2,1)}, u32[]{:S(2)}) copy-start(bf16[2,1,1024,256]{3,2,1,0:T(8,128)(2,1)} %refs_4_.2) | copy-start | bytes 3145732
  13.1 26.0 %all-to-all-start = ((bf16[32,32,256]{2,1,0:T(8,128)(2,1)}), bf16[32,32,256]{2,1,0:T(8,128)(2,1)S(1)}, u32[]{:S(2)}, u32[]{:S(2)}) async-start(bf16[32,32,256]{2,1,0:T(8,128)(2,1)} %bitcast.8), calls=%async_computation | async-start | bytes 1048576 | tf_op jit(solution)/shard_map/all_to_all | solution.py:185
  31.9 1.0 copy-start.2
  36.0 1.2 copy-start
  39.1 11.0 %copy-start.5 = (s32[2,64]{1,0:T(2,128)S(1)}, s32[2,64]{1,0:T(2,128)}, u32[]{:S(2)}) copy-start(s32[2,64]{1,0:T(2,128)} %modules.5) | copy-start | bytes 1540
  39.2 11.1 %copy-start.6 = (s32[3]{0:T(128)S(1)}, s32[3]{0:T(128)}, u32[]{:S(2)}) copy-start(s32[3]{0:T(128)} %get-tuple-element.34.where) | copy-start | bytes 40
  39.2 50.2 %all-to-all-start.2 = ((bf16[64,16,768]{2,1,0:T(8,128)(2,1)}), bf16[64,16,768]{2,1,0:T(8,128)(2,1)S(1)}, u32[]{:S(2)}, u32[]{:S(2)}) async-start(bf16[64,16,768]{2,1,0:T(8,128)(2,1)} %bitcast.7), calls=%async_computation.2 | async-start | bytes 3145728 | tf_op jit(solution)/shard_map/all_to_all | solution.py:213
  50.3 83.0 %copy-start.3 = (f32[2,8,16,256]{3,2,1,0:T(8,128)S(1)}, f32[2,8,16,256]{3,2,1,0:T(8,128)}, u32[]{:S(2)}) copy-start(f32[2,8,16,256]{3,2,1,0:T(8,128)} %refs_3_.1) | copy-start | bytes 786436
  50.3 83.0 %copy-start.4 = (f32[2,8,16,256]{3,2,1,0:T(8,128)S(1)}, f32[2,8,16,256]{3,2,1,0:T(8,128)}, u32[]{:S(2)}) copy-start(f32[2,8,16,256]{3,2,1,0:T(8,128)} %refs_4_.3) | copy-start | bytes 786436
  51.1 3.2 %collective-permute-start.3 = (f32[8,16,256]{2,1,0:T(8,128)S(1)}, f32[8,16,256]{2,1,0:T(8,128)S(1)}, u32[]{:S(2)}, u32[]{:S(2)}) collective-permute-start(f32[8,16,256]{2,1,0:T(8,128)S(1)} %get-tuple-element.25), channel_id=1, source_target_pairs={{0,16},{16,0},{1,17},{17,1},{2,18},{18,2},{3,19},{19,3},{4,20},{20... | collective-permute-start | bytes 393224 | tf_op jit(solution)/shard_map/ppermute | solution.py:224
  89.3 36.1 %all-to-all-start.1 = ((bf16[64,16,256]{2,1,0:T(8,128)(2,1)}), bf16[64,16,256]{2,1,0:T(8,128)(2,1)S(1)}, u32[]{:S(2)}, u32[]{:S(2)}) async-start(bf16[64,16,256]{2,1,0:T(8,128)(2,1)} %bitcast.5), calls=%async_computation.1 | async-start | bytes 1048576 | tf_op jit(solution)/shard_map/all_to_all | solution.py:226
  100.0 25.4 %collective-permute-start.4 = (bf16[8,16,256]{2,1,0:T(8,128)(2,1)S(1)}, bf16[8,16,256]{2,1,0:T(8,128)(2,1)S(1)}, u32[]{:S(2)}, u32[]{:S(2)}) collective-permute-start(bf16[8,16,256]{2,1,0:T(8,128)(2,1)S(1)} %get-tuple-element.29), channel_id=1, source_target_pairs={{0,8},{4,12},{8,0},{12,4},{1,9},{5,13},{9,1},{13,5},{2,10},{6,14},... | collective-permute-start | bytes 196616 | tf_op jit(solution)/shard_map/ppermute | solution.py:237
  116.2 10.4 %collective-permute-start.5 = (bf16[8,16,256]{2,1,0:T(8,128)(2,1)S(1)}, bf16[8,16,256]{2,1,0:T(8,128)(2,1)S(1)}, u32[]{:S(2)}, u32[]{:S(2)}) collective-permute-start(bf16[8,16,256]{2,1,0:T(8,128)(2,1)S(1)} %get-tuple-element.30), channel_id=1, source_target_pairs={{0,12},{4,0},{8,4},{12,8},{1,13},{5,1},{9,5},{13,9},{2,14},{6,2},{... | collective-permute-start | bytes 196616 | tf_op jit(solution)/shard_map/ppermute | solution.py:237
  118.1 15.2 %collective-permute-start.6 = (bf16[8,16,256]{2,1,0:T(8,128)(2,1)S(1)}, bf16[8,16,256]{2,1,0:T(8,128)(2,1)S(1)}, u32[]{:S(2)}, u32[]{:S(2)}) collective-permute-start(bf16[8,16,256]{2,1,0:T(8,128)(2,1)S(1)} %get-tuple-element.31), channel_id=1, source_target_pairs={{0,4},{4,8},{8,12},{12,0},{1,5},{5,9},{9,13},{13,1},{2,6},{6,10},{... | collective-permute-start | bytes 196616 | tf_op jit(solution)/shard_map/ppermute | solution.py:237

commit v9 on v8

--- a/solution.py
+++ b/solution.py
@@ -103,7 +103,7 @@
         total[m] = total[m] + weights[level, p] * got[p].astype(jnp.float32)
         return carry
 
-    lax.fori_loop(0, got.shape[0], add, 0, unroll=4)
+    lax.fori_loop(0, got.shape[0], add, 0, unroll=16)
 
 
 def module_kernel(weights, modules, got, *refs):
@@ -125,7 +125,7 @@
         total[m] = total[m] + weights[0, p] * got[i].astype(jnp.float32)
         return carry
 
-    lax.fori_loop(0, got.shape[0], add, 0, unroll=4)
+    lax.fori_loop(0, got.shape[0], add, 0, unroll=16)
     mine[...] = total[:, pl.ds(pl.multiple_of(core * rows, rows), rows)]
     other[...] = total[:, pl.ds(pl.multiple_of((1 - core) * rows, rows), rows)]
 

time: 136 us -> 136 us (level)
  no operation moved by 1% of the time
where the time goes in v9:
time: 136 us; the launch traced here: 135 us
  starting transfers between devices  69.8 us (51%)
  waiting for transfers between devices  48.4 us (36%)
  Pallas kernels  11.9 us (9%)
  local copies, waits for them, and re-layouts  2.24 us (2%)
  other arithmetic  1.98 us (1%)
    all_to_all x1, waiting for transfers between devices, body(): lax.all_to_all(foreign.reshape(paths, owner_rows, foreign_cols), PATH, sp...  35 us
    ppermute x3, starting transfers between devices, body(): lax.ppermute(sums[k - 1], 'zh', shift('zh', NZ, k))  25.4 us
    all_to_all x1, starting transfers between devices, body(): lax.all_to_all(send0.reshape(chips, 2 * owner_rows, cols), CHIPS, split_a...  11.7 us
    all_to_all x1, starting transfers between devices, body(): lax.all_to_all(foreign.reshape(paths, owner_rows, foreign_cols), PATH, sp...  11 us
    ppermute x3, starting transfers between devices, body(): lax.ppermute(packed[k - 1], 'x', shift('x', NX, k))  9.92 us
    all_to_all x1, starting transfers between devices, body(): lax.all_to_all(own.reshape(paths, owner_rows, cols), PATH, split_axis=0,...  9.53 us
    ppermute x3, waiting for transfers between devices, body(): lax.ppermute(sums[k - 1], 'zh', shift('zh', NZ, k))  7.89 us
    pallas_call x1, Pallas kernels, body(): pl.pallas_call(grad_kernel, out_shape=[jax.ShapeDtypeStruct((width, forei...  3.13 us
  transfers between devices with their start and end apart: 10, of which 7 were waited for; matrix products, arithmetic and copies ran while one was open for 1% of the time, Pallas kernels for 6%

profile of v9, /device:TPU:81, one launch (start us, length us, event | category | flops | bytes accessed | tf_op | source)
XLA Modules:
  0.0 135.1 jit_solution(13736656594012091312)
XLA Ops:
  0.6 2.5 %shard_map.86 = (bf16[128,2048]{1,0:T(8,128)(2,1)}, bf16[128,2048]{1,0:T(8,128)(2,1)}, bf16[128,2048]{1,0:T(8,128)(2,1)}, bf16[1024,256]{1,0:T(8,128)(2,1)}) custom-call(bf16[1,128,1024]{2,1,0:T(8,128)(2,1)} %cot.3, bf16[1,128,4096]{2,1,0:T(8,128)(2,1)} %hid.3, bf16[2,1,1024,256]{3,2,1,0:T(8,128)(2,1)} %refs_4_.2), custom_call_target="tpu_custom_call" | custom-call | tf_op jit(solution)/shard_map/pallas_call | solution.py:160
  3.2 4.6 %collective-permute-start = (bf16[128,2048]{1,0:T(8,128)(2,1)}, bf16[128,2048]{1,0:T(8,128)(2,1)S(1)}, u32[]{:S(2)}, u32[]{:S(2)}) collective-permute-start(bf16[128,2048]{1,0:T(8,128)(2,1)} %get-tuple-element.18), channel_id=1, source_target_pairs={{0,2},{1,3},{2,0},{3,1},{4,6},{5,7},{6,4},{7,5},{8,10},{9,11},{10,... | collective-permute-start | bytes 1572872 | tf_op jit(solution)/shard_map/ppermute | solution.py:174
  7.8 2.8 %collective-permute-start.1 = (bf16[128,2048]{1,0:T(8,128)(2,1)}, bf16[128,2048]{1,0:T(8,128)(2,1)S(1)}, u32[]{:S(2)}, u32[]{:S(2)}) collective-permute-start(bf16[128,2048]{1,0:T(8,128)(2,1)} %get-tuple-element.19), channel_id=1, source_target_pairs={{0,3},{1,0},{2,1},{3,2},{4,7},{5,4},{6,5},{7,6},{8,11},{9,8},{10,9... | collective-permute-start | bytes 1572872 | tf_op jit(solution)/shard_map/ppermute | solution.py:174
  10.6 2.5 %collective-permute-start.2 = (bf16[128,2048]{1,0:T(8,128)(2,1)}, bf16[128,2048]{1,0:T(8,128)(2,1)S(1)}, u32[]{:S(2)}, u32[]{:S(2)}) collective-permute-start(bf16[128,2048]{1,0:T(8,128)(2,1)} %get-tuple-element.20), channel_id=1, source_target_pairs={{0,1},{1,2},{2,3},{3,0},{4,5},{5,6},{6,7},{7,4},{8,9},{9,10},{10,1... | collective-permute-start | bytes 1572872 | tf_op jit(solution)/shard_map/ppermute | solution.py:174
  13.1 0.0 copy-start.1
  13.1 11.7 %all-to-all-start = ((bf16[32,32,256]{2,1,0:T(8,128)(2,1)}), bf16[32,32,256]{2,1,0:T(8,128)(2,1)S(1)}, u32[]{:S(2)}, u32[]{:S(2)}) async-start(bf16[32,32,256]{2,1,0:T(8,128)(2,1)} %bitcast.8), calls=%async_computation | async-start | bytes 1048576 | tf_op jit(solution)/shard_map/all_to_all | solution.py:185
  24.9 0.6 fusion.6
  25.5 1.3 pad_add_fusion
  26.8 2.5 %shard_map.87.refs_0_ = bf16[128,2048]{1,0:T(8,128)(2,1)} custom-call(s32[3]{0:T(128)} %get-tuple-element.34.where, bf16[1,128,1024]{2,1,0:T(8,128)(2,1)} %cot.3, bf16[1,128,4096]{2,1,0:T(8,128)(2,1)} %hid.3, bf16[1024,256]{1,0:T(8,128)(2,1)} %get-tuple-element.17._), custom_call_target="tpu_custom_call" | custom-call | tf_op jit(solution)/shard_map/pallas_call | solution.py:175
  29.3 0.0 collective-permute-done.refs_1_
  29.3 1.7 %collective-permute-done.1.refs_2_ = bf16[128,2048]{1,0:T(8,128)(2,1)S(1)} collective-permute-done((bf16[128,2048]{1,0:T(8,128)(2,1)}, bf16[128,2048]{1,0:T(8,128)(2,1)S(1)}, u32[]{:S(2)}, u32[]{:S(2)}) %collective-permute-start.1) | collective-permute-done | bytes 524320 | tf_op jit(solution)/shard_map/ppermute | solution.py:174
  31.0 0.8 collective-permute-done.2.refs_3_
  31.9 1.0 copy-done.2
  32.9 3.1 %shard_map.88 = (bf16[1024,768]{1,0:T(8,128)(2,1)S(1)}, bf16[1024,256]{1,0:T(8,128)(2,1)}) custom-call(s32[3]{0:T(128)S(1)} %get-tuple-element.35.where, bf16[128,2048]{1,0:T(8,128)(2,1)S(1)} %copy-done.2, bf16[128,2048]{1,0:T(8,128)(2,1)S(1)} %collective-permute-done.refs_1_, bf16[128,2048]{1,0:T(8,128)(2,1)S(1)} %collective-permute-done.1.refs_2_, ...), custom_call_target="tpu_custom_call" | custom-call | flops 30000001024 | bytes 4000000 | tf_op jit(solution)/shard_map/pallas_call | solution.py:197
  36.0 1.2 copy-done
  37.2 1.9 %all-to-all-done.got = bf16[32,32,256]{2,1,0:T(8,128)(2,1)S(1)} async-done(((bf16[32,32,256]{2,1,0:T(8,128)(2,1)}), bf16[32,32,256]{2,1,0:T(8,128)(2,1)S(1)}, u32[]{:S(2)}, u32[]{:S(2)}) %all-to-all-start) | async-done | bytes 524320 | tf_op jit(solution)/shard_map/all_to_all | solution.py:185
  39.2 11.0 %all-to-all-start.2 = ((bf16[64,16,768]{2,1,0:T(8,128)(2,1)}), bf16[64,16,768]{2,1,0:T(8,128)(2,1)S(1)}, u32[]{:S(2)}, u32[]{:S(2)}) async-start(bf16[64,16,768]{2,1,0:T(8,128)(2,1)} %bitcast.7), calls=%async_computation.2 | async-start | bytes 3145728 | tf_op jit(solution)/shard_map/all_to_all | solution.py:213
  50.2 0.1 fusion.8.weights
  50.3 0.0 copy-start.3
  50.3 0.0 copy-start.4
  50.3 0.8 shard_map.89
  51.1 2.3 %collective-permute-start.3 = (f32[8,16,256]{2,1,0:T(8,128)S(1)}, f32[8,16,256]{2,1,0:T(8,128)S(1)}, u32[]{:S(2)}, u32[]{:S(2)}) collective-permute-start(f32[8,16,256]{2,1,0:T(8,128)S(1)} %get-tuple-element.25), channel_id=1, source_target_pairs={{0,16},{16,0},{1,17},{17,1},{2,18},{18,2},{3,19},{19,3},{4,20},{20... | collective-permute-start | bytes 393224 | tf_op jit(solution)/shard_map/ppermute | solution.py:224
  53.3 1.0 collective-permute-done.3.other0
  54.3 35.0 %all-to-all-done.2.got = bf16[64,16,768]{2,1,0:T(8,128)(2,1)S(1)} async-done(((bf16[64,16,768]{2,1,0:T(8,128)(2,1)}), bf16[64,16,768]{2,1,0:T(8,128)(2,1)S(1)}, u32[]{:S(2)}, u32[]{:S(2)}) %all-to-all-start.2) | async-done | bytes 1572896 | tf_op jit(solution)/shard_map/all_to_all | solution.py:213
  89.3 9.5 %all-to-all-start.1 = ((bf16[64,16,256]{2,1,0:T(8,128)(2,1)}), bf16[64,16,256]{2,1,0:T(8,128)(2,1)S(1)}, u32[]{:S(2)}, u32[]{:S(2)}) async-start(bf16[64,16,256]{2,1,0:T(8,128)(2,1)} %bitcast.5), calls=%async_computation.1 | async-start | bytes 1048576 | tf_op jit(solution)/shard_map/all_to_all | solution.py:226
  98.9 1.1 shard_map.90
  100.0 16.2 %collective-permute-start.4 = (bf16[8,16,256]{2,1,0:T(8,128)(2,1)S(1)}, bf16[8,16,256]{2,1,0:T(8,128)(2,1)S(1)}, u32[]{:S(2)}, u32[]{:S(2)}) collective-permute-start(bf16[8,16,256]{2,1,0:T(8,128)(2,1)S(1)} %get-tuple-element.29), channel_id=1, source_target_pairs={{0,8},{4,12},{8,0},{12,4},{1,9},{5,13},{9,1},{13,5},{2,10},{6,14},... | collective-permute-start | bytes 196616 | tf_op jit(solution)/shard_map/ppermute | solution.py:237
  116.2 1.9 %collective-permute-start.5 = (bf16[8,16,256]{2,1,0:T(8,128)(2,1)S(1)}, bf16[8,16,256]{2,1,0:T(8,128)(2,1)S(1)}, u32[]{:S(2)}, u32[]{:S(2)}) collective-permute-start(bf16[8,16,256]{2,1,0:T(8,128)(2,1)S(1)} %get-tuple-element.30), channel_id=1, source_target_pairs={{0,12},{4,0},{8,4},{12,8},{1,13},{5,1},{9,5},{13,9},{2,14},{6,2},{... | collective-permute-start | bytes 196616 | tf_op jit(solution)/shard_map/ppermute | solution.py:237
  118.1 7.3 %collective-permute-start.6 = (bf16[8,16,256]{2,1,0:T(8,128)(2,1)S(1)}, bf16[8,16,256]{2,1,0:T(8,128)(2,1)S(1)}, u32[]{:S(2)}, u32[]{:S(2)}) collective-permute-start(bf16[8,16,256]{2,1,0:T(8,128)(2,1)S(1)} %get-tuple-element.31), channel_id=1, source_target_pairs={{0,4},{4,8},{8,12},{12,0},{1,5},{5,9},{9,13},{13,1},{2,6},{6,10},{... | collective-permute-start | bytes 196616 | tf_op jit(solution)/shard_map/ppermute | solution.py:237
  125.4 1.2 collective-permute-done.5.refs_1_
  126.6 6.7 %collective-permute-done.6.refs_2_ = bf16[8,16,256]{2,1,0:T(8,128)(2,1)S(1)} collective-permute-done((bf16[8,16,256]{2,1,0:T(8,128)(2,1)S(1)}, bf16[8,16,256]{2,1,0:T(8,128)(2,1)S(1)}, u32[]{:S(2)}, u32[]{:S(2)}) %collective-permute-start.6) | collective-permute-done | bytes 65568 | tf_op jit(solution)/shard_map/ppermute | solution.py:237
  133.3 1.8 %shard_map.91 = (f32[2,8,16,256]{3,2,1,0:T(8,128)}, f32[2,8,16,256]{3,2,1,0:T(8,128)}) custom-call(f32[2,64]{1,0:T(2,128)S(1)} %fusion.8.weights, s32[2,64]{1,0:T(2,128)S(1)} %copy-done.5, f32[8,16,256]{2,1,0:T(8,128)S(1)} %get-tuple-element.23.mine0, f32[8,16,256]{2,1,0:T(8,128)S(1)} %collective-permute-done.3.other0, ...), custom_call_target="tpu_custom_call" | custom-call | tf_op jit(solution)/shard_map/pallas_call | solution.py:238
  (13 shorter events, 0.0 us)
Async XLA Ops:
  0.6 24.2 %copy-start.7 = (s32[64]{0:T(128)S(1)}, s32[64]{0:T(128)}, u32[]{:S(2)}) copy-start(s32[64]{0:T(128)} %param.10) | copy-start | bytes 772
  3.2 26.1 %collective-permute-start = (bf16[128,2048]{1,0:T(8,128)(2,1)}, bf16[128,2048]{1,0:T(8,128)(2,1)S(1)}, u32[]{:S(2)}, u32[]{:S(2)}) collective-permute-start(bf16[128,2048]{1,0:T(8,128)(2,1)} %get-tuple-element.18), channel_id=1, source_target_pairs={{0,2},{1,3},{2,0},{3,1},{4,6},{5,7},{6,4},{7,5},{8,10},{9,11},{10,... | collective-permute-start | bytes 1572872 | tf_op jit(solution)/shard_map/ppermute | solution.py:174
  7.8 23.2 %collective-permute-start.1 = (bf16[128,2048]{1,0:T(8,128)(2,1)}, bf16[128,2048]{1,0:T(8,128)(2,1)S(1)}, u32[]{:S(2)}, u32[]{:S(2)}) collective-permute-start(bf16[128,2048]{1,0:T(8,128)(2,1)} %get-tuple-element.19), channel_id=1, source_target_pairs={{0,3},{1,0},{2,1},{3,2},{4,7},{5,4},{6,5},{7,6},{8,11},{9,8},{10,9... | collective-permute-start | bytes 1572872 | tf_op jit(solution)/shard_map/ppermute | solution.py:174
  10.6 21.3 %collective-permute-start.2 = (bf16[128,2048]{1,0:T(8,128)(2,1)}, bf16[128,2048]{1,0:T(8,128)(2,1)S(1)}, u32[]{:S(2)}, u32[]{:S(2)}) collective-permute-start(bf16[128,2048]{1,0:T(8,128)(2,1)} %get-tuple-element.20), channel_id=1, source_target_pairs={{0,1},{1,2},{2,3},{3,0},{4,5},{5,6},{6,7},{7,4},{8,9},{9,10},{10,1... | collective-permute-start | bytes 1572872 | tf_op jit(solution)/shard_map/ppermute | solution.py:174
  13.1 18.7 %copy-start.1 = (bf16[2,1,1024,256]{3,2,1,0:T(8,128)(2,1)S(1)}, bf16[2,1,1024,256]{3,2,1,0:T(8,128)(2,1)}, u32[]{:S(2)}) copy-start(bf16[2,1,1024,256]{3,2,1,0:T(8,128)(2,1)} %refs_4_.2) | copy-start | bytes 3145732
  13.1 26.0 %all-to-all-start = ((bf16[32,32,256]{2,1,0:T(8,128)(2,1)}), bf16[32,32,256]{2,1,0:T(8,128)(2,1)S(1)}, u32[]{:S(2)}, u32[]{:S(2)}) async-start(bf16[32,32,256]{2,1,0:T(8,128)(2,1)} %bitcast.8), calls=%async_computation | async-start | bytes 1048576 | tf_op jit(solution)/shard_map/all_to_all | solution.py:185
  31.9 1.0 copy-start.2
  36.0 1.2 copy-start
  39.1 11.0 %copy-start.5 = (s32[2,64]{1,0:T(2,128)S(1)}, s32[2,64]{1,0:T(2,128)}, u32[]{:S(2)}) copy-start(s32[2,64]{1,0:T(2,128)} %modules.5) | copy-start | bytes 1540
  39.2 11.1 %copy-start.6 = (s32[3]{0:T(128)S(1)}, s32[3]{0:T(128)}, u32[]{:S(2)}) copy-start(s32[3]{0:T(128)} %get-tuple-element.34.where) | copy-start | bytes 40
  39.2 50.2 %all-to-all-start.2 = ((bf16[64,16,768]{2,1,0:T(8,128)(2,1)}), bf16[64,16,768]{2,1,0:T(8,128)(2,1)S(1)}, u32[]{:S(2)}, u32[]{:S(2)}) async-start(bf16[64,16,768]{2,1,0:T(8,128)(2,1)} %bitcast.7), calls=%async_computation.2 | async-start | bytes 3145728 | tf_op jit(solution)/shard_map/all_to_all | solution.py:213
  50.3 83.1 %copy-start.3 = (f32[2,8,16,256]{3,2,1,0:T(8,128)S(1)}, f32[2,8,16,256]{3,2,1,0:T(8,128)}, u32[]{:S(2)}) copy-start(f32[2,8,16,256]{3,2,1,0:T(8,128)} %refs_3_.1) | copy-start | bytes 786436
  50.3 83.0 %copy-start.4 = (f32[2,8,16,256]{3,2,1,0:T(8,128)S(1)}, f32[2,8,16,256]{3,2,1,0:T(8,128)}, u32[]{:S(2)}) copy-start(f32[2,8,16,256]{3,2,1,0:T(8,128)} %refs_4_.3) | copy-start | bytes 786436
  51.1 3.2 %collective-permute-start.3 = (f32[8,16,256]{2,1,0:T(8,128)S(1)}, f32[8,16,256]{2,1,0:T(8,128)S(1)}, u32[]{:S(2)}, u32[]{:S(2)}) collective-permute-start(f32[8,16,256]{2,1,0:T(8,128)S(1)} %get-tuple-element.25), channel_id=1, source_target_pairs={{0,16},{16,0},{1,17},{17,1},{2,18},{18,2},{3,19},{19,3},{4,20},{20... | collective-permute-start | bytes 393224 | tf_op jit(solution)/shard_map/ppermute | solution.py:224
  89.3 36.1 %all-to-all-start.1 = ((bf16[64,16,256]{2,1,0:T(8,128)(2,1)}), bf16[64,16,256]{2,1,0:T(8,128)(2,1)S(1)}, u32[]{:S(2)}, u32[]{:S(2)}) async-start(bf16[64,16,256]{2,1,0:T(8,128)(2,1)} %bitcast.5), calls=%async_computation.1 | async-start | bytes 1048576 | tf_op jit(solution)/shard_map/all_to_all | solution.py:226
  100.0 25.4 %collective-permute-start.4 = (bf16[8,16,256]{2,1,0:T(8,128)(2,1)S(1)}, bf16[8,16,256]{2,1,0:T(8,128)(2,1)S(1)}, u32[]{:S(2)}, u32[]{:S(2)}) collective-permute-start(bf16[8,16,256]{2,1,0:T(8,128)(2,1)S(1)} %get-tuple-element.29), channel_id=1, source_target_pairs={{0,8},{4,12},{8,0},{12,4},{1,9},{5,13},{9,1},{13,5},{2,10},{6,14},... | collective-permute-start | bytes 196616 | tf_op jit(solution)/shard_map/ppermute | solution.py:237
  116.2 10.4 %collective-permute-start.5 = (bf16[8,16,256]{2,1,0:T(8,128)(2,1)S(1)}, bf16[8,16,256]{2,1,0:T(8,128)(2,1)S(1)}, u32[]{:S(2)}, u32[]{:S(2)}) collective-permute-start(bf16[8,16,256]{2,1,0:T(8,128)(2,1)S(1)} %get-tuple-element.30), channel_id=1, source_target_pairs={{0,12},{4,0},{8,4},{12,8},{1,13},{5,1},{9,5},{13,9},{2,14},{6,2},{... | collective-permute-start | bytes 196616 | tf_op jit(solution)/shard_map/ppermute | solution.py:237
  118.1 15.2 %collective-permute-start.6 = (bf16[8,16,256]{2,1,0:T(8,128)(2,1)S(1)}, bf16[8,16,256]{2,1,0:T(8,128)(2,1)S(1)}, u32[]{:S(2)}, u32[]{:S(2)}) collective-permute-start(bf16[8,16,256]{2,1,0:T(8,128)(2,1)S(1)} %get-tuple-element.31), channel_id=1, source_target_pairs={{0,4},{4,8},{8,12},{12,0},{1,5},{5,9},{9,13},{13,1},{2,6},{6,10},{... | collective-permute-start | bytes 196616 | tf_op jit(solution)/shard_map/ppermute | solution.py:237
